TPU v7x, 32 devices: a whole 2x2x4 slice. The times are simulated.
32 devices in a mesh: dp: 8 (over z, x), mp: 4 (over y, core).
Axes of the slice: x: 2, y: 2, z: 4, core: 2. Of those that a mesh axis runs over, the one named last changes fastest.
Arguments:
- tokens: bfloat16 [32768, 768], P(('dp', 'mp')), may hold values from -6 to 6
- lengths: int32 [128], P('dp'), may hold values from 65 to 512, as said below
- cotangent: bfloat16 [32768, 768], P(('dp', 'mp')), may hold values from -6 to 6
- w_qkv: float32 [768, 12, 192], P('dp', 'mp'), may hold values from -0.109375 to 0.109375
- w_o: float32 [768, 768], P(('dp', 'mp')), may hold values from -0.875 to 0.875
- w_in: float32 [768, 3072], P(None, ('dp', 'mp')), may hold values from -0.21875 to 0.21875
- w_out: float32 [3072, 768], P(('dp', 'mp')), may hold values from -0.109375 to 0.109375
- gain_attn: float32 [768], replicated, may hold values from 0.5 to 1.5
- gain_ffn: float32 [768], replicated, may hold values from 0.5 to 1.5
- pos_table: float32 [32, 12], replicated, may hold values from -4 to 4
- phm_rules: float32 [4, 4, 4], replicated, may hold values from -4 to 4
- down_left: float32 [4, 192], replicated, may hold values from -1.2 to 1.2
- down_right: float32 [4, 12], replicated, may hold values from -1.2 to 1.2
- up_left: float32 [4, 12], replicated, may hold values from -1.2 to 1.2
- up_right: float32 [4, 192], replicated, may hold values from -1.2 to 1.2
Outputs:
- out: bfloat16 [32768, 768], P(('dp', 'mp'))
- grad_tokens: bfloat16 [32768, 768], P(('dp', 'mp'))
- grad_w_qkv: float32 [768, 12, 192], P('dp', 'mp')
- grad_w_o: float32 [768, 768], P(('dp', 'mp'))
- grad_w_in: float32 [768, 3072], P(None, ('dp', 'mp'))
- grad_w_out: float32 [3072, 768], P(('dp', 'mp'))
- grad_gain_attn: float32 [768], replicated
- grad_gain_ffn: float32 [768], replicated
- grad_pos_table: float32 [32, 12], replicated
- grad_phm_rules: float32 [4, 4, 4], replicated
- grad_down_left: float32 [4, 192], replicated
- grad_down_right: float32 [4, 12], replicated
- grad_up_left: float32 [4, 12], replicated
- grad_up_right: float32 [4, 192], replicated
Inputs may be any that keep to these rules, and one draw needn't show every extreme that they name: `lengths`: entry g * 16 + j is the length of sequence j of group g; its slot length is 512 for j below 4, 256 for j below 8, else 128; each length is more than half of its slot length and at most the slot length, and in every group one of the first 4 sequences fills its slot.
All inputs are finite; a program needn't handle non-finite values.
Results may differ from a plain program's by a relative error of at most 0.024.
The roundings to bfloat16 on the way count: a program that leaves them out, or rounds other values in their place, can miss the bound.
Values may be sent and summed in bfloat16 or wider, within the bound.
A program may use at most 192 MiB of HBM per device.

v0:
```python
import jax
import jax.numpy as jnp
import numpy as np
from jax import lax
from jax.sharding import PartitionSpec as P

D = 768
DH = 64
NB = 32
MAXDIST = 128
ADAPT = 48
LEN_LONG = 512
LEN_MID = 256
LEN_SHORT = 128
SEG = 128
NSET = 4


NORM_EPS = 1e-06
MASK_FILL = -1000000000.0
FULL_PRECISION = lax.Precision.HIGHEST


def rel_buckets(length):
    offsets = np.arange(-(length - 1), length)
    half_count = NB // 2
    exact_count = half_count // 2
    upward = (offsets > 0).astype(np.int64) * half_count
    distance = np.abs(offsets)
    scaled = (
        np.log(np.maximum(distance, 1) / exact_count)
        / np.log(MAXDIST / exact_count)
        * (half_count - exact_count)
    )
    far_bucket = np.minimum(
        exact_count + np.floor(np.maximum(scaled, 0.0)).astype(np.int64), half_count - 1
    )
    return upward + np.where(distance < exact_count, distance, far_bucket)


def bucket_shapes():
    return ((LEN_LONG, NSET), (LEN_MID, NSET), (LEN_SHORT, 2 * NSET))


def bucket_blocks(length, seq_count):
    per_block = min(seq_count, max(1, 512 // length))
    return (per_block, seq_count // per_block)


def valid_rows(lengths):
    pieces = []
    offset = 0
    for length, seq_count in bucket_shapes():
        places = jnp.arange(length, dtype=jnp.int32)
        chosen = lengths[offset : offset + seq_count]
        pieces.append((places[None, :] < chosen[:, None]).reshape(length * seq_count))
        offset = offset + seq_count
    return jnp.concatenate(pieces)


def normed(values, gain):
    return values * lax.rsqrt(jnp.mean(values * values, axis=-1, keepdims=True) + NORM_EPS) * gain


def gelu_exact(values):
    return jax.nn.gelu(values, approximate=False)


def adapter_weights(phm_rules, down_left, down_right, up_left, up_right):
    w_down = jnp.einsum(
        "iab,ip,iq->apbq", phm_rules, down_left, down_right, precision=FULL_PRECISION
    ).reshape(D, ADAPT)
    w_up = jnp.einsum(
        "iab,ip,iq->apbq", phm_rules, up_left, up_right, precision=FULL_PRECISION
    ).reshape(ADAPT, D)
    return (w_down, w_up)


def offset_onehot(length):
    buckets = jnp.asarray(rel_buckets(length), dtype=jnp.int32)
    return (buckets[:, None] == jnp.arange(NB, dtype=jnp.int32)[None, :]).astype(jnp.float32)


def spread_bias(offset_values, length):
    head_count = offset_values.shape[0]
    padded = jnp.pad(offset_values, ((0, 0), (0, 1)))
    tiled = jnp.tile(padded, (1, length + 1))[:, : length * (2 * length - 1)]
    return tiled.reshape(head_count, length, 2 * length - 1)[:, :, length - 1 :]


def fold_bias(score_grid, length):
    head_count = score_grid.shape[0]
    widened = jnp.pad(score_grid, ((0, 0), (0, 0), (length - 1, 0)))
    flat_rows = widened.reshape(head_count, length * (2 * length - 1))
    flat_rows = jnp.pad(flat_rows, ((0, 0), (0, length)))
    return jnp.sum(flat_rows.reshape(head_count, length, 2 * length), axis=1)[:, : 2 * length - 1]


def block_scores(queries, key_part, score_bias, live_mask):
    raw_scores = (
        jnp.einsum("slhd,smhd->shlm", queries, key_part, preferred_element_type=jnp.float32)
        + score_bias[None]
    )
    return jnp.where(live_mask[:, None, None, :], raw_scores, MASK_FILL)


def attend_block(packed, live_mask, score_bias):
    scores = block_scores(packed[:, :, :, 0], packed[:, :, :, 1], score_bias, live_mask)
    row_max = jnp.max(scores, axis=-1, keepdims=True)
    raised = jnp.exp(scores - row_max)
    row_total = jnp.sum(raised, axis=-1, keepdims=True)
    attn_probs = (raised / row_total).astype(jnp.bfloat16)
    context = jnp.einsum(
        "shlm,smhd->slhd", attn_probs, packed[:, :, :, 2], preferred_element_type=jnp.float32
    )
    return (context.astype(jnp.bfloat16), (row_max + jnp.log(row_total))[..., 0])


def attend_back(packed, live_mask, score_bias, log_total, grad_context):
    queries = packed[:, :, :, 0]
    key_part = packed[:, :, :, 1]
    values = packed[:, :, :, 2]
    scores = block_scores(queries, key_part, score_bias, live_mask)
    attn_probs = jnp.exp(scores - log_total[..., None])
    probs_low = attn_probs.astype(jnp.bfloat16)
    grad_probs = jnp.einsum(
        "slhd,smhd->shlm", grad_context, values, preferred_element_type=jnp.float32
    )
    grad_values = jnp.einsum(
        "shlm,slhd->smhd", probs_low, grad_context, preferred_element_type=jnp.float32
    )
    centre = jnp.sum(attn_probs * grad_probs, axis=-1, keepdims=True)
    grad_scores = (attn_probs * (grad_probs - centre)).astype(jnp.bfloat16)
    grad_queries = jnp.einsum(
        "shlm,smhd->slhd", grad_scores, key_part, preferred_element_type=jnp.float32
    )
    grad_keys = jnp.einsum(
        "shlm,slhd->smhd", grad_scores, queries, preferred_element_type=jnp.float32
    )
    score_grid = jnp.sum(lax.optimization_barrier(grad_scores).astype(jnp.float32), axis=0)
    packed_grad = jnp.stack([grad_queries, grad_keys, grad_values], axis=3).astype(jnp.bfloat16)
    return (packed_grad, score_grid)


def local(
    tokens,
    lengths,
    cotangent,
    w_qkv,
    w_o,
    w_in,
    w_out,
    gain_attn,
    gain_ffn,
    pos_table,
    phm_rules,
    down_left,
    down_right,
    up_left,
    up_right,
):
    mp_count = lax.axis_size("mp")
    member = lax.axis_index("mp")
    tok_rows = tokens.shape[0]
    model_width = tokens.shape[1]
    seg_count = tok_rows // SEG
    group_rows = tok_rows * mp_count
    local_heads = w_qkv.shape[1]
    head_cols = local_heads * 3 * DH
    dense_o, dense_in, dense_out = (
        lax.all_gather(w_o.astype(jnp.bfloat16), ("dp", "mp"), axis=0, tiled=True),
        lax.all_gather(w_in.astype(jnp.bfloat16), ("dp", "mp"), axis=1, tiled=True),
        lax.all_gather(w_out.astype(jnp.bfloat16), ("dp", "mp"), axis=0, tiled=True),
    )
    qkv_rows = lax.all_gather(w_qkv.astype(jnp.bfloat16), "dp", axis=0, tiled=True)
    live_all = valid_rows(lengths)
    live_own = lax.dynamic_index_in_dim(
        live_all.reshape(seg_count, mp_count, SEG), member, axis=1, keepdims=False
    ).reshape(tok_rows)
    table_heads = lax.dynamic_slice_in_dim(pos_table, member * local_heads, local_heads, axis=1)
    x_float = tokens.astype(jnp.float32)
    normed_attn = normed(x_float, gain_attn).astype(jnp.bfloat16)
    qkv_full = lax.all_gather(qkv_rows, "mp", axis=1, tiled=True)
    projected = jnp.dot(
        normed_attn,
        qkv_full.reshape(model_width, mp_count * head_cols),
        preferred_element_type=jnp.float32,
    ).astype(jnp.bfloat16)
    packed_heads = lax.all_to_all(
        projected.reshape(seg_count, 1, SEG, mp_count, head_cols),
        "mp",
        split_axis=3,
        concat_axis=1,
        tiled=True,
    )
    packed_heads = packed_heads.reshape(group_rows, local_heads, 3, DH)
    context_parts = []
    log_totals = []
    offset = 0
    for length, seq_count in bucket_shapes():
        per_block, block_count = bucket_blocks(length, seq_count)
        row_span = length * seq_count
        block_packed = lax.slice_in_dim(packed_heads, offset, offset + row_span, axis=0).reshape(
            block_count, per_block, length, local_heads, 3, DH
        )
        block_live = live_all[offset : offset + row_span].reshape(block_count, per_block, length)
        offset_values = jnp.einsum(
            "rb,bh->hr", offset_onehot(length), table_heads, precision=FULL_PRECISION
        )
        score_bias = spread_bias(offset_values, length)
        context, log_total = lax.map(
            lambda block_item: attend_block(block_item[0], block_item[1], score_bias),
            (block_packed, block_live),
        )
        context_parts.append(context.reshape(row_span, local_heads * DH))
        log_totals.append(log_total)
        offset = offset + row_span
    context_heads = jnp.concatenate(context_parts, axis=0)
    context_rows = lax.all_to_all(
        context_heads.reshape(seg_count, mp_count, SEG, 1, local_heads * DH),
        "mp",
        split_axis=1,
        concat_axis=3,
        tiled=True,
    ).reshape(tok_rows, model_width)
    midway = x_float + jnp.dot(context_rows, dense_o, preferred_element_type=jnp.float32)
    normed_ffn = normed(midway, gain_ffn).astype(jnp.bfloat16)
    ffn_pre = jnp.dot(normed_ffn, dense_in, preferred_element_type=jnp.float32)
    ffn_act = gelu_exact(ffn_pre).astype(jnp.bfloat16)
    ffn_out = jnp.dot(ffn_act, dense_out, preferred_element_type=jnp.float32)
    ffn_low = ffn_out.astype(jnp.bfloat16)
    w_down, w_up = adapter_weights(phm_rules, down_left, down_right, up_left, up_right)
    down_low = w_down.astype(jnp.bfloat16)
    up_low = w_up.astype(jnp.bfloat16)
    squeezed = jnp.dot(ffn_low, down_low, preferred_element_type=jnp.float32)
    lifted = gelu_exact(squeezed).astype(jnp.bfloat16)
    result = (
        midway + ffn_out + jnp.dot(lifted, up_low, preferred_element_type=jnp.float32)
    ).astype(jnp.bfloat16)
    grad_out = cotangent.astype(jnp.float32) * live_own[:, None].astype(jnp.float32)
    grad_out_low = grad_out.astype(jnp.bfloat16)
    grad_w_up = jnp.dot(lifted.T, grad_out_low, preferred_element_type=jnp.float32)
    _, gelu_back_sq = jax.vjp(gelu_exact, squeezed)
    grad_sq = gelu_back_sq(jnp.dot(grad_out_low, up_low.T, preferred_element_type=jnp.float32))[
        0
    ].astype(jnp.bfloat16)
    grad_w_down = jnp.dot(ffn_low.T, grad_sq, preferred_element_type=jnp.float32)
    grad_ffn = (grad_out + jnp.dot(grad_sq, down_low.T, preferred_element_type=jnp.float32)).astype(
        jnp.bfloat16
    )
    grad_w_out = jnp.dot(ffn_act.T, grad_ffn, preferred_element_type=jnp.float32)
    _, gelu_back_pre = jax.vjp(gelu_exact, ffn_pre)
    grad_pre = gelu_back_pre(jnp.dot(grad_ffn, dense_out.T, preferred_element_type=jnp.float32))[
        0
    ].astype(jnp.bfloat16)
    grad_w_in = jnp.dot(normed_ffn.T, grad_pre, preferred_element_type=jnp.float32)
    _, norm_back_ffn = jax.vjp(normed, midway, gain_ffn)
    grad_mid_part, grad_gain_ffn = norm_back_ffn(
        jnp.dot(grad_pre, dense_in.T, preferred_element_type=jnp.float32)
    )
    grad_mid = grad_out + grad_mid_part
    grad_mid_low = grad_mid.astype(jnp.bfloat16)
    grad_w_o = jnp.dot(context_rows.T, grad_mid_low, preferred_element_type=jnp.float32)
    grad_context = jnp.dot(grad_mid_low, dense_o.T, preferred_element_type=jnp.float32).astype(
        jnp.bfloat16
    )
    grad_context_heads = lax.all_to_all(
        grad_context.reshape(seg_count, 1, SEG, mp_count, local_heads * DH),
        "mp",
        split_axis=3,
        concat_axis=1,
        tiled=True,
    ).reshape(group_rows, local_heads, DH)
    packed_grad_parts = []
    table_grad = jnp.zeros((NB, local_heads), jnp.float32)
    offset = 0
    for bucket_number, (length, seq_count) in enumerate(bucket_shapes()):
        per_block, block_count = bucket_blocks(length, seq_count)
        row_span = length * seq_count
        block_packed = lax.slice_in_dim(packed_heads, offset, offset + row_span, axis=0).reshape(
            block_count, per_block, length, local_heads, 3, DH
        )
        block_live = live_all[offset : offset + row_span].reshape(block_count, per_block, length)
        block_grad = lax.slice_in_dim(
            grad_context_heads, offset, offset + row_span, axis=0
        ).reshape(block_count, per_block, length, local_heads, DH)
        onehot = offset_onehot(length)
        score_bias = spread_bias(
            jnp.einsum("rb,bh->hr", onehot, table_heads, precision=FULL_PRECISION), length
        )

        def back_step(grid_sum, block_item):
            packed_grad, score_grid = attend_back(
                block_item[0], block_item[1], score_bias, block_item[2], block_item[3]
            )
            return (grid_sum + score_grid, packed_grad)

        grid_sum, packed_grad = lax.scan(
            back_step,
            jnp.zeros((local_heads, length, length), jnp.float32),
            (block_packed, block_live, log_totals[bucket_number], block_grad),
        )
        table_grad = table_grad + jnp.einsum(
            "hr,rb->bh", fold_bias(grid_sum, length), onehot, precision=FULL_PRECISION
        )
        packed_grad_parts.append(packed_grad.reshape(row_span, head_cols))
        offset = offset + row_span
    packed_grads = jnp.concatenate(packed_grad_parts, axis=0)
    row_grads = lax.all_to_all(
        packed_grads.reshape(seg_count, mp_count, SEG, 1, head_cols),
        "mp",
        split_axis=1,
        concat_axis=3,
        tiled=True,
    ).reshape(tok_rows, mp_count * head_cols)
    full_weight_grad = jnp.dot(
        normed_attn.T, row_grads, preferred_element_type=jnp.float32
    ).reshape(model_width, mp_count * local_heads, 3 * DH)
    head_weight_grad = lax.psum_scatter(
        full_weight_grad.astype(jnp.bfloat16), "mp", scatter_dimension=1, tiled=True
    ).astype(jnp.float32)
    grad_n1 = jnp.dot(
        row_grads,
        qkv_full.reshape(model_width, mp_count * head_cols).T,
        preferred_element_type=jnp.float32,
    )
    grad_w_qkv = lax.psum_scatter(head_weight_grad, "dp", scatter_dimension=0, tiled=True)
    _, norm_back_attn = jax.vjp(normed, x_float, gain_attn)
    grad_x_part, grad_gain_attn = norm_back_attn(grad_n1)
    grad_tokens = (grad_mid + grad_x_part).astype(jnp.bfloat16)
    grad_w_o, grad_w_in, grad_w_out = (
        lax.psum_scatter(grad_w_o, ("dp", "mp"), scatter_dimension=0, tiled=True),
        lax.psum_scatter(grad_w_in, ("dp", "mp"), scatter_dimension=1, tiled=True),
        lax.psum_scatter(grad_w_out, ("dp", "mp"), scatter_dimension=0, tiled=True),
    )
    _, adapter_back = jax.vjp(adapter_weights, phm_rules, down_left, down_right, up_left, up_right)
    grad_rules, grad_dleft, grad_dright, grad_uleft, grad_uright = adapter_back(
        (grad_w_down, grad_w_up)
    )
    table_full = lax.dynamic_update_slice_in_dim(
        jnp.zeros_like(pos_table), table_grad, member * local_heads, axis=1
    )
    summed_small = lax.psum(
        (
            grad_gain_attn,
            grad_gain_ffn,
            table_full,
            grad_rules,
            grad_dleft,
            grad_dright,
            grad_uleft,
            grad_uright,
        ),
        ("dp", "mp"),
    )
    return (
        result,
        grad_tokens,
        grad_w_qkv,
        grad_w_o,
        grad_w_in,
        grad_w_out,
        summed_small[0],
        summed_small[1],
        summed_small[2],
        summed_small[3],
        summed_small[4],
        summed_small[5],
        summed_small[6],
        summed_small[7],
    )


def solution(mesh):
    return jax.shard_map(
        local,
        mesh=mesh,
        in_specs=(
            P(("dp", "mp"), None),
            P("dp"),
            P(("dp", "mp"), None),
            P("dp", "mp", None),
            P(("dp", "mp"), None),
            P(None, ("dp", "mp")),
            P(("dp", "mp"), None),
            P(),
            P(),
            P(),
            P(),
            P(),
            P(),
            P(),
            P(),
        ),
        out_specs=(
            P(("dp", "mp"), None),
            P(("dp", "mp"), None),
            P("dp", "mp", None),
            P(("dp", "mp"), None),
            P(None, ("dp", "mp")),
            P(("dp", "mp"), None),
            P(),
            P(),
            P(),
            P(),
            P(),
            P(),
            P(),
            P(),
        ),
        check_vma=False,
    )
```

profile of v0, /device:TPU:0, one launch (start us, length us, event | category | flops | bytes accessed | tf_op | source)
XLA Modules:
  0.0 1077.3 jit_solution(7718930165567288082)
XLA Ops:
  8.4 38.9 %all_gather.15 = bf16[768,3,192]{2,1,0:T(4,128)(2,1)S(1)} all-gather(bf16[96,3,192]{2,1,0:T(4,128)(2,1)S(1)} %copy.331), channel_id=1, replica_groups=mesh['dp'=8,'mp'=4] {'dp'}, dimensions={0}, use_global_device_ids=true | all-gather | bytes 995328 | tf_op jit(solution)/shard_map/all_gather | solution.py:175
  52.8 26.7 %all-gather.5.cloned.1.call-done = bf16[768,12,192]{0,2,1:T(8,128)(2,1)} async-done(((bf16[768,3,192]{0,2,1:T(8,128)(2,1)}), bf16[768,12,192]{0,2,1:T(8,128)(2,1)}) %all-gather.5.cloned.1.call-update) | async-done | bytes 3538960 | tf_op jit(solution)/shard_map/all_gather | solution.py:183
  79.5 8.0 convolution_convert_fusion.10
  87.5 11.5 %reshape.703 = bf16[8,1,128,4,576]{4,3,2,0,1:T(4,128)(2,1)} reshape(bf16[1024,2304]{1,0:T(8,128)(2,1)} %convolution_convert_fusion.10) | data formatting | bytes 9437184 | tf_op jit(solution)/shard_map/reshape | solution.py:190
  99.0 7.5 copy.334
  106.5 5.1 all-to-all-start
  123.5 10.4 copy.436
  134.0 7.8 slice.199
  141.8 13.2 %reshape.653 = f32[3,512,1023]{2,1,0:T(8,128)} reshape(f32[3,523776]{1,0:T(4,128)} %slice.199) | data formatting | bytes 12570624 | tf_op jit(solution)/shard_map/reshape | solution.py:88
  155.0 4.7 slice.200
  159.8 3.7 copy.338
  176.7 5.8 while.76
  184.1 5.5 copy.336
  189.6 5.1 reshape.652
  198.1 24.8 %while.75 = (s32[]{:T(128)}, bf16[4,1,512,3,64]{2,4,3,1,0:T(8,128)(2,1)}, f32[4,1,3,512]{3,2,1,0:T(4,128)}, bf16[4,1,512,3,3,64]{2,5,3,4,1,0:T(8,128)(2,1)}, pre...) while((s32[]{:T(128)}, bf16[4,1,512,3,64]{2,4,3,1,0:T(8,128)(2,1)}, ...), condition=%wide.region_4.5_spmd, body=%wide.region_1.4_spmd.sunk | while | flops 207714816 | bytes 14606933 | solution.py:211
  228.9 3.8 reshape.661
  235.5 4.7 all-to-all-start.1
  244.1 24.0 %all-to-all-done.1 = bf16[8,4,128,1,192]{2,0,4,3,1:T(8,128)(2,1)} async-done(((bf16[8,4,128,1,192]{2,0,4,3,1:T(8,128)(2,1)}), bf16[8,4,128,1,192]{2,0,4,3,1:T(8,128)(2,1)}, u32[]{:S(2)}, u32[]{:S(2)}) %all-to-all-start.1) | async-done | bytes 1572896 | tf_op jit(solution)/shard_map/all_to_all | solution.py:219
  268.1 5.0 multiply_reduce_fusion.5
  273.1 36.9 %multiply_convert_fusion.3 = (bf16[1024,3072]{1,0:T(8,128)(2,1)}, f32[1024,3072]{1,0:T(8,128)}, f32[1024,3072]{1,0:T(8,128)}) fusion(bf16[768,3072]{0,1:T(8,128)(2,1)} %all-gather.9.cloned.1.call-done, f32[1024,768]{0,1:T(8,128)} %get-tuple-element.746, f32[768]{0:T(1024)S(1)} %copy-done.74, f32[1024]{0:T(1024)S(1)} %fusion.138), kind=kOutput, calls=%fused_computation.123 | convolution fusion | flops 5038669824 | bytes 39328768 | tf_op jit(solution)/shard_map/dot_general | solution.py:228
  310.0 8.9 fusion.155
  323.3 16.4 %add_convert_fusion = bf16[1024,3072]{1,0:T(8,128)(2,1)} fusion(f32[1024,3072]{1,0:T(8,128)} %get-tuple-element.726, f32[1024,3072]{1,0:T(8,128)} %get-tuple-element.747, bf16[1024,768]{0,1:T(8,128)(2,1)S(1)} %add_convert_fusion.1, bf16[3072,768]{1,0:T(8,128)(2,1)} %all-gather.11.cloned.1.call-done), kind=kOutput, calls=%fused_computation.122 | convolution fusion | flops 4875878400 | bytes 37748736 | tf_op jit(solution)/shard_map/dot_general | solution.py:253
  339.6 9.8 multiply_reduce_fusion.3
  354.7 4.4 reshape.704
  365.6 19.9 %all-to-all-done.2 = bf16[8,1,128,4,192]{2,0,4,1,3:T(8,128)(2,1)S(1)} async-done(((bf16[8,1,128,4,192]{2,0,4,1,3:T(8,128)(2,1)}), bf16[8,1,128,4,192]{2,0,4,1,3:T(8,128)(2,1)S(1)}, u32[]{:S(2)}, u32[]{:S(2)}) %all-to-all-start.2) | async-done | bytes 1572896 | tf_op jit(solution)/shard_map/all_to_all | solution.py:267
  389.3 60.7 %while.78 = (s32[]{:T(128)}, f32[3,512,512]{1,2,0:T(8,128)}, bf16[4,1,512,3,3,64]{2,5,3,4,1,0:T(8,128)(2,1)}, pred[4,1,512]{2,1,0:T(4,128)(4,1)}, bf16[4,1,512,3...) while((s32[]{:T(128)}, f32[3,512,512]{1,2,0:T(8,128)}, ...), condition=%wide.region_17.18_spmd.clone, body=%wide.region_15.17_spmd.clone.sunk | while | flops 514816512 | bytes 38964344 | solution.py:298
  414.7 4.1 convert_add_fusion.3
  430.2 4.1 convert_add_fusion.3
  445.8 4.1 convert_add_fusion.3
  452.3 14.0 %while.79 = (s32[]{:T(128)}, f32[3,256,256]{1,2,0:T(8,128)}, bf16[2,2,256,3,3,64]{2,1,0,5,4,3:T(2,128)(2,1)}, pred[2,2,256]{2,1,0:T(4,128)(4,1)S(1)}, bf16[2,2,2...) while((s32[]{:T(128)}, f32[3,256,256]{1,2,0:T(8,128)}, ...), condition=%wide.region_21.22_spmd.clone, body=%wide.region_18.21_spmd.clone.sunk | while | flops 257063424 | bytes 38226192 | solution.py:298
  467.4 15.1 %while.80 = (s32[]{:T(128)}, f32[3,128,128]{1,2,0:T(8,128)}, bf16[2,4,128,3,3,64]{2,1,0,5,4,3:T(4,128)(2,1)}, pred[2,4,128]{2,1,0:T(4,128)(4,1)S(1)}, bf16[2,4,1...) while((s32[]{:T(128)}, f32[3,128,128]{1,2,0:T(8,128)}, ...), condition=%wide.region_25.26_spmd.clone, body=%wide.region_22.25_spmd.clone.sunk | while | flops 128924160 | bytes 23824120 | solution.py:298
  494.9 8.7 reshape.674
  506.5 56.4 %all_to_all.60 = bf16[8,4,128,1,576]{2,0,4,3,1:T(8,128)(2,1)S(1)} all-to-all(bf16[8,4,128,1,576]{2,0,4,3,1:T(8,128)(2,1)S(1)} %copy.372), channel_id=1, replica_groups=mesh['dp'=8,'mp'=4] {'mp'}, dimensions={1} | all-to-all | bytes 9437184 | tf_op jit(solution)/shard_map/all_to_all | solution.py:309
  565.5 5.5 convolution_convert_fusion.11
  571.0 40.0 %reduce-scatter.8.cloned.1.call-done = bf16[768,3,192]{0,2,1:T(8,128)(2,1)} async-done(((bf16[768,12,192]{0,2,1:T(8,128)(2,1)}), bf16[768,3,192]{0,2,1:T(8,128)(2,1)}) %reduce-scatter.8.cloned.1.call-update) | async-done | bytes 884752 | tf_op jit(solution)/shard_map/reduce_scatter | solution.py:319
  616.6 4.3 fusion.62
  620.9 10.1 fusion.156
  632.9 12.7 %fusion.145 = f32[768,3072]{0,1:T(8,128)} fusion(bf16[1024,3072]{1,0:T(8,128)(2,1)} %add_convert_fusion, f32[1024,768]{0,1:T(8,128)S(1)} %copy-done.25, f32[768]{0:T(1024)S(1)} %copy-done.75, f32[1024]{0:T(1024)S(1)} %copy-done.65), kind=kOutput, calls=%fused_computation.286 | convolution fusion | flops 4834197504 | bytes 18881536 | tf_op jit(solution)/shard_map/dot_general | solution.py:256
  656.2 4.2 add_convert_fusion.2
  675.7 5.9 pad.51.clone
  681.6 13.5 %reshape.676 = f32[3,523776]{1,0:T(4,128)} reshape(f32[3,512,1023]{2,1,0:T(8,128)} %pad.51.clone) | data formatting | bytes 12570624 | tf_op jit(solution)/shard_map/reshape | solution.py:94
  695.1 8.0 pad.52
  710.6 6.9 bitcast_reduce_fusion
  718.9 8.3 fusion.55
  729.8 40.8 %all-reduce.12 = (f32[768]{0:T(1024)}, f32[768]{0:T(1024)}, f32[32,12]{0,1:T(8,128)}, f32[4,4,4]{2,1,0:T(4,128)}, f32[4,192]{1,0:T(4,128)}, /*index=5*/f32[4,12]{1,0:T(4,128)}, f32[4,12]{1,0:T(4,128)}, f32[4,192]{1,0:T(4,128)}) all-reduce(f32[768]{0:T(1024)S(1)} %get-tuple-element.631, ...), channel_id=1, replica_groups=mesh['dp'=8,'mp'=4] {'dp','mp'}, use_global_device_ids=true, to_apply=%region_33.34 | all-reduce | flops 3616 | bytes 28928 | tf_op jit(solution)/shard_map/psum | solution.py:343
  772.6 14.6 %reduce-scatter.10.cloned.1.call-done = f32[24,768]{1,0:T(8,128)} async-done(((f32[768,768]{1,0:T(8,128)}), f32[24,768]{1,0:T(8,128)}) %reduce-scatter.10.cloned.1.call-update) | async-done | bytes 73744 | tf_op jit(solution)/shard_map/reduce_scatter | solution.py:332
  787.2 142.1 %reduce-scatter.14.cloned.1.call-done = f32[96,768]{1,0:T(8,128)} async-done(((f32[3072,768]{1,0:T(8,128)}), f32[96,768]{1,0:T(8,128)}) %reduce-scatter.14.cloned.1.call-update) | async-done | bytes 294928 | tf_op jit(solution)/shard_map/reduce_scatter | solution.py:334
  929.3 141.0 %reduce-scatter.12.cloned.1.call-done = f32[768,96]{0,1:T(8,128)} async-done(((f32[768,3072]{0,1:T(8,128)}), f32[768,96]{0,1:T(8,128)}) %reduce-scatter.12.cloned.1.call-update) | async-done | bytes 294928 | tf_op jit(solution)/shard_map/reduce_scatter | solution.py:333
  (508 shorter events, 245.1 us)
Async XLA Ops:
  7.2 105.4 %copy-start = (f32[32,12]{0,1:T(8,128)S(1)}, f32[32,12]{0,1:T(8,128)}, u32[]{:S(2)}) copy-start(f32[32,12]{0,1:T(8,128)} %param.42) | copy-start | bytes 4612
  7.2 42.3 %copy-start.55 = (f32[24,768]{1,0:T(8,128)S(1)}, f32[24,768]{1,0:T(8,128)}, u32[]{:S(2)}) copy-start(f32[24,768]{1,0:T(8,128)} %param.37) | copy-start | bytes 221188
  7.2 43.0 %copy-start.45 = (f32[768,96]{0,1:T(8,128)S(1)}, f32[768,96]{0,1:T(8,128)}, u32[]{:S(2)}) copy-start(f32[768,96]{0,1:T(8,128)} %param.38) | copy-start | bytes 884740
  7.2 72.3 %all-gather.5.cloned.1.call-start = ((), (), s32[]{:S(2)}) async-start(), calls=%async_computation.9 | async-start | bytes 4423680 | tf_op jit(solution)/shard_map/all_gather | solution.py:183
  8.3 42.6 %copy-start.31 = (bf16[1024,768]{1,0:T(8,128)(2,1)S(1)}, bf16[1024,768]{1,0:T(8,128)(2,1)}, u32[]{:S(2)}) copy-start(bf16[1024,768]{1,0:T(8,128)(2,1)} %param.33) | copy-start | bytes 4718596
  49.4 30.1 %copy-start.71 = (f32[768]{0:T(1024)S(1)}, f32[768]{0:T(1024)}, u32[]{:S(2)}) copy-start(f32[768]{0:T(1024)} %param.40) | copy-start | bytes 9220
  49.4 194.7 %all-gather.7.cloned.1.call-start = ((), (), s32[]{:S(2)}) async-start(), calls=%async_computation.10 | async-start | bytes 1216512 | tf_op jit(solution)/shard_map/all_gather | solution.py:171
  50.2 222.9 %all-gather.9.cloned.1.call-start = ((), (), s32[]{:S(2)}) async-start(), calls=%async_computation.11 | async-start | bytes 4866048 | tf_op jit(solution)/shard_map/all_gather | solution.py:172
  51.7 35.8 %copy-start.15 = (bf16[1024,768]{0,1:T(8,128)(2,1)}, bf16[1024,768]{0,1:T(8,128)(2,1)S(1)}, u32[]{:S(2)}) copy-start(bf16[1024,768]{0,1:T(8,128)(2,1)S(1)} %copy.330) | copy-start | bytes 4718596
  52.8 34.7 %copy-start.60 = (f32[1024]{0:T(1024)}, f32[1024]{0:T(1024)S(1)}, u32[]{:S(2)}) copy-start(f32[1024]{0:T(1024)S(1)} %fusion.137) | copy-start | bytes 12292
  106.5 62.1 %all-to-all-start = ((bf16[8,1,128,4,576]{2,0,4,1,3:T(8,128)(2,1)}), bf16[8,1,128,4,576]{2,0,4,1,3:T(8,128)(2,1)}, u32[]{:S(2)}, u32[]{:S(2)}) async-start(bf16[8,1,128,4,576]{2,0,4,1,3:T(8,128)(2,1)} %copy.334), calls=%async_computation | async-start | bytes 9437184 | tf_op jit(solution)/shard_map/all_to_all | solution.py:189
  111.6 198.5 %all-gather.11.cloned.1.call-start = ((), (), s32[]{:S(2)}) async-start(), calls=%async_computation.12 | async-start | bytes 4866048 | tf_op jit(solution)/shard_map/all_gather | solution.py:173
  165.1 76.3 %copy-start.51 = (f32[4,4,4]{0,2,1:T(4,128)}, f32[4,4,4]{0,2,1:T(4,128)S(1)}, u32[]{:S(2)}) copy-start(f32[4,4,4]{0,2,1:T(4,128)S(1)} %copy.349) | copy-start | bytes 772
  182.6 12.2 %copy-start.3 = (f32[3,256,256]{1,2,0:T(8,128)}, f32[3,256,256]{1,2,0:T(8,128)S(1)}, u32[]{:S(2)}) copy-start(f32[3,256,256]{1,2,0:T(8,128)S(1)} %get-tuple-element.1194) | copy-start | bytes 2359300
  182.6 12.2 %copy-start.5 = (bf16[2,2,256,3,3,64]{2,5,3,1,4,0:T(8,128)(2,1)}, bf16[2,2,256,3,3,64]{2,5,3,1,4,0:T(8,128)(2,1)S(1)}, u32[]{:S(2)}) copy-start(bf16[2,2,256,3,3,64]{2,5,3,1,4,0:T(8,128)(2,1)S(1)} %get-tuple-element.1195) | copy-start | bytes 3538948
  182.6 12.2 %copy-start.48 = (f32[2,2,3,256]{3,2,1,0:T(4,128)}, f32[2,2,3,256]{3,2,1,0:T(4,128)S(1)}, u32[]{:S(2)}) copy-start(f32[2,2,3,256]{3,2,1,0:T(4,128)S(1)} %get-tuple-element.1131) | copy-start | bytes 36868
  182.6 12.2 %copy-start.53 = (pred[2,2,256]{2,1,0:T(4,128)(4,1)}, pred[2,2,256]{2,1,0:T(4,128)(4,1)S(1)}, u32[]{:S(2)}) copy-start(pred[2,2,256]{2,1,0:T(4,128)(4,1)S(1)} %get-tuple-element.1227) | copy-start | bytes 3076
  232.7 7.5 copy-start.66
  232.7 8.6 copy-start.68
  232.7 8.6 copy-start.77
  235.5 32.6 %copy-start.16 = (bf16[1024,768]{0,1:T(8,128)(2,1)S(1)}, bf16[1024,768]{0,1:T(8,128)(2,1)}, u32[]{:S(2)}) copy-start(bf16[1024,768]{0,1:T(8,128)(2,1)} %copy-done.15) | copy-start | bytes 4718596
  235.5 32.6 %all-to-all-start.1 = ((bf16[8,4,128,1,192]{2,0,4,3,1:T(8,128)(2,1)}), bf16[8,4,128,1,192]{2,0,4,3,1:T(8,128)(2,1)}, u32[]{:S(2)}, u32[]{:S(2)}) async-start(bf16[8,4,128,1,192]{2,0,4,3,1:T(8,128)(2,1)} %copy.347), calls=%async_computation.1 | async-start | bytes 3145728 | tf_op jit(solution)/shard_map/all_to_all | solution.py:219
  242.2 77.4 %copy-start.44 = (bf16[48,768]{1,0:T(8,128)(2,1)}, bf16[48,768]{1,0:T(8,128)(2,1)S(1)}, u32[]{:S(2)}) copy-start(bf16[48,768]{1,0:T(8,128)(2,1)S(1)} %convert_element_type.224) | copy-start | bytes 221188
  244.0 105.5 %copy-start.19 = (bf16[1024,768]{0,1:T(8,128)(2,1)}, bf16[1024,768]{0,1:T(8,128)(2,1)S(1)}, u32[]{:S(2)}) copy-start(bf16[1024,768]{0,1:T(8,128)(2,1)S(1)} %copy.353) | copy-start | bytes 4718596
  244.1 105.4 %copy-start.56 = (f32[8,1,128]{2,1,0:T(1,128)}, f32[8,1,128]{2,1,0:T(1,128)S(1)}, u32[]{:S(2)}) copy-start(f32[8,1,128]{2,1,0:T(1,128)S(1)} %dynamic-slice_convert_fusion) | copy-start | bytes 12292
  273.1 76.4 %copy-start.64 = (f32[1024]{0:T(1024)}, f32[1024]{0:T(1024)S(1)}, u32[]{:S(2)}) copy-start(f32[1024]{0:T(1024)S(1)} %fusion.138) | copy-start | bytes 12292
  323.3 16.4 %copy-start.24 = (f32[1024,768]{0,1:T(8,128)S(1)}, f32[1024,768]{0,1:T(8,128)}, u32[]{:S(2)}) copy-start(f32[1024,768]{0,1:T(8,128)} %get-tuple-element.746) | copy-start | bytes 9437188
  361.9 23.6 %all-to-all-start.2 = ((bf16[8,1,128,4,192]{2,0,4,1,3:T(8,128)(2,1)}), bf16[8,1,128,4,192]{2,0,4,1,3:T(8,128)(2,1)S(1)}, u32[]{:S(2)}, u32[]{:S(2)}) async-start(bf16[8,1,128,4,192]{2,0,4,1,3:T(8,128)(2,1)} %copy.357), calls=%async_computation.2 | async-start | bytes 3145728 | tf_op jit(solution)/shard_map/all_to_all | solution.py:267
  365.5 245.5 %reduce-scatter.8.cloned.1.call-start = ((), (), s32[]{:S(2)}) async-start(), calls=%async_computation.13 | async-start | bytes 4423680 | tf_op jit(solution)/shard_map/reduce_scatter | solution.py:319
  389.3 63.0 %copy-start.4 = (f32[3,256,256]{1,2,0:T(8,128)S(1)}, f32[3,256,256]{1,2,0:T(8,128)}, u32[]{:S(2)}) copy-start(f32[3,256,256]{1,2,0:T(8,128)} %copy-done.3) | copy-start | bytes 2359300
  389.3 63.0 %copy-start.6 = (bf16[2,2,256,3,3,64]{2,5,3,1,4,0:T(8,128)(2,1)S(1)}, bf16[2,2,256,3,3,64]{2,5,3,1,4,0:T(8,128)(2,1)}, u32[]{:S(2)}) copy-start(bf16[2,2,256,3,3,64]{2,5,3,1,4,0:T(8,128)(2,1)} %copy-done.5) | copy-start | bytes 3538948
  389.3 63.0 %copy-start.54 = (pred[2,2,256]{2,1,0:T(4,128)(4,1)S(1)}, pred[2,2,256]{2,1,0:T(4,128)(4,1)}, u32[]{:S(2)}) copy-start(pred[2,2,256]{2,1,0:T(4,128)(4,1)} %copy-done.53) | copy-start | bytes 3076
  452.3 15.1 %copy-start.81 = (pred[2,4,128]{2,1,0:T(4,128)(4,1)S(1)}, pred[2,4,128]{2,1,0:T(4,128)(4,1)}, u32[]{:S(2)}) copy-start(pred[2,4,128]{2,1,0:T(4,128)(4,1)} %copy-done.80) | copy-start | bytes 3076
  467.4 15.1 %copy-start.30 = (bf16[4,1,512,3,3,64]{2,5,3,4,1,0:T(8,128)(2,1)S(1)}, bf16[4,1,512,3,3,64]{2,5,3,4,1,0:T(8,128)(2,1)}, u32[]{:S(2)}) copy-start(bf16[4,1,512,3,3,64]{2,5,3,4,1,0:T(8,128)(2,1)} %get-tuple-element.246) | copy-start | bytes 7077892
  571.0 199.6 %reduce-scatter.16.cloned.1.call-start = ((), (), s32[]{:S(2)}) async-start(), calls=%async_computation.17 | async-start | bytes 2211840
  616.5 170.7 %reduce-scatter.10.cloned.1.call-start = ((), (), s32[]{:S(2)}) async-start(), calls=%async_computation.14 | async-start | bytes 2433024 | tf_op jit(solution)/shard_map/reduce_scatter | solution.py:332
  620.8 308.4 %reduce-scatter.14.cloned.1.call-start = ((), (), s32[]{:S(2)}) async-start(), calls=%async_computation.16 | async-start | bytes 9732096 | tf_op jit(solution)/shard_map/reduce_scatter | solution.py:334
  631.0 439.3 %reduce-scatter.12.cloned.1.call-start = ((), (), s32[]{:S(2)}) async-start(), calls=%async_computation.15 | async-start | bytes 9732096 | tf_op jit(solution)/shard_map/reduce_scatter | solution.py:333
  660.4 8.2 copy-start.52
  660.4 12.8 %copy-start.2 = (f32[3,512,512]{1,2,0:T(8,128)S(1)}, f32[3,512,512]{1,2,0:T(8,128)}, u32[]{:S(2)}) copy-start(f32[3,512,512]{1,2,0:T(8,128)} %get-tuple-element.251) | copy-start | bytes 9437188
  695.1 8.0 copy-start.10
  710.6 7.6 copy-start.88
  710.6 8.3 copy-start.18
  710.6 8.3 copy-start.62
  710.6 8.3 copy-start.73
  718.9 8.4 copy-start.59
  718.9 8.4 copy-start.22
  727.3 343.0 %copy-start.1 = (f32[32,12]{0,1:T(8,128)S(1)}, f32[32,12]{0,1:T(8,128)}, u32[]{:S(2)}) copy-start(f32[32,12]{0,1:T(8,128)} %param.42) | copy-start | bytes 4612
  (64 other events, 173.4 us)
Sparse Core Ops, SparseCore 0:
  49.5 29.9 all-gather.4
  83.0 55.4 all-gather.6
  141.9 62.6 all-gather.8
  207.9 69.4 all-gather.10
  571.1 39.8 reduce-scatter.7
  616.6 66.6 reduce-scatter.15
  689.1 98.0 reduce-scatter.9
  794.7 134.5 reduce-scatter.13
  935.8 134.5 reduce-scatter.11
where the time goes:
time: 1090 us; the launch traced here: 1080 us
  waiting for transfers between devices  412 us (38%)
  local copies, waits for them, and re-layouts  240 us (22%)
  matrix products  209 us (19%)
  blocking collectives  136 us (12%)
  other arithmetic  49 us (4%)
  between operations  15.6 us (1%)
  starting transfers between devices  13.9 us (1%)
    reduce_scatter x1, waiting for transfers between devices, local(): lax.psum_scatter(grad_w_out, ('dp', 'mp'), scatter_dimension=0, tiled=True)  142 us
    reduce_scatter x1, waiting for transfers between devices, local(): lax.psum_scatter(grad_w_in, ('dp', 'mp'), scatter_dimension=1, tiled=True)  141 us
    all_to_all x1, blocking collectives, local(): lax.all_to_all(packed_grads.reshape(seg_count, mp_count, SEG, 1, head_col...  56.4 us
    unnamed x178, local copies, waits for them, and re-layouts  43.6 us
    psum x1, blocking collectives, local(): lax.psum((grad_gain_attn, grad_gain_ffn, table_full, grad_rules, grad_dle...  40.8 us
    reduce_scatter x1, waiting for transfers between devices, local(): lax.psum_scatter(full_weight_grad.astype(jnp.bfloat16), 'mp', scatter_dim...  40 us
    all_gather x1, blocking collectives, local(): lax.all_gather(w_qkv.astype(jnp.bfloat16), 'dp', axis=0, tiled=True)  38.9 us
    dot_general x1, matrix products, local(): ffn_pre = jnp.dot(normed_ffn, dense_in, preferred_element_type=jnp.float32)  36.9 us
  transfers between devices with their start and end apart: 12, of which 8 were waited for; matrix products, arithmetic and copies ran while one was open for 28% of the time, Pallas kernels for 0%

commit v1 on v0

v1 whole, which is shorter than its diff:
```python
import functools

import jax
import jax.experimental.pallas as pl
import jax.experimental.pallas.tpu as pltpu
import jax.numpy as jnp
import numpy as np
from jax import lax
from jax.sharding import PartitionSpec as P

D = 768
DH = 64
NB = 32
MAXDIST = 128
ADAPT = 48
LEN_LONG = 512
LEN_MID = 256
LEN_SHORT = 128
SEG = 128


NORM_EPS = 1e-06
FULL_PRECISION = lax.Precision.HIGHEST


def rel_buckets(length):
    offsets = np.arange(-(length - 1), length)
    half_count = NB // 2
    exact_count = half_count // 2
    upward = (offsets > 0).astype(np.int64) * half_count
    distance = np.abs(offsets)
    scaled = (
        np.log(np.maximum(distance, 1) / exact_count)
        / np.log(MAXDIST / exact_count)
        * (half_count - exact_count)
    )
    far_bucket = np.minimum(
        exact_count + np.floor(np.maximum(scaled, 0.0)).astype(np.int64), half_count - 1
    )
    return upward + np.where(distance < exact_count, distance, far_bucket)


def normed(values, gain):
    return values * lax.rsqrt(jnp.mean(values * values, axis=-1, keepdims=True) + NORM_EPS) * gain


def gelu_exact(values):
    return jax.nn.gelu(values, approximate=False)


def adapter_weights(phm_rules, down_left, down_right, up_left, up_right):
    w_down = jnp.einsum(
        "iab,ip,iq->apbq", phm_rules, down_left, down_right, precision=FULL_PRECISION
    ).reshape(D, ADAPT)
    w_up = jnp.einsum(
        "iab,ip,iq->apbq", phm_rules, up_left, up_right, precision=FULL_PRECISION
    ).reshape(ADAPT, D)
    return (w_down, w_up)


MESH = pl.DeviceIdType.MESH


class Place:
    def __init__(self, depth):
        d, m = lax.axis_index("dp"), lax.axis_index("mp")
        self.depth = depth
        self.d, self.m = d, m
        self.z, self.x, self.y, self.c = d // 2, d % 2, m // 2, m % 2
        dx, dy, c = 1 - 2 * self.x, 2 - 4 * self.y, self.c
        self.sib = (d, m + 1 - 2 * c)
        self.right, self.left = (d + 2, m), (d - 2, m)
        self.mp_peer = ((d, m + 1 - 2 * c), (d, m + dy), (d, 3 - m))
        self.xn, self.yn = (d + dx, m), (d, m + dy)
        self.a_nbr = (d + (1 - c) * dx, m + c * dy)
        self.b_nbr = (d + c * dx, m + (1 - c) * dy)
        self.a = self.x + c * (self.y - self.x)
        self.b = self.y + c * (self.x - self.y)

    def by_core(self, run):
        for core in (0, 1):
            pl.when(self.c == core)(functools.partial(run, core))

    def flip(self, bit):
        step = 1 << bit
        return (self.d + step * (1 - 2 * ((self.d // step) % 2)), self.m)

    def barrier(self, bits):
        sem = pltpu.get_barrier_semaphore()

        def greet(dev):
            pl.semaphore_signal(sem, 1, device_id=dev, device_id_type=MESH)

        pals = [*self.mp_peer, self.xn] + [self.flip(bit) for bit in range(2, bits)]
        for dev in pals:
            greet(dev)
        pl.when(self.z > 0)(lambda: greet(self.left))
        pl.when(self.z < self.depth - 1)(lambda: greet(self.right))
        ends = jnp.minimum(self.z, 1) + jnp.minimum(self.depth - 1 - self.z, 1)
        pl.semaphore_wait(sem, len(pals) + ends)


def remote(src, dst, send, recv, dev):
    return pltpu.make_async_remote_copy(
        src_ref=src, dst_ref=dst, send_sem=send, recv_sem=recv, device_id=dev, device_id_type=MESH
    )


def slot_of(buf, by_head, p):
    return buf.at[p.y, p.c, p.z, p.x] if by_head else buf.at[p.z, p.x, p.y, p.c]


def pair_of(buf, by_head, core, b, z):
    if by_head:
        return buf.at[b, 0, z] if core == 0 else buf.at[:, 1, z, b]
    return buf.at[z, :, b, 0] if core == 0 else buf.at[z, b, :, 1]


class Gather:
    def __init__(self, p, by_head, shard, buf, send, recv, own):
        self.p, self.by_head, self.shard, self.buf = p, by_head, shard, buf
        self.send, self.recv, self.own = send, recv, own
        n = p.depth
        self.first = remote(shard, slot_of(buf, by_head, p), send.at[5 * n], recv.at[4 * n], p.a_nbr)
        self.keep = pltpu.make_async_copy(shard, slot_of(buf, by_head, p), own)

    @staticmethod
    def sems(n):
        return [
            pltpu.SemaphoreType.DMA((5 * n + 1,)),
            pltpu.SemaphoreType.DMA((4 * n + 1,)),
            pltpu.SemaphoreType.DMA,
        ]

    def _copy(self, core, b, z, kind):
        p, n = self.p, self.p.depth
        ref = pair_of(self.buf, self.by_head, core, b, z)
        if kind == "right":
            return remote(ref, ref, self.send.at[z], self.recv.at[z], p.right)
        if kind == "left":
            return remote(ref, ref, self.send.at[n + z], self.recv.at[z], p.left)
        return remote(ref, ref, self.send.at[2 * n + z], self.recv.at[n + z], p.b_nbr)

    def _sib(self, core, b, z):
        n = self.p.depth
        ref = pair_of(self.buf, self.by_head, core, b, z)
        return remote(ref, ref, self.send.at[3 * n + b * n + z], self.recv.at[2 * n + b * n + z], self.p.sib)

    def start(self):
        self.keep.start()
        self.first.start()

    def _spread(self, core, z, right, left):
        p = self.p
        if right:
            pl.when(p.z < p.depth - 1)(lambda: self._copy(core, p.b, z, "right").start())
        if left:
            pl.when(p.z > 0)(lambda: self._copy(core, p.b, z, "left").start())
        self._copy(core, p.b, z, "b").start()
        self._sib(core, p.b, z).start()

    def along(self, k):
        p = self.p
        if isinstance(k, int) and k == 0:
            self.keep.wait()
            self.first.wait_recv()
            p.by_core(lambda core: self._spread(core, p.z, True, True))
            return

        def from_left(core):
            self._copy(core, p.b, p.z - k, "right").wait_recv()
            self._spread(core, p.z - k, True, False)

        def from_right(core):
            self._copy(core, p.b, p.z + k, "left").wait_recv()
            self._spread(core, p.z + k, False, True)

        pl.when(p.z - k >= 0)(lambda: p.by_core(from_left))
        pl.when(p.z + k < p.depth)(lambda: p.by_core(from_right))

    def across(self, k):
        p = self.p

        def one(z, core):
            self._copy(core, 1 - p.b, z, "b").wait_recv()
            self._sib(core, 1 - p.b, z).start()

        pl.when(p.z - k >= 0)(lambda: p.by_core(lambda core: one(p.z - k, core)))
        if not (isinstance(k, int) and k == 0):
            pl.when(p.z + k < p.depth)(lambda: p.by_core(lambda core: one(p.z + k, core)))

    def finish(self):
        p, n = self.p, self.p.depth

        def each(z, carry):
            def one(core):
                for b in (0, 1):
                    self._sib(1 - core, b, z).wait_recv()

            p.by_core(one)
            return carry

        lax.fori_loop(0, n, each, 0)

    def drain(self):
        p, n = self.p, self.p.depth
        self.first.wait_send()

        def each(z, carry):
            def one(core):
                pl.when(jnp.logical_and(p.z < n - 1, z <= p.z))(
                    lambda: self._copy(core, p.b, z, "right").wait_send()
                )
                pl.when(jnp.logical_and(p.z > 0, z >= p.z))(
                    lambda: self._copy(core, p.b, z, "left").wait_send()
                )
                self._copy(core, p.b, z, "b").wait_send()
                for b in (0, 1):
                    self._sib(core, b, z).wait_send()

            p.by_core(one)
            return carry

        lax.fori_loop(0, n, each, 0)


class Exchange:
    def __init__(self, p, src, dst, send, recv, own):
        m = p.m
        c, other = m % 2, 1 - m % 2
        self.local = [
            pltpu.make_async_copy(src.at[m], dst.at[m], own.at[0]),
            pltpu.make_async_copy(src.at[4 + c], dst.at[4 + c], own.at[1]),
            pltpu.make_async_copy(src.at[pl.ds(6, 2)], dst.at[pl.ds(6, 2)], own.at[2]),
        ]
        self.out = [
            remote(src.at[dev[1]], dst.at[m], send.at[j], recv.at[j], dev)
            for j, dev in enumerate(p.mp_peer)
        ] + [remote(src.at[4 + other], dst.at[4 + c], send.at[3], recv.at[3], p.sib)]

    @staticmethod
    def sems():
        return [
            pltpu.SemaphoreType.DMA((4,)),
            pltpu.SemaphoreType.DMA((4,)),
            pltpu.SemaphoreType.DMA((3,)),
        ]

    def start(self):
        for copy in self.out + self.local:
            copy.start()

    def finish(self):
        for copy in self.local:
            copy.wait()
        for copy in self.out:
            copy.wait_recv()

    def drain(self):
        for copy in self.out:
            copy.wait_send()


def add_rows(dst, src, rows):
    step = 32 if rows % 32 == 0 else 16

    def one(i, carry):
        at = pl.ds(pl.multiple_of(i * step, step), step)
        total = dst[at, :].astype(jnp.float32) + src[at, :].astype(jnp.float32)
        dst[at, :] = total.astype(dst.dtype)
        return carry

    lax.fori_loop(0, rows // step, one, 0)


class Scatter:
    def __init__(self, p, by_head, part, total, half, quarter, arrive, last, send, recv):
        self.p, self.by_head, self.part, self.total = p, by_head, part, total
        self.half, self.quarter, self.arrive, self.last = half, quarter, arrive, last
        self.send, self.recv = send, recv
        self.rows = part.shape[-2]

    @staticmethod
    def scratch(n, rows, cols, dtype=jnp.bfloat16):
        return [
            pltpu.VMEM((n, 2, 2, rows, cols), dtype),
            pltpu.VMEM((n, 2, rows, cols), dtype),
            pltpu.VMEM((n + 1, 2, rows, cols), dtype),
            pltpu.VMEM((rows, cols), dtype),
            pltpu.SemaphoreType.DMA((3 * n + 1,)),
            pltpu.SemaphoreType.DMA((3 * n + 2,)),
        ]

    def order(self, k):
        n = self.p.depth
        base = k // 2 if k % 2 == 0 else n - 1 - k // 2
        near = 1 - jnp.minimum(self.p.z // max(n // 2, 1), 1)
        return base + near * (n - 1 - 2 * base)

    def _region(self, core, z):
        return self.part.at[:, core, z] if self.by_head else self.part.at[z, :, :, core]

    def _half_pair(self, core, b, z):
        over_first = (core == 0) != self.by_head
        return self.half.at[z, :, b] if over_first else self.half.at[z, b]

    def _sib(self, core, z):
        return remote(
            self._region(1 - core, z), self.half.at[z], self.send.at[z], self.recv.at[z], self.p.sib
        )

    def _b(self, core, z):
        n, p = self.p.depth, self.p
        return remote(
            self._half_pair(core, 1 - p.b, z), self.quarter.at[z], self.send.at[n + z], self.recv.at[n + z], p.b_nbr
        )

    def _right(self, z):
        n, p = self.p.depth, self.p
        return remote(
            self.quarter.at[z], self.arrive.at[z], self.send.at[2 * n + z], self.recv.at[2 * n + z], p.right
        )

    def _left(self, z, goal):
        n, p = self.p.depth, self.p
        return remote(
            self.quarter.at[z], self.arrive.at[goal], self.send.at[2 * n + z], self.recv.at[2 * n + goal], p.left
        )

    def _a(self):
        n, p = self.p.depth, self.p
        return remote(
            self.quarter.at[p.z, 1 - p.a], self.last, self.send.at[3 * n], self.recv.at[3 * n + 1], p.a_nbr
        )

    def start(self, k):
        z = self.order(k)
        self.p.by_core(lambda core: self._sib(core, z).start())

    def to_half(self, k):
        z = self.order(k)

        def one(core):
            self._sib(core, z).wait_recv()
            region = self._region(core, z)
            for i in (0, 1):
                for j in (0, 1):
                    add_rows(self.half.at[z, i, j], region.at[i, j], self.rows)
            self._b(core, z).start()

        self.p.by_core(one)

    def to_quarter(self, k):
        z = self.order(k)

        def one(core):
            self._b(core, z).wait_recv()
            for i in (0, 1):
                add_rows(self.quarter.at[z, i], self._half_pair(core, self.p.b, z).at[i], self.rows)

        self.p.by_core(one)

    def _take(self, z, slot):
        for i in (0, 1):
            add_rows(self.quarter.at[z, i], self.arrive.at[slot, i], self.rows)

    def pass_on(self, k):
        p, n = self.p, self.p.depth
        z = self.order(k)

        def rightward():
            def take():
                self._right(z).wait_recv()
                self._take(z, z)

            pl.when(p.z > 0)(take)
            self._right(z).start()

        def leftward():
            def take():
                self._left(z, z).wait_recv()
                self._take(z, z)

            pl.when(p.z < n - 1)(take)
            pl.when(z == p.z - 1)(lambda: self._left(z, n).start())
            pl.when(z < p.z - 1)(lambda: self._left(z, z).start())

        pl.when(z > p.z)(rightward)
        pl.when(z < p.z)(leftward)

    def collect(self):
        p, n = self.p, self.p.depth

        def from_left():
            self._right(p.z).wait_recv()
            self._take(p.z, p.z)

        def from_right():
            self._left(p.z, n).wait_recv()
            self._take(p.z, n)

        pl.when(p.z > 0)(from_left)
        pl.when(p.z < n - 1)(from_right)
        self._a().start()

    def finish(self):
        p = self.p
        self._a().wait_recv()
        self.total[...] = self.quarter[p.z, p.a].astype(jnp.float32) + self.last[...].astype(jnp.float32)

    def drain(self):
        p, n = self.p, self.p.depth
        self._a().wait_send()

        def each(z, carry):
            def one(core):
                self._sib(core, z).wait_send()
                self._b(core, z).wait_send()

            p.by_core(one)
            pl.when(z != p.z)(lambda: self._right(z).wait_send())
            return carry

        lax.fori_loop(0, n, each, 0)

    def steps(self):
        n = self.p.depth
        todo = [lambda: [self.start(k) for k in range(n)]]
        todo += [functools.partial(self.to_half, k) for k in range(n)]
        for k in range(n):
            todo.append(functools.partial(lambda k: (self.to_quarter(k), self.pass_on(k)), k))
        return todo + [self.collect, self.finish]


class Sum:
    def __init__(self, p, bits, value, slots, send, recv):
        self.p, self.bits, self.value, self.slots = p, bits, value, slots
        self.send, self.recv = send, recv

    @staticmethod
    def scratch(bits, rows):
        return [
            pltpu.VMEM((2 * (bits + 2), rows, 128), jnp.float32),
            pltpu.SemaphoreType.DMA((bits + 2,)),
            pltpu.SemaphoreType.DMA((bits + 2,)),
        ]

    def _copy(self, s):
        p = self.p
        dev = (p.sib, p.yn, *[p.flip(bit) for bit in range(self.bits)])[s]
        return remote(self.slots.at[2 * s], self.slots.at[2 * s + 1], self.send.at[s], self.recv.at[s], dev)

    def steps(self):
        def begin():
            self.slots[0] = self.value[...]
            self._copy(0).start()

        def one(s):
            self._copy(s).wait_recv()
            total = self.slots[2 * s] + self.slots[2 * s + 1]
            if s == self.bits + 1:
                self.value[...] = total
            else:
                self.slots[2 * s + 2] = total
                self._copy(s + 1).start()

        return [begin] + [functools.partial(one, s) for s in range(self.bits + 2)]

    def drain(self):
        for s in range(self.bits + 2):
            self._copy(s).wait_send()


def in_waves(lists, lag):
    for t in range(max(len(todo) + lag * r for r, todo in enumerate(lists))):
        for r, todo in enumerate(lists):
            if 0 <= t - lag * r < len(todo):
                todo[t - lag * r]()


def gather_kernel(p_depth, tok, cot, wq, wo, wi, wu, tok_s, cot_s, gq, go, gi, gu, *sems):
    p = Place(p_depth)
    n = p_depth
    arrays = []
    for i, (by_head, shard, buf) in enumerate(
        ((True, wq, gq), (False, wo, go), (False, wi, gi), (False, wu, gu))
    ):
        arrays.append(Gather(p, by_head, shard, buf, *sems[3 * i : 3 * i + 3]))
    rows = [Exchange(p, tok, tok_s, *sems[12:15]), Exchange(p, cot, cot_s, *sems[15:18])]
    p.barrier(0)
    for g in arrays:
        g.start()
    rows[0].start()
    if n <= 8:
        for k in range(n):
            for g in arrays:
                g.along(k)
            if k > 0:
                for g in arrays:
                    g.across(k - 1)
            if k == 1:
                rows[1].start()
        for g in arrays:
            g.across(n - 1)
    else:
        for g in arrays:
            g.along(0)
            lax.fori_loop(1, n, lambda k, carry: (g.along(k), carry)[1], 0)
        rows[1].start()
        for g in arrays:
            g.across(0)
            lax.fori_loop(1, n, lambda k, carry: (g.across(k), carry)[1], 0)
    for g in arrays + rows:
        g.finish()
    for g in arrays + rows:
        g.drain()


def gather_all(depth, tok, cot, shards):
    hbm = pl.BlockSpec(memory_space=pl.ANY)
    outs = [jax.ShapeDtypeStruct(tok.shape, tok.dtype)] * 2
    for i, s in enumerate(shards):
        lead = (2, 2, depth, 2) if i == 0 else (depth, 2, 2, 2)
        outs.append(jax.ShapeDtypeStruct(lead + s.shape, s.dtype))
    sems = Gather.sems(depth) * 4 + Exchange.sems() * 2
    return pl.pallas_call(
        functools.partial(gather_kernel, depth),
        out_shape=outs,
        in_specs=[hbm] * 6,
        out_specs=[hbm] * 6,
        scratch_shapes=sems,
        compiler_params=pltpu.CompilerParams(collective_id=0, has_side_effects=True),
        name="gather",
    )(tok, cot, *shards)


def scatter_kernel(depth, bits, pq, po, pi, pu, small, out_s, gtok_s, oq, oo, oi, ou, small_o, out, gtok, *scr):
    p = Place(depth)
    arrays = []
    for i, (by_head, part, total) in enumerate(
        ((False, pu, ou), (False, pi, oi), (False, po, oo), (True, pq, oq))
    ):
        arrays.append(Scatter(p, by_head, part, total, *scr[6 * i : 6 * i + 6]))
    rows = [Exchange(p, out_s, out, *scr[24:27]), Exchange(p, gtok_s, gtok, *scr[27:30])]
    small_o[...] = small[...]
    sums = Sum(p, bits, small_o, *scr[30:33])
    p.barrier(bits)
    for r in rows:
        r.start()
    in_waves([sums.steps()] + [g.steps() for g in arrays], min(depth, 4))
    for r in rows:
        r.finish()
    for g in arrays + rows + [sums]:
        g.drain()


def scatter_all(depth, bits, parts, small, out_s, gtok_s):
    hbm = pl.BlockSpec(memory_space=pl.ANY)
    vmem = pl.BlockSpec(memory_space=pltpu.VMEM)
    outs = [jax.ShapeDtypeStruct(s.shape[4:], jnp.float32) for s in parts]
    outs += [jax.ShapeDtypeStruct(small.shape, jnp.float32)]
    outs += [jax.ShapeDtypeStruct(out_s.shape, out_s.dtype)] * 2
    scr = []
    for s in (parts[3], parts[2], parts[1], parts[0]):
        scr += Scatter.scratch(depth, *s.shape[4:])
    scr += Exchange.sems() * 2 + Sum.scratch(bits, small.shape[0])
    return pl.pallas_call(
        functools.partial(scatter_kernel, depth, bits),
        out_shape=outs,
        in_specs=[vmem] * 5 + [hbm] * 2,
        out_specs=[vmem] * 5 + [hbm] * 2,
        scratch_shapes=scr,
        compiler_params=pltpu.CompilerParams(
            collective_id=1, has_side_effects=True, vmem_limit_bytes=60 * 2**20
        ),
        name="scatter",
    )(*parts, small, out_s, gtok_s)

SPANS = ((0, LEN_LONG), (LEN_LONG, LEN_MID), (LEN_LONG + LEN_MID, LEN_SHORT), (LEN_LONG + LEN_MID + LEN_SHORT, LEN_SHORT))
TILE = 128
QKV_PAD = 640
CTX_PAD = 256
MASK_LOW = -1e9
NN = (((1,), (0,)), ((), ()))
NT = (((1,), (1,)), ((), ()))


def dot(a, b, dims=NN):
    return lax.dot_general(a, b, dims, preferred_element_type=jnp.float32)


def offset_row(pos_table):
    buckets = rel_buckets(257)
    offset = np.clip(256 - np.arange(512), -256, 256) + 256
    onehot = (buckets[offset][:, None] == np.arange(NB)[None, :]).astype(np.float32)
    return jnp.einsum("rb,bh->hr", jnp.asarray(onehot), pos_table, precision=FULL_PRECISION)


def table_onehot():
    buckets = rel_buckets(257)
    offset = np.clip(256 - np.arange(512), -256, 256) + 256
    index = np.concatenate([buckets[offset], np.full(128, NB // 2 - 1), np.full(128, NB - 1)])
    return (index[:, None] == np.arange(NB)[None, :]).astype(np.float32)


def bias_tiles(row):
    spread = pltpu.roll(jnp.broadcast_to(row, (TILE, 512)), 0, 1, stride=1, stride_axis=0)
    far = [jnp.broadcast_to(row[:, at : at + 1], (TILE, TILE)) for at in (511, 0)]
    near = [spread[:, 256 - 128 * delta : 384 - 128 * delta] for delta in (-1, 0, 1)]
    return [far[0], *near, far[1]]


def diagonal_sums(tiles):
    grid = jnp.concatenate([jnp.zeros((TILE, TILE), jnp.float32), tiles[2], tiles[1], tiles[0]], axis=1)
    rows = TILE
    while rows > 8:
        rows //= 2
        grid = grid[:rows] + pltpu.roll(grid[rows:], 512 - rows, 1)
    total = grid[0:1]
    for r in range(1, 8):
        total = total + pltpu.roll(grid[r : r + 1], 512 - r, 1)
    return total


def swap_halves(tile):
    return jnp.concatenate([tile[:, DH:], tile[:, :DH]], axis=1)


def lanes_below(shape, at=DH):
    return lax.broadcasted_iota(jnp.int32, shape, len(shape) - 1) < at


def key_side(qk, mask):
    swapped = swap_halves(qk)
    return jnp.where(lanes_below(qk.shape), swapped, mask), swapped


def query_side(qk):
    lane = lax.broadcasted_iota(jnp.int32, qk.shape, 1)
    return jnp.where(lane < DH, qk, jnp.where(lane == DH, 1.0, 0.0).astype(qk.dtype))


def probabilities(keys, queries, tiles, q0, length, width):
    scores = dot(keys, queries, NT)
    blocks = []
    for kb in range(length // TILE):
        deltas = [max(-2, min(2, kb - (q0 + qi))) + 2 for qi in range(width // TILE)]
        bias = tiles[deltas[0]] if len(deltas) == 1 else jnp.concatenate([tiles[d] for d in deltas], axis=1)
        blocks.append(scores[kb * TILE : (kb + 1) * TILE] + bias)
    top = blocks[0]
    for block in blocks[1:]:
        top = jnp.maximum(top, block)
    top = jnp.max(top, axis=0, keepdims=True)
    blocks = [jnp.exp(block - top) for block in blocks]
    total = blocks[0]
    for block in blocks[1:]:
        total = total + block
    inverse = 1.0 / jnp.sum(total, axis=0, keepdims=True)
    return [block * inverse for block in blocks]


def join(blocks, axis=0):
    return blocks[0] if len(blocks) == 1 else jnp.concatenate(blocks, axis=axis)


def attend_group(packed, mask_ref, rows, context):
    tiles = [bias_tiles(rows[h : h + 1, :]) for h in range(3)]
    for offset, length in SPANS:
        span = pl.ds(offset, length)
        mask = mask_ref[span, :]
        keys = [key_side(packed[span, h * TILE : (h + 1) * TILE], mask)[0] for h in range(3)]
        values = [packed[span, (3 + t) * TILE : (4 + t) * TILE].T for t in range(2)]
        width = min(length, 256)
        for q0 in range(0, length, width):
            here = pl.ds(offset + q0, width)
            outs = []
            for h in range(3):
                queries = query_side(packed[here, h * TILE : (h + 1) * TILE])
                probs = probabilities(keys[h], queries, tiles[h], q0 // TILE, length, width)
                probs = join([block.astype(jnp.bfloat16) for block in probs])
                full = dot(values[h // 2], probs)
                outs.append(full[(h % 2) * DH : (h % 2 + 1) * DH])
            context[here, :TILE] = jnp.concatenate(outs[:2], axis=0).T.astype(jnp.bfloat16)
            last = jnp.concatenate([outs[2], jnp.zeros_like(outs[2])], axis=0)
            context[here, TILE:] = last.T.astype(jnp.bfloat16)


def attend_group_back(packed, mask_ref, rows, grad_context, grad_packed, sums):
    far_shape = (TILE, TILE)
    tiles = [bias_tiles(rows[h : h + 1, :]) for h in range(3)]
    near = [[None] * 3 for _ in range(3)]
    far = [[jnp.zeros(far_shape, jnp.float32)] * 2 for _ in range(3)]
    for offset, length in SPANS:
        span = pl.ds(offset, length)
        mask = mask_ref[span, :]
        width = min(length, 256)
        grad_values = [None, None]
        for h in range(3):
            at = pl.ds(h * TILE, TILE)
            qk = packed[span, at]
            low = lanes_below(qk.shape)
            keys, swapped = key_side(qk, mask)
            upper_queries = jnp.where(low, jnp.zeros_like(qk), swapped)
            plain_keys = jnp.where(low, swapped, jnp.zeros_like(qk)).T
            values = packed[span, (3 + h // 2) * TILE : (4 + h // 2) * TILE]
            grad_keys = None
            grad_queries = []
            for q0 in range(0, length, width):
                here = pl.ds(offset + q0, width)
                probs = probabilities(keys, query_side(packed[here, at]), tiles[h], q0 // TILE, length, width)
                g_tile = grad_context[here, (h // 2) * TILE : (h // 2 + 1) * TILE]
                own = lanes_below(g_tile.shape) == (h % 2 == 0)
                g_tile = jnp.where(own, g_tile, jnp.zeros_like(g_tile))
                g_probs = dot(values, g_tile, NT)
                g_blocks = [g_probs[kb * TILE : (kb + 1) * TILE] for kb in range(length // TILE)]
                total = probs[0] * g_blocks[0]
                for kb in range(1, length // TILE):
                    total = total + probs[kb] * g_blocks[kb]
                centre = jnp.sum(total, axis=0, keepdims=True)
                low_probs = join([block.astype(jnp.bfloat16) for block in probs])
                g_scores = [(a * (g - centre)).astype(jnp.bfloat16) for a, g in zip(probs, g_blocks)]
                for kb, block in enumerate(g_scores):
                    wide = block.astype(jnp.float32)
                    for qi in range(width // TILE):
                        piece = wide[:, qi * TILE : (qi + 1) * TILE]
                        delta = kb - (q0 // TILE + qi)
                        if abs(delta) <= 1:
                            held = near[h][delta + 1]
                            near[h][delta + 1] = piece if held is None else held + piece
                        else:
                            side = 0 if delta < 0 else 1
                            far[h][side] = far[h][side] + piece
                g_scores = join(g_scores)
                g_v = dot(low_probs, g_tile)
                grad_values[h // 2] = g_v if grad_values[h // 2] is None else grad_values[h // 2] + g_v
                g_k = dot(g_scores, upper_queries[q0 : q0 + width])
                grad_keys = g_k if grad_keys is None else grad_keys + g_k
                grad_queries.append(dot(plain_keys, g_scores).T)
            grad_packed[span, at] = (join(grad_queries) + grad_keys).astype(jnp.bfloat16)
        for t in range(2):
            grad_packed[span, (3 + t) * TILE : (4 + t) * TILE] = grad_values[t].astype(jnp.bfloat16)
    for h in range(3):
        sums[h : h + 1, :512] = diagonal_sums(near[h])
        for side in range(2):
            sums[h : h + 1, 512 + side * TILE : 640 + side * TILE] = jnp.sum(far[h][side], axis=0, keepdims=True)


def attention_kernel(x_ref, gain, w_ref, mask, rows, normed_out, packed, context):
    @pl.when(pl.program_id(0) == 0)
    def _():
        x = x_ref[...].astype(jnp.float32)
        scale = lax.rsqrt(jnp.mean(x * x, axis=-1, keepdims=True) + NORM_EPS)
        normed_out[...] = (x * scale * gain[...]).astype(jnp.bfloat16)

    packed[0] = dot(normed_out[...], w_ref[0]).astype(jnp.bfloat16)
    attend_group(packed.at[0], mask, rows[0], context.at[0])


def attention(x, gain, w, mask, rows):
    n = x.shape[0]
    bf = jnp.bfloat16
    return pl.pallas_call(
        attention_kernel,
        grid=(4,),
        out_shape=[
            jax.ShapeDtypeStruct((n, D), bf),
            jax.ShapeDtypeStruct((4, n, QKV_PAD), bf),
            jax.ShapeDtypeStruct((4, n, CTX_PAD), bf),
        ],
        in_specs=[
            pl.BlockSpec((n, D), lambda i: (0, 0)),
            pl.BlockSpec((1, D), lambda i: (0, 0)),
            pl.BlockSpec((1, D, QKV_PAD), lambda i: (i, 0, 0)),
            pl.BlockSpec((n, TILE), lambda i: (0, 0)),
            pl.BlockSpec((1, 3, 512), lambda i: (i, 0, 0)),
        ],
        out_specs=[
            pl.BlockSpec((n, D), lambda i: (0, 0)),
            pl.BlockSpec((1, n, QKV_PAD), lambda i: (i, 0, 0)),
            pl.BlockSpec((1, n, CTX_PAD), lambda i: (i, 0, 0)),
        ],
        compiler_params=pltpu.CompilerParams(vmem_limit_bytes=56 * 2**20),
        name="attention",
    )(x, gain, w, mask, rows)


def attention_back_kernel(packed, grad_context, mask, rows, grad_packed, sums):
    attend_group_back(packed.at[0], mask, rows[0], grad_context.at[0], grad_packed.at[0], sums.at[0])


def attention_back(packed, grad_context, mask, rows):
    n = packed.shape[1]
    return pl.pallas_call(
        attention_back_kernel,
        grid=(4,),
        out_shape=[
            jax.ShapeDtypeStruct((4, n, QKV_PAD), jnp.bfloat16),
            jax.ShapeDtypeStruct((4, 3, 768), jnp.float32),
        ],
        in_specs=[
            pl.BlockSpec((1, n, QKV_PAD), lambda i: (i, 0, 0)),
            pl.BlockSpec((1, n, CTX_PAD), lambda i: (i, 0, 0)),
            pl.BlockSpec((n, TILE), lambda i: (0, 0)),
            pl.BlockSpec((1, 3, 512), lambda i: (i, 0, 0)),
        ],
        out_specs=[
            pl.BlockSpec((1, n, QKV_PAD), lambda i: (i, 0, 0)),
            pl.BlockSpec((1, 3, 768), lambda i: (i, 0, 0)),
        ],
        compiler_params=pltpu.CompilerParams(vmem_limit_bytes=56 * 2**20),
        name="attention_back",
    )(packed, grad_context, mask, rows)


def head_columns(w):
    qk = w[:, :, : 2 * DH].reshape(w.shape[0], 6 * DH)
    v = w[:, :, 2 * DH :].reshape(w.shape[0], 3 * DH)
    return jnp.pad(jnp.concatenate([qk, v], axis=1), ((0, 0), (0, QKV_PAD - 9 * DH)))


def from_head_columns(g):
    qk = g[:, : 6 * DH].reshape(g.shape[0], 3, 2 * DH)
    v = g[:, 6 * DH : 9 * DH].reshape(g.shape[0], 3, DH)
    return jnp.concatenate([qk, v], axis=2)


def key_mask(live):
    lane = jnp.arange(TILE)[None, :]
    return jnp.where((lane == DH) & ~live[:, None], MASK_LOW, 0.0).astype(jnp.bfloat16)


def round_up(n, m):
    return -(-n // m) * m


def pad_rows(a, rows):
    return jnp.pad(a, ((0, rows - a.shape[0]), (0, 0)))


HEADS = 12


def local(
    tokens,
    lengths,
    cotangent,
    w_qkv,
    w_o,
    w_in,
    w_out,
    gain_attn,
    gain_ffn,
    pos_table,
    phm_rules,
    down_left,
    down_right,
    up_left,
    up_right,
):
    dp_count, mp_count = lax.axis_size("dp"), lax.axis_size("mp")
    depth = dp_count // 2
    bits = dp_count.bit_length() - 1
    devices = dp_count * mp_count
    member = lax.axis_index("mp")
    tok_rows = tokens.shape[0]
    seg_count = tok_rows // SEG
    o_rows, in_rows, q_rows = w_o.shape[0], w_in.shape[1], w_qkv.shape[0]
    bf = jnp.bfloat16
    wq = pad_rows(head_columns(w_qkv.astype(bf)), round_up(q_rows, 16))
    wo = pad_rows(w_o.astype(bf), round_up(o_rows, 16))
    wi = pad_rows(w_in.astype(bf).T, round_up(in_rows, 16))
    wu = pad_rows(w_out.astype(bf), round_up(in_rows, 16))
    tok_s, cot_s, gq, go, gi, gu = gather_all(
        depth, tokens.reshape(seg_count, SEG, D), cotangent.reshape(seg_count, SEG, D), (wq, wo, wi, wu)
    )

    def plain(g, rows):
        return g.reshape(devices, g.shape[-2], D)[:, :rows].reshape(devices * rows, D)

    dense_o, dense_in_t, dense_out = plain(go, o_rows), plain(gi, in_rows), plain(gu, in_rows)
    qkv_full = gq.reshape(mp_count, dp_count, wq.shape[0], QKV_PAD)[:, :, :q_rows].reshape(mp_count, D, QKV_PAD)
    tokens_s = tok_s.reshape(tok_rows, D)
    own_lengths = jnp.stack([
        lengths[member], lengths[4 + member // 2 + 2 * (member % 2)], lengths[8 + member], lengths[12 + member]
    ])
    shapes = ((LEN_LONG, 1), (LEN_MID, 1), (LEN_SHORT, 2))
    pieces = []
    first = 0
    for length, seqs in shapes:
        spots = jnp.arange(length, dtype=jnp.int32)
        pieces.append((spots[None, :] < own_lengths[first : first + seqs, None]).reshape(-1))
        first += seqs
    live = jnp.concatenate(pieces)
    x_float = tokens_s.astype(jnp.float32)
    mask = key_mask(live)
    rows = offset_row(pos_table).reshape(mp_count, 3, 512)
    normed_attn, packed, context = attention(tokens_s, gain_attn[None], qkv_full, mask, rows)
    context_rows = context[:, :, : 3 * DH].transpose(1, 0, 2).reshape(tok_rows, D)
    midway = x_float + jnp.dot(context_rows, dense_o, preferred_element_type=jnp.float32)
    normed_ffn = normed(midway, gain_ffn).astype(bf)
    ffn_pre = jnp.dot(normed_ffn, dense_in_t.T, preferred_element_type=jnp.float32)
    ffn_act = gelu_exact(ffn_pre).astype(bf)
    ffn_out = jnp.dot(ffn_act, dense_out, preferred_element_type=jnp.float32)
    ffn_low = ffn_out.astype(bf)
    w_down, w_up = adapter_weights(phm_rules, down_left, down_right, up_left, up_right)
    down_low = w_down.astype(bf)
    up_low = w_up.astype(bf)
    squeezed = jnp.dot(ffn_low, down_low, preferred_element_type=jnp.float32)
    lifted = gelu_exact(squeezed).astype(bf)
    result = (midway + ffn_out + jnp.dot(lifted, up_low, preferred_element_type=jnp.float32)).astype(bf)
    grad_out = cot_s.reshape(tok_rows, D).astype(jnp.float32) * live[:, None].astype(jnp.float32)
    grad_out_low = grad_out.astype(bf)
    grad_w_up = jnp.dot(lifted.T, grad_out_low, preferred_element_type=jnp.float32)
    _, gelu_back_sq = jax.vjp(gelu_exact, squeezed)
    grad_sq = gelu_back_sq(jnp.dot(grad_out_low, up_low.T, preferred_element_type=jnp.float32))[0].astype(bf)
    grad_w_down = jnp.dot(ffn_low.T, grad_sq, preferred_element_type=jnp.float32)
    grad_ffn = (grad_out + jnp.dot(grad_sq, down_low.T, preferred_element_type=jnp.float32)).astype(bf)
    grad_w_out = jnp.dot(ffn_act.T, grad_ffn, preferred_element_type=jnp.float32).astype(bf)
    _, gelu_back_pre = jax.vjp(gelu_exact, ffn_pre)
    grad_pre = gelu_back_pre(jnp.dot(grad_ffn, dense_out.T, preferred_element_type=jnp.float32))[0].astype(bf)
    grad_w_in = jnp.dot(grad_pre.T, normed_ffn, preferred_element_type=jnp.float32).astype(bf)
    _, norm_back_ffn = jax.vjp(normed, midway, gain_ffn)
    grad_mid_part, grad_gain_ffn = norm_back_ffn(jnp.dot(grad_pre, dense_in_t, preferred_element_type=jnp.float32))
    grad_mid = grad_out + grad_mid_part
    grad_mid_low = grad_mid.astype(bf)
    grad_w_o = jnp.dot(context_rows.T, grad_mid_low, preferred_element_type=jnp.float32).astype(bf)
    grad_context = jnp.dot(grad_mid_low, dense_o.T, preferred_element_type=jnp.float32).astype(bf)
    grad_context = grad_context.reshape(tok_rows, mp_count, 3 * DH).transpose(1, 0, 2)
    grad_context = jnp.pad(grad_context, ((0, 0), (0, 0), (0, CTX_PAD - 3 * DH)))
    packed_grads, sums = attention_back(packed, grad_context, mask, rows)
    table_grad = jnp.einsum("hr,rb->bh", sums.reshape(HEADS, 768), table_onehot(), precision=FULL_PRECISION)
    grad_w_qkv = jnp.einsum("td,mtc->mdc", normed_attn, packed_grads, preferred_element_type=jnp.float32).astype(bf)
    grad_n1 = jnp.einsum("mtc,mdc->td", packed_grads, qkv_full, preferred_element_type=jnp.float32)
    _, norm_back_attn = jax.vjp(normed, x_float, gain_attn)
    grad_x_part, grad_gain_attn = norm_back_attn(grad_n1)
    grad_tokens = (grad_mid + grad_x_part).astype(bf)
    _, adapter_back = jax.vjp(adapter_weights, phm_rules, down_left, down_right, up_left, up_right)
    small_list = (grad_gain_attn, grad_gain_ffn, table_grad) + adapter_back((grad_w_down, grad_w_up))
    flat = jnp.concatenate([s.reshape(-1) for s in small_list])
    small_rows = round_up(-(-flat.size // 128), 8)
    small = jnp.pad(flat, (0, small_rows * 128 - flat.size)).reshape(small_rows, 128)

    def slots(g, rows):
        padded = jnp.pad(g.reshape(devices, rows, D), ((0, 0), (0, round_up(rows, 16) - rows), (0, 0)))
        return padded.reshape(depth, 2, 2, 2, padded.shape[1], D)

    part_q = grad_w_qkv.reshape(mp_count, dp_count, q_rows, QKV_PAD)
    part_q = jnp.pad(part_q, ((0, 0), (0, 0), (0, wq.shape[0] - q_rows), (0, 0)))
    part_q = part_q.reshape(2, 2, depth, 2, wq.shape[0], QKV_PAD)
    oq, oo, oi, ou, summed, out, gtok = scatter_all(
        depth,
        bits,
        (part_q, slots(grad_w_o, o_rows), slots(grad_w_in, in_rows), slots(grad_w_out, in_rows)),
        small,
        result.reshape(seg_count, SEG, D),
        grad_tokens.reshape(seg_count, SEG, D),
    )
    smalls = []
    flat = summed.reshape(-1)
    first = 0
    for s in small_list:
        smalls.append(flat[first : first + s.size].reshape(s.shape))
        first += s.size
    return (
        out.reshape(tok_rows, D),
        gtok.reshape(tok_rows, D),
        from_head_columns(oq[:q_rows]),
        oo[:o_rows],
        oi[:in_rows].T,
        ou[:in_rows],
        *smalls,
    )


def solution(mesh):
    return jax.shard_map(
        local,
        mesh=mesh,
        in_specs=(
            P(("dp", "mp"), None),
            P("dp"),
            P(("dp", "mp"), None),
            P("dp", "mp", None),
            P(("dp", "mp"), None),
            P(None, ("dp", "mp")),
            P(("dp", "mp"), None),
            P(),
            P(),
            P(),
            P(),
            P(),
            P(),
            P(),
            P(),
        ),
        out_specs=(
            P(("dp", "mp"), None),
            P(("dp", "mp"), None),
            P("dp", "mp", None),
            P(("dp", "mp"), None),
            P(None, ("dp", "mp")),
            P(("dp", "mp"), None),
            P(),
            P(),
            P(),
            P(),
            P(),
            P(),
            P(),
            P(),
        ),
        check_vma=False,
    )
```

time: 1090 us -> 473 us (0.43)
  waiting for transfers between devices: 412 us -> 0 us
  Pallas kernels: 0 us -> 256 us
  local copies, waits for them, and re-layouts: 240 us -> 56.8 us
  blocking collectives: 136 us -> 0 us
  matrix products: 209 us -> 136 us
  other arithmetic: 49 us -> 17.6 us
  between operations: 15.6 us -> 1.61 us
  starting transfers between devices: 13.9 us -> 0 us
    reduce_scatter x4 -> x0, waiting for transfers between devices: 338 us -> none  [the longest x1 142 us: local(): lax.psum_scatter(grad_w_out, ('dp', 'mp'), scatter_dimension=0, tiled=True)]
    pallas_call x0 -> x4, Pallas kernels: none -> 256 us  [the longest x1 119 us: scatter_all(): pl.pallas_call(functools.partial(scatter_kernel, depth, bits), out_shape=...]
    reshape x23 -> x19, local copies, waits for them, and re-layouts: 95.8 us -> 8.6 us  [the longest x5 2.76 us: local(): smalls.append(flat[first:first + s.size].reshape(s.shape))]
    dot_general x69 -> x8, matrix products: 150 us -> 79.6 us  [the longest x1 36.9 us: local(): jnp.dot(normed_ffn, dense_in_t.T, preferred_element_type=jnp.float32)]
    all_to_all x1 -> x0, blocking collectives: 56.4 us -> none  [local(): lax.all_to_all(packed_grads.reshape(seg_count, mp_count, SEG, 1, head_col...]
    all_to_all x3 -> x0, waiting for transfers between devices: 47.2 us -> none  [the longest x1 24 us: local(): lax.all_to_all(context_heads.reshape(seg_count, mp_count, SEG, 1, local_h...]
    psum x1 -> x0, blocking collectives: 40.8 us -> none  [local(): lax.psum((grad_gain_attn, grad_gain_ffn, table_full, grad_rules, grad_dle...]
    all_gather x1 -> x0, blocking collectives: 38.9 us -> none  [local(): lax.all_gather(w_qkv.astype(jnp.bfloat16), 'dp', axis=0, tiled=True)]
  transfers between devices with their start and end apart: 12 -> 0, of which waited for: 8 -> 0; matrix products, arithmetic and copies ran while one was open for 28% -> 0% of each run, Pallas kernels for 0% -> 0%
where the time goes in v1:
time: 473 us; the launch traced here: 468 us
  Pallas kernels  256 us (54%)
  matrix products  136 us (29%)
  local copies, waits for them, and re-layouts  56.8 us (12%)
  other arithmetic  17.6 us (4%)
    pallas_call x1, Pallas kernels, scatter_all(): pl.pallas_call(functools.partial(scatter_kernel, depth, bits), out_shape=...  119 us
    pallas_call x1, Pallas kernels, gather_all(): pl.pallas_call(functools.partial(gather_kernel, depth), out_shape=outs, i...  79.9 us
    dot_general x1, matrix products, local(): jnp.dot(normed_ffn, dense_in_t.T, preferred_element_type=jnp.float32)  36.9 us
    pallas_call x1, Pallas kernels, attention_back(): pl.pallas_call(attention_back_kernel, grid=(4,), out_shape=[jax.ShapeDtyp...  31 us
    pallas_call x1, Pallas kernels, attention(): pl.pallas_call(attention_kernel, grid=(4,), out_shape=[jax.ShapeDtypeStru...  25.3 us
    dot_general x1, matrix products, local(): jnp.dot(grad_ffn, dense_out.T, preferred_element_type=jnp.float32)  17.4 us
    dot_general x1, matrix products, local(): jnp.dot(ffn_act.T, grad_ffn, preferred_element_type=jnp.float32).astype(bf)  9.77 us

profile of v1, /device:TPU:0, one launch (start us, length us, event | category | flops | bytes accessed | tf_op | source)
XLA Modules:
  0.0 468.0 jit_solution(13168008452246826283)
XLA Ops:
  0.7 1.4 fusion.92
  4.1 1.4 pad_add_fusion.1
  6.2 1.3 broadcast_in_dim.14.gain
  8.3 1.3 convolution_bitcast_fusion.3
  14.7 1.4 fusion.15
  16.3 1.4 fusion.14
  20.2 79.9 %gather.1 = (bf16[8,128,768]{2,1,0:T(8,128)(2,1)}, bf16[8,128,768]{2,1,0:T(8,128)(2,1)}, bf16[2,2,4,2,96,640]{5,4,3,2,1,0:T(8,128)(2,1)}, bf16[4,2,2,2,32,768]{5...) custom-call(bf16[8,128,768]{2,1,0:T(8,128)(2,1)} %bitcast.257, ...), custom_call_target="tpu_custom_call" | custom-call | tf_op jit(solution)/shard_map/gather/pallas_call | solution.py:526
  100.1 2.5 slice.75
  102.6 2.1 multiply_reduce_fusion.1
  104.7 1.3 fusion.94
  106.6 25.3 %attention.1 = (bf16[1024,768]{1,0:T(8,128)(2,1)}, bf16[4,1024,640]{2,1,0:T(8,128)(2,1)}, bf16[4,1024,256]{2,1,0:T(8,128)(2,1)}) custom-call(bf16[1024,768]{1,0:T(8,128)(2,1)} %bitcast.244, f32[1,768]{1,0:T(1,128)} %broadcast_in_dim.14.gain, bf16[4,768,640]{2,1,0:T(8,128)(2,1)} %bitcast.255, bf16[1024,128]{1,0:T(8,128)(2,1)} %select_convert_fusion.mask, ...), custom_call_target="tpu_custom_call" | custom-call | tf_op jit(solution)/shard_map/attention/pallas_call | solution.py:762
  131.9 3.2 slice_bitcast_fusion
  135.1 2.9 copy.44
  138.0 3.6 multiply_reduce_fusion.3
  141.7 36.9 %multiply_convert_fusion = (bf16[1024,3072]{1,0:T(8,128)(2,1)S(1)}, f32[1024,3072]{1,0:T(8,128)}, f32[1024,3072]{1,0:T(8,128)}) fusion(bf16[3072,768]{1,0:T(8,128)(2,1)} %bitcast.284, f32[1024,768]{1,0:T(8,128)S(1)} %get-tuple-element.101, f32[768]{0:T(1024)S(1)} %copy-done.34, f32[1024]{0:T(1024)S(1)} %fusion.81), kind=kOutput, calls=%fused_computation.3 | convolution fusion | flops 5038669824 | bytes 39328768 | tf_op jit(solution)/shard_map/dot_general | solution.py:901
  178.6 5.0 %fusion.93 = f32[1024,768]{1,0:T(8,128)S(1)} fusion(bf16[1024,3072]{1,0:T(8,128)(2,1)S(1)} %get-tuple-element.82, bf16[3072,768]{1,0:T(8,128)(2,1)S(1)} %bitcast.291), kind=kOutput, calls=%fused_computation.170 | convolution fusion | flops 4831838208 | bytes 14155776 | tf_op jit(solution)/shard_map/dot_general | solution.py:903
  183.7 1.6 copy-done.11
  185.4 1.5 fusion.31
  186.9 3.6 fusion.18
  190.6 4.1 add_convert_fusion.1
  194.7 1.1 reshape.314
  196.1 1.1 convolution_bitcast_fusion.1
  198.6 4.0 add_convert_fusion.2
  202.5 17.4 %add_convert_fusion = bf16[1024,3072]{1,0:T(8,128)(2,1)} fusion(f32[1024,3072]{1,0:T(8,128)} %get-tuple-element.83, f32[1024,3072]{1,0:T(8,128)} %get-tuple-element.102, bf16[1024,768]{1,0:T(8,128)(2,1)} %add_convert_fusion.2, bf16[3072,768]{1,0:T(8,128)(2,1)} %bitcast.288), kind=kOutput, calls=%fused_computation.2 | convolution fusion | flops 4875878400 | bytes 37748736 | tf_op jit(solution)/shard_map/dot_general | solution.py:920
  219.9 9.8 %convolution_convert_fusion = bf16[3072,768]{1,0:T(8,128)(2,1)} fusion(bf16[1024,3072]{1,0:T(8,128)(2,1)} %copy-done.37, bf16[1024,768]{1,0:T(8,128)(2,1)} %add_convert_fusion.2), kind=kOutput, calls=%fused_computation.21 | convolution fusion | flops 4834197504 | bytes 12582912 | tf_op jit(solution)/shard_map/dot_general | solution.py:918
  229.7 5.5 %multiply_reduce_fusion = (f32[768]{0:T(1024)S(1)}, f32[1024]{0:T(1024)S(1)}, f32[1024,768]{1,0:T(8,128)S(1)}) fusion(f32[1024,768]{1,0:T(8,128)S(1)} %copy-done.7, f32[1024]{0:T(1024)S(1)} %fusion.81, f32[768]{0:T(1024)S(1)} %copy-done.34, bf16[1024,3072]{1,0:T(8,128)(2,1)S(1)} %copy-done.36, bf16[3072,768]{1,0:T(8,128)(2,1)S(1)} %bitcast.287), kind=kOutput, calls=%fused_computation.35 | convolution fusion | flops 4836554752 | bytes 17315840 | tf_op jit(solution)/shard_map/dot_general | solution.py:923
  235.2 7.6 %convolution_convert_fusion.1 = bf16[3072,768]{1,0:T(8,128)(2,1)} fusion(bf16[1024,3072]{1,0:T(8,128)(2,1)S(1)} %copy-done.36, f32[1024,768]{1,0:T(8,128)S(1)} %copy-done.7, f32[768]{0:T(1024)S(1)} %copy-done.34, f32[1024]{0:T(1024)S(1)} %fusion.81), kind=kOutput, calls=%fused_computation.22 | convolution fusion | flops 4836556800 | bytes 14162944 | tf_op jit(solution)/shard_map/dot_general | solution.py:921
  242.8 2.1 fusion.12
  244.9 2.4 convolution_convert_fusion.3
  247.3 2.8 copy.52
  250.1 2.0 convolution_bitcast_fusion
  252.5 1.1 convolution_bitcast_fusion.2
  255.1 2.6 pad.23
  257.7 3.8 convolution_convert_fusion.2
  261.5 2.7 copy.48
  264.3 1.7 pad.22.grad_context
  266.0 31.0 %attention_back.1 = (bf16[4,1024,640]{2,1,0:T(8,128)(2,1)}, f32[4,3,768]{2,1,0:T(4,128)}) custom-call(bf16[4,1024,640]{2,1,0:T(8,128)(2,1)} %get-tuple-element.34.packed, bf16[4,1024,256]{2,1,0:T(8,128)(2,1)} %pad.22.grad_context, bf16[1024,128]{1,0:T(8,128)(2,1)} %select_convert_fusion.mask, f32[4,3,512]{2,1,0:T(4,128)} %reshape.302.rows), custom_call_target="tpu_custom_call" | custom-call | tf_op jit(solution)/shard_map/attention_back/pallas_call | solution.py:793
  297.1 8.7 %fusion.11 = (f32[1024]{0:T(1024)S(1)}, f32[768]{0:T(1024)S(1)}, f32[1024,768,1]{1,0,2:T(8,128)}) fusion(f32[768]{0:T(1024)S(1)} %copy-done.26, bf16[8,128,768]{2,1,0:T(8,128)(2,1)S(1)} %copy-done.4, f32[1024]{0:T(1024)S(1)} %copy-done.27, bf16[4,1024,640]{2,1,0:T(8,128)(2,1)} %get-tuple-element.40, bf16[4,768,640]{2,1,0:T(8,128)(2,1)S(1)} %bitcast.256), kind=kOutput, calls=%fused_computation.31 | convolution fusion | flops 4032035072 | bytes 13907968 | tf_op jit(solution)/shard_map/mtc,mdc->td/dot_general | solution.py:933
  306.7 4.8 %fusion.8 = bf16[1024,768]{1,0:T(8,128)(2,1)} fusion(f32[1024,768]{1,0:T(8,128)} %copy-done.5, f32[1024,768,1]{1,0,2:T(8,128)} %get-tuple-element.104, f32[1024]{0:T(1024)S(1)} %fusion.80, f32[768]{0:T(1024)S(1)} %copy-done.26, f32[1024]{0:T(1024)S(1)} %copy-done.27, bf16[8,128,768]{2,1,0:T(8,128)(2,1)S(1)} %copy-done.4), kind=kLoop, calls=%fused_computation.28 | loop fusion | flops 6291456 | bytes 9448448 | tf_op jit(solution)/shard_map/convert_element_type | solution.py:936
  312.2 9.2 %convert_bitcast_fusion = bf16[4,768,640]{1,2,0:T(8,128)(2,1)} fusion(bf16[4,1024,640]{2,1,0:T(8,128)(2,1)} %get-tuple-element.40, bf16[1024,768]{1,0:T(8,128)(2,1)} %get-tuple-element.41), kind=kOutput, calls=%fused_computation.25 | convolution fusion | flops 4028497920 | bytes 10747904 | tf_op jit(solution)/shard_map/td,mtc->mdc/dot_general | solution.py:932
  321.4 6.4 %copy.50 = bf16[4,768,640]{2,1,0:T(8,128)(2,1)} copy(bf16[4,768,640]{1,2,0:T(8,128)(2,1)} %convert_bitcast_fusion) | data formatting | bytes 7864320 | tf_op jit(solution)/shard_map/convert_element_type | solution.py:932
  327.8 119.3 %scatter.1 = (f32[96,640]{1,0:T(8,128)}, f32[32,768]{1,0:T(8,128)}, f32[96,768]{1,0:T(8,128)}, f32[96,768]{1,0:T(8,128)}, f32[32,128]{1,0:T(8,128)}, /*index=5*/...) custom-call(bf16[2,2,4,2,96,640]{5,4,3,2,1,0:T(8,128)(2,1)} %bitcast.243, bf16[4,2,2,2,32,768]{5,4,3,2,1,0:T(8,128)(2,1)} %bitcast.249, ...), custom_call_target="tpu_custom_call" | custom-call | tf_op jit(solution)/shard_map/scatter/pallas_call | solution.py:567
  452.2 1.3 slice_bitcast_fusion.1
  454.3 1.5 slice.61
  460.5 2.2 slice.67
  462.7 1.3 slice.76
  464.0 1.1 copy.100
  465.2 1.1 copy.101
  (152 shorter events, 29.2 us)
Async XLA Ops:
  0.6 7.7 %copy-start = (f32[32,12]{0,1:T(8,128)S(1)}, f32[32,12]{0,1:T(8,128)}, u32[]{:S(2)}) copy-start(f32[32,12]{0,1:T(8,128)} %param.26) | copy-start | bytes 4612
  0.7 18.0 %copy-start.18 = (f32[96,768]{1,0:T(8,128)S(1)}, f32[96,768]{1,0:T(8,128)}, u32[]{:S(2)}) copy-start(f32[96,768]{1,0:T(8,128)} %param.23) | copy-start | bytes 884740
  0.7 17.2 %copy-start.17 = (f32[768,96]{0,1:T(8,128)S(1)}, f32[768,96]{0,1:T(8,128)}, u32[]{:S(2)}) copy-start(f32[768,96]{0,1:T(8,128)} %param.22) | copy-start | bytes 884740
  17.9 165.8 %copy-start.22 = (bf16[768,48]{0,1:T(8,128)(2,1)}, bf16[768,48]{0,1:T(8,128)(2,1)S(1)}, u32[]{:S(2)}) copy-start(bf16[768,48]{0,1:T(8,128)(2,1)S(1)} %convert_element_type.147) | copy-start | bytes 221188
  100.1 2.5 copy-start.2
  104.7 27.2 %copy-start.24 = (f32[8,128]{1,0:T(8,128)}, f32[8,128]{1,0:T(8,128)S(1)}, u32[]{:S(2)}) copy-start(f32[8,128]{1,0:T(8,128)S(1)} %get-tuple-element.107) | copy-start | bytes 12292
  131.9 6.1 %copy-start.3 = (bf16[8,128,768]{2,1,0:T(8,128)(2,1)S(1)}, bf16[8,128,768]{2,1,0:T(8,128)(2,1)}, u32[]{:S(2)}) copy-start(bf16[8,128,768]{2,1,0:T(8,128)(2,1)} %get-tuple-element.32) | copy-start | bytes 4718596
  138.0 3.6 copy-start.12
  138.0 3.6 copy-start.34
  138.0 40.6 %slice-start.2 = ((s8[4718592]{0:T(1024)(128)(4,1)}), s8[4194304]{0:T(1024)(128)(4,1)S(1)}, s32[]{:S(2)}) async-start(s8[4718592]{0:T(1024)(128)(4,1)} %bitcast.289), calls=%async_computation.2 | async-start | bytes 8388608
  141.6 37.0 %copy-start.6 = (f32[1024,768]{1,0:T(8,128)}, f32[1024,768]{1,0:T(8,128)S(1)}, u32[]{:S(2)}) copy-start(f32[1024,768]{1,0:T(8,128)S(1)} %get-tuple-element.101) | copy-start | bytes 9437188
  141.6 37.0 %copy-start.28 = (f32[1024]{0:T(1024)}, f32[1024]{0:T(1024)S(1)}, u32[]{:S(2)}) copy-start(f32[1024]{0:T(1024)S(1)} %get-tuple-element.100) | copy-start | bytes 12292
  141.6 37.0 %slice-start.3 = ((s8[4718592]{0:T(1024)(128)(4,1)}), s8[524288]{0:T(1024)(128)(4,1)S(1)}, s32[]{:S(2)}) async-start(s8[4718592]{0:T(1024)(128)(4,1)} %bitcast.289), calls=%async_computation.3 | async-start | bytes 1048576
  178.6 5.1 %copy-start.37 = (bf16[1024,3072]{1,0:T(8,128)(2,1)}, bf16[1024,3072]{1,0:T(8,128)(2,1)S(1)}, u32[]{:S(2)}) copy-start(bf16[1024,3072]{1,0:T(8,128)(2,1)S(1)} %get-tuple-element.82) | copy-start | bytes 18874372
  183.7 1.6 copy-start.11
  186.9 3.7 copy-start.7
  186.9 3.7 copy-start.21
  190.6 5.2 %copy-start.30 = (f32[4,12]{1,0:T(4,128)S(1)}, f32[4,12]{1,0:T(4,128)}, u32[]{:S(2)}) copy-start(f32[4,12]{1,0:T(4,128)} %param.29) | copy-start | bytes 580
  190.6 5.5 %copy-start.33 = (f32[4,192]{1,0:T(4,128)S(1)}, f32[4,192]{1,0:T(4,128)}, u32[]{:S(2)}) copy-start(f32[4,192]{1,0:T(4,128)} %param.28) | copy-start | bytes 9220
  190.6 6.6 %copy-start.32 = (f32[4,4,4]{2,1,0:T(4,128)S(1)}, f32[4,4,4]{2,1,0:T(4,128)}, u32[]{:S(2)}) copy-start(f32[4,4,4]{2,1,0:T(4,128)} %param.27) | copy-start | bytes 772
  198.6 31.1 %slice-start = ((s8[4718592]{0:T(1024)(128)(4,1)}), s8[4194304]{0:T(1024)(128)(4,1)S(1)}, s32[]{:S(2)}) async-start(s8[4718592]{0:T(1024)(128)(4,1)} %bitcast.285), calls=%async_computation | async-start | bytes 8388608
  202.5 27.2 %slice-start.1 = ((s8[4718592]{0:T(1024)(128)(4,1)}), s8[524288]{0:T(1024)(128)(4,1)S(1)}, s32[]{:S(2)}) async-start(s8[4718592]{0:T(1024)(128)(4,1)} %bitcast.285), calls=%async_computation.1 | async-start | bytes 1048576
  219.9 9.8 %copy-start.36 = (bf16[1024,3072]{1,0:T(8,128)(2,1)S(1)}, bf16[1024,3072]{1,0:T(8,128)(2,1)}, u32[]{:S(2)}) copy-start(bf16[1024,3072]{1,0:T(8,128)(2,1)} %add_convert_fusion) | copy-start | bytes 18874372
  235.2 7.6 %copy-start.29 = (f32[1024]{0:T(1024)S(1)}, f32[1024]{0:T(1024)}, u32[]{:S(2)}) copy-start(f32[1024]{0:T(1024)} %copy-done.28) | copy-start | bytes 12292
  235.2 7.6 %copy-start.8 = (f32[1024,768]{1,0:T(8,128)S(1)}, f32[1024,768]{1,0:T(8,128)}, u32[]{:S(2)}) copy-start(f32[1024,768]{1,0:T(8,128)} %copy-done.6) | copy-start | bytes 9437188
  235.2 7.6 %copy-start.9 = (bf16[8,128,768]{2,1,0:T(8,128)(2,1)S(1)}, bf16[8,128,768]{2,1,0:T(8,128)(2,1)}, u32[]{:S(2)}) copy-start(bf16[8,128,768]{2,1,0:T(8,128)(2,1)} %get-tuple-element.35) | copy-start | bytes 4718596
  242.8 2.1 copy-start.13
  244.9 12.8 %copy-start.5 = (f32[1024,768]{1,0:T(8,128)}, f32[1024,768]{1,0:T(8,128)S(1)}, u32[]{:S(2)}) copy-start(f32[1024,768]{1,0:T(8,128)S(1)} %get-tuple-element.85) | copy-start | bytes 9437188
  247.3 4.8 %copy-start.31 = (f32[4,12]{1,0:T(4,128)S(1)}, f32[4,12]{1,0:T(4,128)}, u32[]{:S(2)}) copy-start(f32[4,12]{1,0:T(4,128)} %param.30) | copy-start | bytes 580
  247.3 5.1 %copy-start.35 = (f32[4,192]{1,0:T(4,128)S(1)}, f32[4,192]{1,0:T(4,128)}, u32[]{:S(2)}) copy-start(f32[4,192]{1,0:T(4,128)} %param.31) | copy-start | bytes 9220
  266.0 31.1 %copy-start.4 = (bf16[8,128,768]{2,1,0:T(8,128)(2,1)S(1)}, bf16[8,128,768]{2,1,0:T(8,128)(2,1)}, u32[]{:S(2)}) copy-start(bf16[8,128,768]{2,1,0:T(8,128)(2,1)} %get-tuple-element.32) | copy-start | bytes 4718596
  266.0 31.1 %copy-start.10 = (bf16[2,2,4,2,96,640]{5,4,3,2,1,0:T(8,128)(2,1)S(1)}, bf16[2,2,4,2,96,640]{5,4,3,2,1,0:T(8,128)(2,1)}, u32[]{:S(2)}) copy-start(bf16[2,2,4,2,96,640]{5,4,3,2,1,0:T(8,128)(2,1)} %get-tuple-element.33) | copy-start | bytes 11796484
  266.0 31.1 %copy-start.26 = (f32[768]{0:T(1024)S(1)}, f32[768]{0:T(1024)}, u32[]{:S(2)}) copy-start(f32[768]{0:T(1024)} %param.24) | copy-start | bytes 9220
  266.0 31.1 %copy-start.27 = (f32[1024]{0:T(1024)S(1)}, f32[1024]{0:T(1024)}, u32[]{:S(2)}) copy-start(f32[1024]{0:T(1024)} %bitcast_rsqrt_fusion) | copy-start | bytes 12292
  297.1 8.7 %copy-start.23 = (f32[4,3,768]{2,1,0:T(4,128)S(1)}, f32[4,3,768]{2,1,0:T(4,128)}, u32[]{:S(2)}) copy-start(f32[4,3,768]{2,1,0:T(4,128)} %get-tuple-element.42) | copy-start | bytes 110596
  297.1 8.7 %copy-start.16 = (f32[768,32]{1,0:T(8,128)S(1)}, f32[768,32]{1,0:T(8,128)}, u32[]{:S(2)}) copy-start(f32[768,32]{1,0:T(8,128)} %constant.43.clone) | copy-start | bytes 294916
  297.1 9.6 %copy-start.25 = (f32[8,128]{1,0:T(8,128)S(1)}, f32[8,128]{1,0:T(8,128)}, u32[]{:S(2)}) copy-start(f32[8,128]{1,0:T(8,128)} %copy-done.24) | copy-start | bytes 12292
  447.1 16.9 %copy-start.15 = (bf16[8,128,768]{2,1,0:T(8,128)(2,1)S(1)}, bf16[8,128,768]{2,1,0:T(8,128)(2,1)}, u32[]{:S(2)}) copy-start(bf16[8,128,768]{2,1,0:T(8,128)(2,1)} %get-tuple-element.43) | copy-start | bytes 4718596
  456.7 8.4 %copy-start.14 = (bf16[8,128,768]{2,1,0:T(8,128)(2,1)S(1)}, bf16[8,128,768]{2,1,0:T(8,128)(2,1)}, u32[]{:S(2)}) copy-start(bf16[8,128,768]{2,1,0:T(8,128)(2,1)} %get-tuple-element.44) | copy-start | bytes 4718596
  462.7 5.0 %copy-start.1 = (f32[32,12]{0,1:T(8,128)S(1)}, f32[32,12]{0,1:T(8,128)}, u32[]{:S(2)}) copy-start(f32[32,12]{0,1:T(8,128)} %param.26) | copy-start | bytes 4612
  464.0 2.3 copy-start.20
  464.0 3.0 copy-start.19

commit v2 on v1

--- a/solution.py
+++ b/solution.py
@@ -1,4 +1,5 @@
 import functools
+import itertools
 
 import jax
 import jax.experimental.pallas as pl
@@ -274,8 +275,9 @@
 
 
 class Scatter:
-    def __init__(self, p, by_head, part, total, half, quarter, arrive, last, send, recv):
+    def __init__(self, p, by_head, part, total, half, quarter, arrive, last, send, recv, mine=None, mine_sem=None):
         self.p, self.by_head, self.part, self.total = p, by_head, part, total
+        self.mine, self.mine_sem = mine, mine_sem
         self.half, self.quarter, self.arrive, self.last = half, quarter, arrive, last
         self.send, self.recv = send, recv
         self.rows = part.shape[-2]
@@ -333,9 +335,18 @@
             self.quarter.at[p.z, 1 - p.a], self.last, self.send.at[3 * n], self.recv.at[3 * n + 1], p.a_nbr
         )
 
+    def _keep(self, core, z):
+        return pltpu.make_async_copy(self._region(core, z), self.mine.at[z], self.mine_sem.at[z])
+
     def start(self, k):
         z = self.order(k)
-        self.p.by_core(lambda core: self._sib(core, z).start())
+
+        def one(core):
+            self._sib(core, z).start()
+            if self.mine is not None:
+                self._keep(core, z).start()
+
+        self.p.by_core(one)
 
     def to_half(self, k):
         z = self.order(k)
@@ -343,6 +354,9 @@
         def one(core):
             self._sib(core, z).wait_recv()
             region = self._region(core, z)
+            if self.mine is not None:
+                self._keep(core, z).wait()
+                region = self.mine.at[z]
             for i in (0, 1):
                 for j in (0, 1):
                     add_rows(self.half.at[z, i, j], region.at[i, j], self.rows)
@@ -364,29 +378,33 @@
         for i in (0, 1):
             add_rows(self.quarter.at[z, i], self.arrive.at[slot, i], self.rows)
 
-    def pass_on(self, k):
+    def _send_left(self, z):
+        p, n = self.p, self.p.depth
+        pl.when(z == p.z - 1)(lambda: self._left(z, n).start())
+        pl.when(z < p.z - 1)(lambda: self._left(z, z).start())
+
+    def origin(self, k):
         p, n = self.p, self.p.depth
         z = self.order(k)
+        pl.when(jnp.logical_and(p.z == 0, z > p.z))(lambda: self._right(z).start())
+        pl.when(jnp.logical_and(p.z == n - 1, z < p.z))(lambda: self._send_left(z))
+
+    def forward(self, k):
+        p, n = self.p, self.p.depth
+        z = self.order(k)
 
         def rightward():
-            def take():
-                self._right(z).wait_recv()
-                self._take(z, z)
-
-            pl.when(p.z > 0)(take)
+            self._right(z).wait_recv()
+            self._take(z, z)
             self._right(z).start()
 
         def leftward():
-            def take():
-                self._left(z, z).wait_recv()
-                self._take(z, z)
-
-            pl.when(p.z < n - 1)(take)
-            pl.when(z == p.z - 1)(lambda: self._left(z, n).start())
-            pl.when(z < p.z - 1)(lambda: self._left(z, z).start())
-
-        pl.when(z > p.z)(rightward)
-        pl.when(z < p.z)(leftward)
+            self._left(z, z).wait_recv()
+            self._take(z, z)
+            self._send_left(z)
+
+        pl.when(jnp.logical_and(p.z > 0, z > p.z))(rightward)
+        pl.when(jnp.logical_and(p.z < n - 1, z < p.z))(leftward)
 
     def collect(self):
         p, n = self.p, self.p.depth
@@ -428,8 +446,8 @@
         todo = [lambda: [self.start(k) for k in range(n)]]
         todo += [functools.partial(self.to_half, k) for k in range(n)]
         for k in range(n):
-            todo.append(functools.partial(lambda k: (self.to_quarter(k), self.pass_on(k)), k))
-        return todo + [self.collect, self.finish]
+            todo.append(functools.partial(lambda k: (self.to_quarter(k), self.origin(k), self.forward(k)), k))
+        return todo
 
 
 class Sum:
@@ -545,13 +563,21 @@
     small_o[...] = small[...]
     sums = Sum(p, bits, small_o, *scr[30:33])
     p.barrier(bits)
-    for r in rows:
-        r.start()
-    in_waves([sums.steps()] + [g.steps() for g in arrays], min(depth, 4))
+    rows[0].start()
+    in_waves([g.steps() for g in arrays], min(depth, 4))
+    rows[1].start()
+    close(arrays, sums)
     for r in rows:
         r.finish()
     for g in arrays + rows + [sums]:
         g.drain()
+
+
+def close(arrays, sums):
+    closing = [g.collect for g in arrays] + [g.finish for g in arrays]
+    for step in itertools.chain(*itertools.zip_longest(sums.steps(), closing)):
+        if step is not None:
+            step()
 
 
 def scatter_all(depth, bits, parts, small, out_s, gtok_s):
@@ -663,13 +689,47 @@
     return blocks[0] if len(blocks) == 1 else jnp.concatenate(blocks, axis=axis)
 
 
-def attend_group(packed, mask_ref, rows, context):
+def value_lanes(group):
+    stride = group * CTX_PAD // (3 * DH)
+    lane = np.arange(CTX_PAD)
+    column = lane // stride * group + lane % stride
+    return np.where(lane % stride < group, column // DH, -1), column
+
+
+def head_runs(group):
+    heads, _ = value_lanes(group)
+    runs = []
+    for lane in range(CTX_PAD):
+        head = int(heads[lane])
+        head = runs[-1][2] if head < 0 else head
+        if runs and runs[-1][2] == head:
+            runs[-1][1] = lane + 1
+        else:
+            runs.append([lane, lane + 1, head])
+    return runs
+
+
+def head_lanes(shape, group, head):
+    lane = lax.broadcasted_iota(jnp.int32, shape, len(shape) - 1)
+    inside = None
+    for lo, hi, h in head_runs(group):
+        if h == head:
+            run = jnp.logical_and(lane >= lo, lane < hi)
+            inside = run if inside is None else jnp.logical_or(inside, run)
+    return inside
+
+
+def no_tick(j):
+    pass
+
+
+def attend_group(packed, mask_ref, rows, context, group, tick=no_tick):
     tiles = [bias_tiles(rows[h : h + 1, :]) for h in range(3)]
-    for offset, length in SPANS:
+    for number, (offset, length) in enumerate(SPANS):
         span = pl.ds(offset, length)
         mask = mask_ref[span, :]
         keys = [key_side(packed[span, h * TILE : (h + 1) * TILE], mask)[0] for h in range(3)]
-        values = [packed[span, (3 + t) * TILE : (4 + t) * TILE].T for t in range(2)]
+        values = packed[span, 3 * TILE :].T
         width = min(length, 256)
         for q0 in range(0, length, width):
             here = pl.ds(offset + q0, width)
@@ -678,23 +738,23 @@
                 queries = query_side(packed[here, h * TILE : (h + 1) * TILE])
                 probs = probabilities(keys[h], queries, tiles[h], q0 // TILE, length, width)
                 probs = join([block.astype(jnp.bfloat16) for block in probs])
-                full = dot(values[h // 2], probs)
-                outs.append(full[(h % 2) * DH : (h % 2 + 1) * DH])
-            context[here, :TILE] = jnp.concatenate(outs[:2], axis=0).T.astype(jnp.bfloat16)
-            last = jnp.concatenate([outs[2], jnp.zeros_like(outs[2])], axis=0)
-            context[here, TILE:] = last.T.astype(jnp.bfloat16)
-
-
-def attend_group_back(packed, mask_ref, rows, grad_context, grad_packed, sums):
+                outs.append(dot(values, probs))
+            whole = jnp.concatenate([outs[h][lo:hi] for lo, hi, h in head_runs(group)], axis=0)
+            context[here, :] = whole.T.astype(jnp.bfloat16)
+        tick(number)
+
+
+def attend_group_back(packed, mask_ref, rows, grad_context, grad_packed, sums, group, tick=no_tick):
     far_shape = (TILE, TILE)
     tiles = [bias_tiles(rows[h : h + 1, :]) for h in range(3)]
     near = [[None] * 3 for _ in range(3)]
     far = [[jnp.zeros(far_shape, jnp.float32)] * 2 for _ in range(3)]
-    for offset, length in SPANS:
+    for number, (offset, length) in enumerate(SPANS):
         span = pl.ds(offset, length)
         mask = mask_ref[span, :]
         width = min(length, 256)
-        grad_values = [None, None]
+        values = packed[span, 3 * TILE :]
+        value_sums = {}
         for h in range(3):
             at = pl.ds(h * TILE, TILE)
             qk = packed[span, at]
@@ -702,15 +762,13 @@
             keys, swapped = key_side(qk, mask)
             upper_queries = jnp.where(low, jnp.zeros_like(qk), swapped)
             plain_keys = jnp.where(low, swapped, jnp.zeros_like(qk)).T
-            values = packed[span, (3 + h // 2) * TILE : (4 + h // 2) * TILE]
             grad_keys = None
             grad_queries = []
             for q0 in range(0, length, width):
                 here = pl.ds(offset + q0, width)
                 probs = probabilities(keys, query_side(packed[here, at]), tiles[h], q0 // TILE, length, width)
-                g_tile = grad_context[here, (h // 2) * TILE : (h // 2 + 1) * TILE]
-                own = lanes_below(g_tile.shape) == (h % 2 == 0)
-                g_tile = jnp.where(own, g_tile, jnp.zeros_like(g_tile))
+                g_tile = grad_context[here, :]
+                g_tile = jnp.where(head_lanes(g_tile.shape, group, h), g_tile, jnp.zeros_like(g_tile))
                 g_probs = dot(values, g_tile, NT)
                 g_blocks = [g_probs[kb * TILE : (kb + 1) * TILE] for kb in range(length // TILE)]
                 total = probs[0] * g_blocks[0]
@@ -732,20 +790,23 @@
                             far[h][side] = far[h][side] + piece
                 g_scores = join(g_scores)
                 g_v = dot(low_probs, g_tile)
-                grad_values[h // 2] = g_v if grad_values[h // 2] is None else grad_values[h // 2] + g_v
+                if q0 not in value_sums:
+                    value_sums[q0] = g_v
+                else:
+                    value_sums[q0] = value_sums[q0] + g_v
                 g_k = dot(g_scores, upper_queries[q0 : q0 + width])
                 grad_keys = g_k if grad_keys is None else grad_keys + g_k
                 grad_queries.append(dot(plain_keys, g_scores).T)
             grad_packed[span, at] = (join(grad_queries) + grad_keys).astype(jnp.bfloat16)
-        for t in range(2):
-            grad_packed[span, (3 + t) * TILE : (4 + t) * TILE] = grad_values[t].astype(jnp.bfloat16)
+            tick(3 * number + h)
+        grad_packed[span, 3 * TILE :] = functools.reduce(jnp.add, value_sums.values()).astype(jnp.bfloat16)
     for h in range(3):
         sums[h : h + 1, :512] = diagonal_sums(near[h])
         for side in range(2):
             sums[h : h + 1, 512 + side * TILE : 640 + side * TILE] = jnp.sum(far[h][side], axis=0, keepdims=True)
 
 
-def attention_kernel(x_ref, gain, w_ref, mask, rows, normed_out, packed, context):
+def attention_kernel(group, x_ref, gain, w_ref, mask, rows, normed_out, packed, context):
     @pl.when(pl.program_id(0) == 0)
     def _():
         x = x_ref[...].astype(jnp.float32)
@@ -753,14 +814,14 @@
         normed_out[...] = (x * scale * gain[...]).astype(jnp.bfloat16)
 
     packed[0] = dot(normed_out[...], w_ref[0]).astype(jnp.bfloat16)
-    attend_group(packed.at[0], mask, rows[0], context.at[0])
-
-
-def attention(x, gain, w, mask, rows):
+    attend_group(packed.at[0], mask, rows[0], context.at[0], group)
+
+
+def attention(x, gain, w, mask, rows, group):
     n = x.shape[0]
     bf = jnp.bfloat16
     return pl.pallas_call(
-        attention_kernel,
+        functools.partial(attention_kernel, group),
         grid=(4,),
         out_shape=[
             jax.ShapeDtypeStruct((n, D), bf),
@@ -784,14 +845,14 @@
     )(x, gain, w, mask, rows)
 
 
-def attention_back_kernel(packed, grad_context, mask, rows, grad_packed, sums):
-    attend_group_back(packed.at[0], mask, rows[0], grad_context.at[0], grad_packed.at[0], sums.at[0])
-
-
-def attention_back(packed, grad_context, mask, rows):
+def attention_back_kernel(group, packed, grad_context, mask, rows, grad_packed, sums):
+    attend_group_back(packed.at[0], mask, rows[0], grad_context.at[0], grad_packed.at[0], sums.at[0], group)
+
+
+def attention_back(packed, grad_context, mask, rows, group):
     n = packed.shape[1]
     return pl.pallas_call(
-        attention_back_kernel,
+        functools.partial(attention_back_kernel, group),
         grid=(4,),
         out_shape=[
             jax.ShapeDtypeStruct((4, n, QKV_PAD), jnp.bfloat16),
@@ -812,21 +873,498 @@
     )(packed, grad_context, mask, rows)
 
 
-def head_columns(w):
-    qk = w[:, :, : 2 * DH].reshape(w.shape[0], 6 * DH)
-    v = w[:, :, 2 * DH :].reshape(w.shape[0], 3 * DH)
-    return jnp.pad(jnp.concatenate([qk, v], axis=1), ((0, 0), (0, QKV_PAD - 9 * DH)))
-
-
-def from_head_columns(g):
-    qk = g[:, : 6 * DH].reshape(g.shape[0], 3, 2 * DH)
-    v = g[:, 6 * DH : 9 * DH].reshape(g.shape[0], 3, DH)
+def head_columns(w, group):
+    n = w.shape[0]
+    qk = w[:, :, : 2 * DH].reshape(n, 6 * DH)
+    v = w[:, :, 2 * DH :].reshape(n, 3 * DH // group, group)
+    v = jnp.pad(v, ((0, 0), (0, 0), (0, group // 3))).reshape(n, CTX_PAD)
+    return jnp.concatenate([qk, v], axis=1)
+
+
+def from_head_columns(g, group):
+    n = g.shape[0]
+    qk = g[:, : 6 * DH].reshape(n, 3, 2 * DH)
+    v = g[:, 6 * DH :].reshape(n, 3 * DH // group, group * 4 // 3)[:, :, :group].reshape(n, 3, DH)
     return jnp.concatenate([qk, v], axis=2)
 
 
 def key_mask(live):
     lane = jnp.arange(TILE)[None, :]
     return jnp.where((lane == DH) & ~live[:, None], MASK_LOW, 0.0).astype(jnp.bfloat16)
+
+
+TN = (((0,), (0,)), ((), ()))
+FCH = 512
+RCH = 256
+ADAPT_PAD = 128
+
+
+def gelu_both(v):
+    phi = 0.5 + 0.5 * lax.erf(v * np.float32(np.sqrt(0.5)))
+    return v * phi, phi + v * (jnp.exp(-0.5 * v * v) * np.float32(1.0 / np.sqrt(2.0 * np.pi)))
+
+
+def rows_of(i, size=RCH):
+    return pl.ds(pl.multiple_of(i * size, size), size)
+
+
+def each_of(count, body):
+    lax.fori_loop(0, count, lambda i, carry: (body(i), carry)[1], 0)
+
+
+def middle_kernel(
+    x_hbm, ctx_hbm, wo_hbm, wi_hbm, wu_hbm, cot_hbm, gain, down, up, live,
+    res_hbm, gmid_hbm, gctx_hbm, go_hbm, gi_hbm, gu_hbm, g_gain, g_down, g_up,
+    x, ctx, wo, wi, wu, cot, mid, n2, act, dg, acc, gffn, glow, stage, sems,
+):
+    n = x.shape[0]
+    ff = wi.shape[0]
+    bf = jnp.bfloat16
+    loads = [
+        pltpu.make_async_copy(src, dst, sems.at[i])
+        for i, (src, dst) in enumerate(
+            ((x_hbm, x), (ctx_hbm, ctx), (wo_hbm, wo), (wi_hbm, wi), (wu_hbm, wu), (cot_hbm, cot))
+        )
+    ]
+    for load in loads:
+        load.start()
+    for load in loads[:3]:
+        load.wait()
+
+    def first(i):
+        r = rows_of(i)
+        total = x[r, :].astype(jnp.float32)
+        for m in range(4):
+            total = total + dot(ctx[m, r, :], wo[m])
+        mid[r, :] = total
+        scale = lax.rsqrt(jnp.mean(total * total, axis=-1, keepdims=True) + NORM_EPS)
+        n2[r, :] = (total * scale * gain[...]).astype(bf)
+
+    each_of(n // RCH, first)
+    loads[3].wait()
+    loads[4].wait()
+    acc[...] = jnp.zeros_like(acc)
+
+    def forward(j):
+        f = rows_of(j, FCH)
+        for half in range(2):
+            r = pl.ds(half * (n // 2), n // 2)
+            value, slope = gelu_both(dot(n2[r, :], wi[f, :], NT))
+            value = value.astype(bf)
+            act[r, f] = value
+            dg[r, f] = slope.astype(bf)
+            acc[r, :] += dot(value, wu[f, :])
+
+    each_of(ff // FCH, forward)
+    loads[5].wait()
+    g_down[...] = jnp.zeros_like(g_down)
+    g_up[...] = jnp.zeros_like(g_up)
+    g_gain[...] = jnp.zeros_like(g_gain)
+
+    def adapter(i):
+        r = rows_of(i)
+        ffn = acc[r, :]
+        low = ffn.astype(bf)
+        value, slope = gelu_both(dot(low, down[...]))
+        value = value.astype(bf)
+        x[r, :] = (mid[r, :] + ffn + dot(value, up[...], NT)).astype(bf)
+        g_out = cot[r, :].astype(jnp.float32) * live[r, :]
+        g_low = g_out.astype(bf)
+        cot[r, :] = g_low
+        g_sq = (dot(g_low, up[...]) * slope).astype(bf)
+        g_up[...] += dot(g_low, value, TN)
+        g_down[...] += dot(low, g_sq, TN)
+        gffn[r, :] = (g_out + dot(g_sq, down[...], NT)).astype(bf)
+
+    each_of(n // RCH, adapter)
+    out_copy = pltpu.make_async_copy(x, res_hbm, sems.at[0])
+    out_copy.start()
+    acc[...] = jnp.zeros_like(acc)
+
+    def stores(j, slot):
+        f = rows_of(j, FCH)
+        return [
+            pltpu.make_async_copy(stage.at[k, slot], dst.at[f], sems.at[6 + 2 * k + slot])
+            for k, dst in enumerate((gu_hbm, gi_hbm))
+        ]
+
+    def backward(j):
+        f = rows_of(j, FCH)
+        slot = lax.rem(j, 2)
+
+        def settle():
+            for store in stores(j - 2, slot):
+                store.wait()
+
+        pl.when(j >= 2)(settle)
+        for half in range(2):
+            r = pl.ds(half * (n // 2), n // 2)
+            g = (dot(gffn[r, :], wu[f, :], NT) * dg[r, f].astype(jnp.float32)).astype(bf)
+            dg[r, f] = g
+            acc[r, :] += dot(g, wi[f, :])
+        stage[0, slot] = dot(act[:, f], gffn[...], TN).astype(bf)
+        stage[1, slot] = dot(dg[:, f], n2[...], TN).astype(bf)
+        for store in stores(j, slot):
+            store.start()
+
+    count = ff // FCH
+    each_of(count, backward)
+
+    def last(i):
+        r = rows_of(i)
+        total = mid[r, :]
+        g_n2 = acc[r, :]
+        scale = lax.rsqrt(jnp.mean(total * total, axis=-1, keepdims=True) + NORM_EPS)
+        g_gain[...] += jnp.sum(total * scale * g_n2, axis=0, keepdims=True)
+        scaled = gain[...] * g_n2
+        centre = jnp.mean(total * scaled, axis=-1, keepdims=True)
+        g_mid = cot[r, :].astype(jnp.float32) + scale * scaled - total * (scale * scale * scale * centre)
+        mid[r, :] = g_mid
+        low = g_mid.astype(bf)
+        glow[r, :] = low
+
+    each_of(n // RCH, last)
+    mid_copy = pltpu.make_async_copy(mid, gmid_hbm, sems.at[1])
+    mid_copy.start()
+    for j in range(max(count - 2, 0), count):
+        for store in stores(j, j % 2):
+            store.wait()
+    for m in range(4):
+        stage[0, m // 2, (m % 2) * 256 : (m % 2 + 1) * 256] = dot(ctx[m], glow[...], TN).astype(bf)
+    go_copies = [pltpu.make_async_copy(stage.at[0, k], go_hbm.at[pl.ds(512 * k, 512)], sems.at[6 + k]) for k in range(2)]
+    for copy in go_copies:
+        copy.start()
+    for m in range(4):
+        ctx[m] = dot(glow[...], wo[m], NT).astype(bf)
+    ctx_copy = pltpu.make_async_copy(ctx, gctx_hbm, sems.at[2])
+    ctx_copy.start()
+    for copy in (out_copy, mid_copy, *go_copies, ctx_copy):
+        copy.wait()
+
+
+def middle(x, ctx, wo, wi, wu, cot, gain, down, up, live):
+    n, ff = x.shape[0], wi.shape[0]
+    bf, f32 = jnp.bfloat16, jnp.float32
+    hbm = pl.BlockSpec(memory_space=pl.ANY)
+    vmem = pl.BlockSpec(memory_space=pltpu.VMEM)
+    shape = jax.ShapeDtypeStruct
+    return pl.pallas_call(
+        middle_kernel,
+        out_shape=[
+            shape((n, D), bf),
+            shape((n, D), f32),
+            shape((4, n, CTX_PAD), bf),
+            shape((4 * CTX_PAD, D), bf),
+            shape((ff, D), bf),
+            shape((ff, D), bf),
+            shape((1, D), f32),
+            shape((D, ADAPT_PAD), f32),
+            shape((D, ADAPT_PAD), f32),
+        ],
+        in_specs=[hbm] * 6 + [vmem] * 4,
+        out_specs=[hbm] * 6 + [vmem] * 3,
+        scratch_shapes=[
+            pltpu.VMEM((n, D), bf),
+            pltpu.VMEM((4, n, CTX_PAD), bf),
+            pltpu.VMEM((4, CTX_PAD, D), bf),
+            pltpu.VMEM((ff, D), bf),
+            pltpu.VMEM((ff, D), bf),
+            pltpu.VMEM((n, D), bf),
+            pltpu.VMEM((n, D), f32),
+            pltpu.VMEM((n, D), bf),
+            pltpu.VMEM((n, ff), bf),
+            pltpu.VMEM((n, ff), bf),
+            pltpu.VMEM((n, D), f32),
+            pltpu.VMEM((n, D), bf),
+            pltpu.VMEM((n, D), bf),
+            pltpu.VMEM((2, 2, FCH, D), bf),
+            pltpu.SemaphoreType.DMA((10,)),
+        ],
+        compiler_params=pltpu.CompilerParams(vmem_limit_bytes=63 * 2**20),
+        name="middle",
+    )(x, ctx, wo, wi, wu, cot, gain, down, up, live)
+
+
+class Slots:
+    def __init__(self, places, timed):
+        self.at = {}
+        times = sorted(places.items(), key=lambda item: item[1])
+        for when, step in sorted(timed, key=lambda item: item[0]):
+            place = next((name for name, t in times if t >= when), None)
+            self.at.setdefault(place, []).append(step)
+
+    def run(self, place):
+        for step in self.at.pop(place, ()):
+            step()
+
+    def tick(self, i, j):
+        for place in sorted(name for name in self.at if name is not None and name[1] == j):
+            pl.when(i == place[0])(functools.partial(self.run, place))
+
+
+def front_kernel(
+    depth, group, tok, cot, wq, wo, wi, wu, gain, mask, rows,
+    tok_s, cot_s, gq_hbm, go, gi, gu, normed_hbm, packed_hbm, ctx_hbm,
+    x, gq, nrm, packed, ctx, local, *sems,
+):
+    p = Place(depth)
+    n = depth
+    bf = jnp.bfloat16
+    arrays = [
+        Gather(p, by_head, shard, buf, *sems[3 * i : 3 * i + 3])
+        for i, (by_head, shard, buf) in enumerate(
+            ((True, wq, gq), (False, wo, go), (False, wi, gi), (False, wu, gu))
+        )
+    ]
+    q, rest = arrays[0], arrays[1:]
+    first, second = Exchange(p, tok, x, *sems[12:15]), Exchange(p, cot, cot_s, *sems[15:18])
+    p.barrier(0)
+    for g in arrays:
+        g.start()
+    first.start()
+    for g in arrays:
+        g.along(0)
+    for k in range(1, n):
+        for g in arrays:
+            g.along(k)
+        for g in arrays if k < n - 1 else [q]:
+            g.across(k - 1)
+        if k == 1:
+            first.finish()
+            keep_x = pltpu.make_async_copy(x, tok_s, local.at[0])
+            keep_x.start()
+            second.start()
+
+            def norm(i):
+                v = x[i].astype(jnp.float32)
+                scale = lax.rsqrt(jnp.mean(v * v, axis=-1, keepdims=True) + NORM_EPS)
+                nrm[rows_of(i, SEG), :] = (v * scale * gain[...]).astype(bf)
+
+            each_of(x.shape[0], norm)
+            keep_n = pltpu.make_async_copy(nrm, normed_hbm, local.at[1])
+            keep_n.start()
+    q.across(n - 1)
+    q.finish()
+    keep_q = pltpu.make_async_copy(gq, gq_hbm, local.at[2])
+    keep_q.start()
+    places = {(m, j): 5.0 * m + t for m in range(4) for j, t in enumerate((2.5, 4.0, 4.5, 5.0))}
+    timed = []
+    for i, g in enumerate(rest):
+        timed.append((2.0 * i + 1.0, functools.partial(g.across, n - 2)))
+        timed.append((2.0 * i + 7.0, functools.partial(g.across, n - 1)))
+    slots = Slots(places, timed)
+
+    def keeps(m):
+        return [
+            pltpu.make_async_copy(packed.at[m], packed_hbm.at[m], local.at[3 + m]),
+            pltpu.make_async_copy(ctx.at[m], ctx_hbm.at[m], local.at[7 + m]),
+        ]
+
+    def heads(m):
+        w = gq[m // 2, m % 2].reshape(D, QKV_PAD)
+        packed[m] = dot(nrm[...], w).astype(bf)
+        attend_group(packed.at[m], mask, rows[m], ctx.at[m], group, functools.partial(slots.tick, m))
+        for copy in keeps(m):
+            copy.start()
+
+    each_of(4, heads)
+    slots.run(None)
+    for g in rest:
+        g.finish()
+    second.finish()
+    for copy in [keep_x, keep_n, keep_q] + [c for m in range(4) for c in keeps(m)]:
+        copy.wait()
+    for g in arrays + [first, second]:
+        g.drain()
+
+
+def front(depth, group, tok, cot, shards, gain, mask, rows):
+    hbm = pl.BlockSpec(memory_space=pl.ANY)
+    vmem = pl.BlockSpec(memory_space=pltpu.VMEM)
+    bf = jnp.bfloat16
+    n = tok.shape[0] * SEG
+    outs = [jax.ShapeDtypeStruct(tok.shape, tok.dtype)] * 2
+    for i, s in enumerate(shards):
+        lead = (2, 2, depth, 2) if i == 0 else (depth, 2, 2, 2)
+        outs.append(jax.ShapeDtypeStruct(lead + s.shape, s.dtype))
+    outs += [jax.ShapeDtypeStruct(shape, bf) for shape in ((n, D), (4, n, QKV_PAD), (4, n, CTX_PAD))]
+    return pl.pallas_call(
+        functools.partial(front_kernel, depth, group),
+        out_shape=outs,
+        in_specs=[hbm] * 6 + [vmem] * 3,
+        out_specs=[hbm] * 9,
+        scratch_shapes=[
+            pltpu.VMEM(tok.shape, bf),
+            pltpu.VMEM(outs[2].shape, bf),
+            pltpu.VMEM((n, D), bf),
+            pltpu.VMEM((4, n, QKV_PAD), bf),
+            pltpu.VMEM((4, n, CTX_PAD), bf),
+            pltpu.SemaphoreType.DMA((11,)),
+        ]
+        + Gather.sems(depth) * 4
+        + Exchange.sems() * 2,
+        compiler_params=pltpu.CompilerParams(
+            collective_id=2, has_side_effects=True, vmem_limit_bytes=56 * 2**20
+        ),
+        name="front",
+    )(tok, cot, *shards, gain, mask, rows)
+
+
+ROW_GAIN, ROW_TABLE, ROW_OTHER = 0, 8, 24
+
+
+def back_kernel(
+    depth, bits, group,
+    packed_hbm, gctx_hbm, gq_hbm, nrm_hbm, x_hbm, gmid_hbm, pu, pi, po, out_s, gain, mask, rows, onehot, other,
+    oq, oo, oi, ou, small, out, gtok,
+    packed, gctx, gq, nrm, x, gmid, acc, sums_s, part_q, gtok_s, local, mine_u, mine_i, mine_o, sem_u, sem_i, sem_o, *scr,
+):
+    p = Place(depth)
+    n = depth
+    bf = jnp.bfloat16
+    u = Scatter(p, False, pu, ou, *scr[0:6], mine_u, sem_u)
+    i_ = Scatter(p, False, pi, oi, *scr[6:12], mine_i, sem_i)
+    o = Scatter(p, False, po, oo, *scr[12:18], mine_o, sem_o)
+    q = Scatter(p, True, part_q, oq, *scr[18:24])
+    arrays = [u, i_, o, q]
+    row_out, row_g = Exchange(p, out_s, out, *scr[24:27]), Exchange(p, gtok_s, gtok, *scr[27:30])
+    total = Sum(p, bits, small, *scr[30:33])
+    heads_in = [
+        [
+            pltpu.make_async_copy(packed_hbm.at[m], packed.at[m], local.at[m]),
+            pltpu.make_async_copy(gctx_hbm.at[m], gctx.at[m], local.at[4 + m]),
+        ]
+        for m in range(4)
+    ]
+    others_in = [
+        pltpu.make_async_copy(src, dst, local.at[8 + k])
+        for k, (src, dst) in enumerate(((nrm_hbm, nrm), (gq_hbm, gq), (x_hbm, x), (gmid_hbm, gmid)))
+    ]
+    for copy in heads_in[0]:
+        copy.start()
+    p.barrier(bits)
+    for g in (u, i_):
+        for k in range(n):
+            g.start(k)
+    for copy in others_in:
+        copy.start()
+    for copies in heads_in[1:]:
+        for copy in copies:
+            copy.start()
+    row_out.start()
+    for k in range(n):
+        o.start(k)
+    small[...] = jnp.zeros_like(small)
+    small[ROW_OTHER:, :] = other[...]
+    acc[...] = jnp.zeros_like(acc)
+    for copies in heads_in:
+        for copy in copies:
+            copy.wait()
+    for copy in others_in:
+        copy.wait()
+
+    span = 10.0
+    places = {(m, j): span * m + 0.63 * (j + 1) for m in range(4) for j in range(12)}
+    places |= {(m, 12): span * (m + 1) for m in range(4)}
+    timed = []
+    for g, half, quarter, ahead in ((u, 0.6, 6.0, 14.0), (i_, 5.0, 18.0, 30.0), (o, 11.0, 27.0, 39.0)):
+        for k in range(n):
+            timed.append((half + 1.3 * k, functools.partial(g.to_half, k)))
+            timed.append((quarter + 3.0 * k, functools.partial(lambda g, k: (g.to_quarter(k), g.origin(k)), g, k)))
+            timed.append((ahead + 4.0 * k, functools.partial(g.forward, k)))
+    slots = Slots(places, timed)
+
+    def heads(m):
+        tick = functools.partial(slots.tick, m)
+        attend_group_back(packed.at[m], mask, rows[m], gctx.at[m], packed.at[m], sums_s.at[m], group, tick)
+        g = packed[m]
+        for y in range(2):
+            for c in range(2):
+                pl.when(m == 2 * y + c)(functools.partial(weight_part, y, c))
+        acc[...] += dot(g, gq[m // 2, m % 2].reshape(D, QKV_PAD), NT)
+        tick(12)
+
+    def weight_part(y, c):
+        g = dot(nrm[...], packed[2 * y + c], TN).astype(bf)
+        part_q[y, c] = g.reshape(part_q.shape[2:])
+
+    each_of(4, heads)
+    for k in range(n):
+        q.start(k)
+    slots.run(None)
+    small[ROW_TABLE : ROW_TABLE + 16, :] = jnp.zeros((16, 128), jnp.float32)
+    for m in range(4):
+        small[ROW_TABLE + 3 * m : ROW_TABLE + 3 * m + 3, :] = lax.dot_general(
+            sums_s[m], onehot[...], NN, precision=FULL_PRECISION, preferred_element_type=jnp.float32
+        )
+
+    def last(s, g_gain):
+        r = rows_of(s, SEG)
+        v = x[s].astype(jnp.float32)
+        g_n1 = acc[r, :]
+        scale = lax.rsqrt(jnp.mean(v * v, axis=-1, keepdims=True) + NORM_EPS)
+        scaled = gain[...] * g_n1
+        centre = jnp.mean(v * scaled, axis=-1, keepdims=True)
+        gtok_s[s] = (gmid[r, :] + scale * scaled - v * (scale * scale * scale * centre)).astype(bf)
+        return g_gain + jnp.sum(v * scale * g_n1, axis=0, keepdims=True)
+
+    g_gain = lax.fori_loop(0, x.shape[0], last, jnp.zeros((1, D), jnp.float32))
+    for k in range(D // 128):
+        small[ROW_GAIN + k : ROW_GAIN + k + 1, :] = g_gain[:, 128 * k : 128 * (k + 1)]
+    for k in range(n):
+        q.to_half(k)
+    row_g.start()
+    for k in range(n):
+        q.to_quarter(k)
+        q.origin(k)
+    for k in range(n):
+        q.forward(k)
+    close(arrays, total)
+    for r in (row_out, row_g):
+        r.finish()
+    for g in arrays + [row_out, row_g, total]:
+        g.drain()
+
+
+def back(depth, bits, group, packed, gctx, gq, nrm, x, gmid, parts, out_s, gain, mask, rows, onehot, other):
+    hbm = pl.BlockSpec(memory_space=pl.ANY)
+    vmem = pl.BlockSpec(memory_space=pltpu.VMEM)
+    bf, f32 = jnp.bfloat16, jnp.float32
+    pq_shape = gq.shape
+    shape = jax.ShapeDtypeStruct
+    small_rows = ROW_OTHER + other.shape[0]
+    outs = [shape(pq_shape[4:], f32)] + [shape(s.shape[4:], f32) for s in (parts[2], parts[1], parts[0])]
+    outs += [shape((small_rows, 128), f32), shape(out_s.shape, bf), shape(x.shape, bf)]
+    dma = pltpu.SemaphoreType.DMA
+    scratch = [
+        pltpu.VMEM(packed.shape, bf),
+        pltpu.VMEM(gctx.shape, bf),
+        pltpu.VMEM(gq.shape, bf),
+        pltpu.VMEM(nrm.shape, bf),
+        pltpu.VMEM(x.shape, bf),
+        pltpu.VMEM(gmid.shape, f32),
+        pltpu.VMEM(gmid.shape, f32),
+        pltpu.VMEM((4, 3, 768), f32),
+        pltpu.VMEM(pq_shape, bf),
+        pltpu.VMEM(x.shape, bf),
+        dma((12,)),
+    ]
+    scratch += [pltpu.VMEM((depth, 2, 2) + s.shape[4:], bf) for s in parts]
+    scratch += [dma((depth,))] * 3
+    for s in (*(s.shape for s in parts), pq_shape):
+        scratch += Scatter.scratch(depth, *s[4:])
+    scratch += Exchange.sems() * 2 + Sum.scratch(bits, small_rows)
+    return pl.pallas_call(
+        functools.partial(back_kernel, depth, bits, group),
+        out_shape=outs,
+        in_specs=[hbm] * 10 + [vmem] * 5,
+        out_specs=[vmem] * 5 + [hbm] * 2,
+        scratch_shapes=scratch,
+        compiler_params=pltpu.CompilerParams(
+            collective_id=3, has_side_effects=True, vmem_limit_bytes=63 * 2**20
+        ),
+        name="back",
+    )(packed, gctx, gq, nrm, x, gmid, *parts, out_s, gain, mask, rows, onehot, other)
 
 
 def round_up(n, m):
@@ -866,20 +1404,11 @@
     seg_count = tok_rows // SEG
     o_rows, in_rows, q_rows = w_o.shape[0], w_in.shape[1], w_qkv.shape[0]
     bf = jnp.bfloat16
-    wq = pad_rows(head_columns(w_qkv.astype(bf)), round_up(q_rows, 16))
+    group = o_rows if o_rows % 24 == 0 and round_up(o_rows, 16) * 3 == o_rows * 4 else 3 * DH
+    wq = pad_rows(head_columns(w_qkv.astype(bf), group), round_up(q_rows, 16))
     wo = pad_rows(w_o.astype(bf), round_up(o_rows, 16))
     wi = pad_rows(w_in.astype(bf).T, round_up(in_rows, 16))
     wu = pad_rows(w_out.astype(bf), round_up(in_rows, 16))
-    tok_s, cot_s, gq, go, gi, gu = gather_all(
-        depth, tokens.reshape(seg_count, SEG, D), cotangent.reshape(seg_count, SEG, D), (wq, wo, wi, wu)
-    )
-
-    def plain(g, rows):
-        return g.reshape(devices, g.shape[-2], D)[:, :rows].reshape(devices * rows, D)
-
-    dense_o, dense_in_t, dense_out = plain(go, o_rows), plain(gi, in_rows), plain(gu, in_rows)
-    qkv_full = gq.reshape(mp_count, dp_count, wq.shape[0], QKV_PAD)[:, :, :q_rows].reshape(mp_count, D, QKV_PAD)
-    tokens_s = tok_s.reshape(tok_rows, D)
     own_lengths = jnp.stack([
         lengths[member], lengths[4 + member // 2 + 2 * (member % 2)], lengths[8 + member], lengths[12 + member]
     ])
@@ -891,80 +1420,99 @@
         pieces.append((spots[None, :] < own_lengths[first : first + seqs, None]).reshape(-1))
         first += seqs
     live = jnp.concatenate(pieces)
-    x_float = tokens_s.astype(jnp.float32)
     mask = key_mask(live)
     rows = offset_row(pos_table).reshape(mp_count, 3, 512)
-    normed_attn, packed, context = attention(tokens_s, gain_attn[None], qkv_full, mask, rows)
-    context_rows = context[:, :, : 3 * DH].transpose(1, 0, 2).reshape(tok_rows, D)
-    midway = x_float + jnp.dot(context_rows, dense_o, preferred_element_type=jnp.float32)
-    normed_ffn = normed(midway, gain_ffn).astype(bf)
-    ffn_pre = jnp.dot(normed_ffn, dense_in_t.T, preferred_element_type=jnp.float32)
-    ffn_act = gelu_exact(ffn_pre).astype(bf)
-    ffn_out = jnp.dot(ffn_act, dense_out, preferred_element_type=jnp.float32)
-    ffn_low = ffn_out.astype(bf)
-    w_down, w_up = adapter_weights(phm_rules, down_left, down_right, up_left, up_right)
-    down_low = w_down.astype(bf)
-    up_low = w_up.astype(bf)
-    squeezed = jnp.dot(ffn_low, down_low, preferred_element_type=jnp.float32)
-    lifted = gelu_exact(squeezed).astype(bf)
-    result = (midway + ffn_out + jnp.dot(lifted, up_low, preferred_element_type=jnp.float32)).astype(bf)
-    grad_out = cot_s.reshape(tok_rows, D).astype(jnp.float32) * live[:, None].astype(jnp.float32)
-    grad_out_low = grad_out.astype(bf)
-    grad_w_up = jnp.dot(lifted.T, grad_out_low, preferred_element_type=jnp.float32)
-    _, gelu_back_sq = jax.vjp(gelu_exact, squeezed)
-    grad_sq = gelu_back_sq(jnp.dot(grad_out_low, up_low.T, preferred_element_type=jnp.float32))[0].astype(bf)
-    grad_w_down = jnp.dot(ffn_low.T, grad_sq, preferred_element_type=jnp.float32)
-    grad_ffn = (grad_out + jnp.dot(grad_sq, down_low.T, preferred_element_type=jnp.float32)).astype(bf)
-    grad_w_out = jnp.dot(ffn_act.T, grad_ffn, preferred_element_type=jnp.float32).astype(bf)
-    _, gelu_back_pre = jax.vjp(gelu_exact, ffn_pre)
-    grad_pre = gelu_back_pre(jnp.dot(grad_ffn, dense_out.T, preferred_element_type=jnp.float32))[0].astype(bf)
-    grad_w_in = jnp.dot(grad_pre.T, normed_ffn, preferred_element_type=jnp.float32).astype(bf)
-    _, norm_back_ffn = jax.vjp(normed, midway, gain_ffn)
-    grad_mid_part, grad_gain_ffn = norm_back_ffn(jnp.dot(grad_pre, dense_in_t, preferred_element_type=jnp.float32))
-    grad_mid = grad_out + grad_mid_part
-    grad_mid_low = grad_mid.astype(bf)
-    grad_w_o = jnp.dot(context_rows.T, grad_mid_low, preferred_element_type=jnp.float32).astype(bf)
-    grad_context = jnp.dot(grad_mid_low, dense_o.T, preferred_element_type=jnp.float32).astype(bf)
-    grad_context = grad_context.reshape(tok_rows, mp_count, 3 * DH).transpose(1, 0, 2)
-    grad_context = jnp.pad(grad_context, ((0, 0), (0, 0), (0, CTX_PAD - 3 * DH)))
-    packed_grads, sums = attention_back(packed, grad_context, mask, rows)
-    table_grad = jnp.einsum("hr,rb->bh", sums.reshape(HEADS, 768), table_onehot(), precision=FULL_PRECISION)
-    grad_w_qkv = jnp.einsum("td,mtc->mdc", normed_attn, packed_grads, preferred_element_type=jnp.float32).astype(bf)
-    grad_n1 = jnp.einsum("mtc,mdc->td", packed_grads, qkv_full, preferred_element_type=jnp.float32)
-    _, norm_back_attn = jax.vjp(normed, x_float, gain_attn)
-    grad_x_part, grad_gain_attn = norm_back_attn(grad_n1)
-    grad_tokens = (grad_mid + grad_x_part).astype(bf)
-    _, adapter_back = jax.vjp(adapter_weights, phm_rules, down_left, down_right, up_left, up_right)
-    small_list = (grad_gain_attn, grad_gain_ffn, table_grad) + adapter_back((grad_w_down, grad_w_up))
-    flat = jnp.concatenate([s.reshape(-1) for s in small_list])
-    small_rows = round_up(-(-flat.size // 128), 8)
-    small = jnp.pad(flat, (0, small_rows * 128 - flat.size)).reshape(small_rows, 128)
+    tok_in, cot_in = tokens.reshape(seg_count, SEG, D), cotangent.reshape(seg_count, SEG, D)
+    merged = depth <= 8 and wq.shape[0] == q_rows
+    if merged:
+        tok_s, cot_s, gq, go, gi, gu, normed_attn, packed, context = front(
+            depth, group, tok_in, cot_in, (wq, wo, wi, wu), gain_attn[None], mask, rows
+        )
+    else:
+        tok_s, cot_s, gq, go, gi, gu = gather_all(depth, tok_in, cot_in, (wq, wo, wi, wu))
+    tokens_s = tok_s.reshape(tok_rows, D)
+
+    def plain(g, rows):
+        return g.reshape(devices, g.shape[-2], D)[:, :rows].reshape(devices * rows, D)
 
     def slots(g, rows):
         padded = jnp.pad(g.reshape(devices, rows, D), ((0, 0), (0, round_up(rows, 16) - rows), (0, 0)))
         return padded.reshape(depth, 2, 2, 2, padded.shape[1], D)
 
-    part_q = grad_w_qkv.reshape(mp_count, dp_count, q_rows, QKV_PAD)
-    part_q = jnp.pad(part_q, ((0, 0), (0, 0), (0, wq.shape[0] - q_rows), (0, 0)))
-    part_q = part_q.reshape(2, 2, depth, 2, wq.shape[0], QKV_PAD)
-    oq, oo, oi, ou, summed, out, gtok = scatter_all(
-        depth,
-        bits,
-        (part_q, slots(grad_w_o, o_rows), slots(grad_w_in, in_rows), slots(grad_w_out, in_rows)),
-        small,
-        result.reshape(seg_count, SEG, D),
-        grad_tokens.reshape(seg_count, SEG, D),
+    dense_in, dense_out = plain(gi, in_rows), plain(gu, in_rows)
+    if group == o_rows:
+        dense_o = go.reshape(mp_count, CTX_PAD, D)
+    else:
+        dense_o = plain(go, o_rows).reshape(mp_count, 3 * DH, D)
+        dense_o = jnp.pad(dense_o, ((0, 0), (0, CTX_PAD - 3 * DH), (0, 0)))
+    qkv_full = gq.reshape(mp_count, dp_count, wq.shape[0], QKV_PAD)[:, :, :q_rows].reshape(mp_count, D, QKV_PAD)
+    if not merged:
+        normed_attn, packed, context = attention(tokens_s, gain_attn[None], qkv_full, mask, rows, group)
+    w_down, w_up = adapter_weights(phm_rules, down_left, down_right, up_left, up_right)
+    wide = ((0, 0), (0, ADAPT_PAD - ADAPT))
+    result, grad_mid, grad_context, grad_w_o, grad_w_in, grad_w_out, grad_gain_ffn, grad_w_down, grad_w_up = middle(
+        tokens_s,
+        context,
+        dense_o,
+        dense_in,
+        dense_out,
+        cot_s.reshape(tok_rows, D),
+        gain_ffn[None],
+        jnp.pad(w_down.astype(bf), wide),
+        jnp.pad(w_up.T.astype(bf), wide),
+        live[:, None].astype(jnp.float32),
     )
-    smalls = []
-    flat = summed.reshape(-1)
+    grad_w_down, grad_w_up = grad_w_down[:, :ADAPT], grad_w_up[:, :ADAPT].T
+    if group == o_rows:
+        part_o = grad_w_o.reshape(depth, 2, 2, 2, round_up(o_rows, 16), D)
+    else:
+        part_o = slots(grad_w_o.reshape(mp_count, CTX_PAD, D)[:, : 3 * DH].reshape(D, D), o_rows)
+    _, adapter_back = jax.vjp(adapter_weights, phm_rules, down_left, down_right, up_left, up_right)
+    small_list = (grad_gain_ffn[0],) + adapter_back((grad_w_down, grad_w_up))
+    flat = jnp.concatenate([s.reshape(-1) for s in small_list])
+    other_rows = round_up(-(-flat.size // 128), 8)
+    other = jnp.pad(flat, (0, other_rows * 128 - flat.size)).reshape(other_rows, 128)
+    part_in, part_out = slots(grad_w_in, in_rows), slots(grad_w_out, in_rows)
+    result = result.reshape(seg_count, SEG, D)
+    onehot = jnp.asarray(np.pad(table_onehot(), ((0, 0), (0, 128 - NB))))
+    if merged:
+        oq, oo, oi, ou, summed, out, gtok = back(
+            depth, bits, group, packed, grad_context, gq, normed_attn, tok_s, grad_mid,
+            (part_out, part_in, part_o), result, gain_attn[None], mask, rows, onehot, other,
+        )
+    else:
+        packed_grads, sums = attention_back(packed, grad_context, mask, rows, group)
+        table_grad = jnp.dot(sums.reshape(HEADS, 768), onehot, precision=FULL_PRECISION)
+        grad_w_qkv = jnp.einsum("td,mtc->mdc", normed_attn, packed_grads, preferred_element_type=jnp.float32).astype(bf)
+        grad_n1 = jnp.einsum("mtc,mdc->td", packed_grads, qkv_full, preferred_element_type=jnp.float32)
+        _, norm_back_attn = jax.vjp(normed, tokens_s.astype(jnp.float32), gain_attn)
+        grad_x_part, grad_gain_attn = norm_back_attn(grad_n1)
+        grad_tokens = (grad_mid + grad_x_part).astype(bf)
+        small = jnp.concatenate([
+            jnp.pad(grad_gain_attn.reshape(D // 128, 128), ((0, ROW_TABLE - D // 128), (0, 0))),
+            jnp.pad(table_grad, ((0, ROW_OTHER - ROW_TABLE - HEADS), (0, 0))),
+            other,
+        ])
+        part_q = grad_w_qkv.reshape(mp_count, dp_count, q_rows, QKV_PAD)
+        part_q = jnp.pad(part_q, ((0, 0), (0, 0), (0, wq.shape[0] - q_rows), (0, 0)))
+        part_q = part_q.reshape(2, 2, depth, 2, wq.shape[0], QKV_PAD)
+        oq, oo, oi, ou, summed, out, gtok = scatter_all(
+            depth, bits, (part_q, part_o, part_in, part_out), small, result, grad_tokens.reshape(seg_count, SEG, D)
+        )
+    smalls = [
+        summed[ROW_GAIN : ROW_GAIN + D // 128].reshape(D),
+        summed[ROW_TABLE : ROW_TABLE + HEADS, :NB].T,
+    ]
+    flat = summed[ROW_OTHER:].reshape(-1)
     first = 0
     for s in small_list:
         smalls.append(flat[first : first + s.size].reshape(s.shape))
         first += s.size
+    smalls = [smalls[0], smalls[2], smalls[1], *smalls[3:]]
     return (
         out.reshape(tok_rows, D),
         gtok.reshape(tok_rows, D),
-        from_head_columns(oq[:q_rows]),
+        from_head_columns(oq[:q_rows], group),
         oo[:o_rows],
         oi[:in_rows].T,
         ou[:in_rows],

time: 473 us -> 327 us (0.69); the launches traced: 468 us -> 329 us
  matrix products: 136 us -> 7.92 us
  local copies, waits for them, and re-layouts: 56.8 us -> 30.6 us
  Pallas kernels: 256 us -> 282 us
  other arithmetic: 17.6 us -> 7.43 us
    dot_general x18 -> x0, matrix products: 127 us -> none  [the longest x1 36.9 us: local(): jnp.dot(normed_ffn, dense_in_t.T, preferred_element_type=jnp.float32)]
    pallas_call x4 -> x3, Pallas kernels: 256 us -> 282 us  [the longest x1 118 us: back(): pl.pallas_call(functools.partial(back_kernel, depth, bits, group), out_sh...]
    convert_element_type x2 -> x0, other arithmetic: 6.91 us -> none  [the longest x1 4.82 us: local(): grad_tokens = (grad_mid + grad_x_part).astype(bf)]
    convert_element_type x5 -> x7, local copies, waits for them, and re-layouts: 6.74 us -> 1.74 us  [the longest x1 1.04 us: local(): live[:, None].astype(jnp.float32)]
where the time goes in v2:
time: 327 us; the launch traced here: 329 us
  Pallas kernels  282 us (86%)
  local copies, waits for them, and re-layouts  30.6 us (9%)
  matrix products  7.92 us (2%)
  other arithmetic  7.43 us (2%)
    pallas_call x1, Pallas kernels, back(): pl.pallas_call(functools.partial(back_kernel, depth, bits, group), out_sh...  118 us
    pallas_call x1, Pallas kernels, front(): pl.pallas_call(functools.partial(front_kernel, depth, group), out_shape=o...  94.4 us
    pallas_call x1, Pallas kernels, middle(): pl.pallas_call(middle_kernel, out_shape=[shape((n, D), bf), shape((n, D),...  68.9 us

profile of v2, /device:TPU:0, one launch (start us, length us, event | category | flops | bytes accessed | tf_op | source)
XLA Modules:
  0.0 328.9 jit_solution(3499138469892532299)
XLA Ops:
  0.7 1.4 fusion.38
  2.1 0.7 iota_compare_fusion
  2.8 0.7 iota_compare_fusion.2
  3.4 1.4 pad_add_fusion
  4.9 1.3 broadcast_in_dim.12.gain
  6.2 1.3 broadcast_in_dim.25.gain
  7.5 0.8 copy.75
  8.3 1.3 convolution_bitcast_fusion.2
  9.6 0.6 reshape.228.rows
  10.2 0.9 convert_element_type.49
  11.1 0.6 pad.20.wo
  11.7 0.9 slice.78
  12.9 0.9 slice.77
  14.1 0.7 pad_maximum_fusion.1.wq
  14.8 0.7 fusion.1
  15.8 0.7 pad.22.up
  16.5 0.7 fusion
  17.6 0.7 pad.21.down
  18.3 0.7 convert_bitcast_fusion.wi
  19.0 0.7 convert_element_type.51.wu
  19.7 0.9 select_convert_fusion.mask
  20.6 1.0 copy.80.live
  21.6 94.4 %front.1 = (bf16[8,128,768]{2,1,0:T(8,128)(2,1)}, bf16[8,128,768]{2,1,0:T(8,128)(2,1)}, bf16[2,2,4,2,96,640]{5,4,3,2,1,0:T(8,128)(2,1)}, bf16[4,2,2,2,32,768]{5,...) custom-call(bf16[8,128,768]{2,1,0:T(8,128)(2,1)} %bitcast.128, ...), custom_call_target="tpu_custom_call" | custom-call | tf_op jit(solution)/shard_map/front/pallas_call | solution.py:1191
  116.0 68.9 %middle.1 = (bf16[1024,768]{1,0:T(8,128)(2,1)}, f32[1024,768]{1,0:T(8,128)}, bf16[4,1024,256]{2,1,0:T(8,128)(2,1)}, bf16[1024,768]{1,0:T(8,128)(2,1)}, bf16[3072...) custom-call(bf16[1024,768]{1,0:T(8,128)(2,1)} %bitcast.117, ...), custom_call_target="tpu_custom_call" | custom-call | tf_op jit(solution)/shard_map/middle/pallas_call | solution.py:1051
  184.9 0.7 reduce
  185.7 1.1 copy.83
  187.3 1.1 convolution_bitcast_fusion
  188.8 1.0 fusion.16
  190.5 1.1 convolution_bitcast_fusion.1
  191.9 1.0 fusion.20
  193.2 0.6 pad_bitcast_fusion.other
  193.8 118.4 %back.1 = (f32[96,640]{1,0:T(8,128)}, f32[32,768]{1,0:T(8,128)}, f32[96,768]{1,0:T(8,128)}, f32[96,768]{1,0:T(8,128)}, f32[48,128]{1,0:T(8,128)}, /*index=5*/bf1...) custom-call(bf16[4,1024,640]{2,1,0:T(8,128)(2,1)} %get-tuple-element.39.packed_hbm, ...), custom_call_target="tpu_custom_call" | custom-call | tf_op jit(solution)/shard_map/back/pallas_call | solution.py:1357
  312.2 1.3 slice_bitcast_fusion.1
  313.5 1.3 slice_bitcast_fusion.2
  314.8 0.7 slice_bitcast_fusion.4
  315.7 0.7 reshape.254
  316.3 0.7 reshape.253
  317.0 0.7 reshape.252
  317.6 0.7 reshape.251
  318.3 1.5 slice.65
  319.8 0.9 slice.63
  320.7 1.0 slice.62
  322.2 0.8 copy.87
  324.1 1.1 copy.135
  325.2 0.8 copy-done.1
  326.1 1.1 copy.136
  327.2 0.7 copy.137
  327.9 0.7 copy.138
  (67 shorter events, 5.2 us)
Async XLA Ops:
  0.6 7.7 %copy-start = (f32[32,12]{0,1:T(8,128)S(1)}, f32[32,12]{0,1:T(8,128)}, u32[]{:S(2)}) copy-start(f32[32,12]{0,1:T(8,128)} %param.26) | copy-start | bytes 4612
  0.7 14.1 %copy-start.9 = (f32[4,12]{1,0:T(4,128)S(1)}, f32[4,12]{1,0:T(4,128)}, u32[]{:S(2)}) copy-start(f32[4,12]{1,0:T(4,128)} %param.30) | copy-start | bytes 580
  0.7 14.1 %copy-start.12 = (f32[4,192]{1,0:T(4,128)S(1)}, f32[4,192]{1,0:T(4,128)}, u32[]{:S(2)}) copy-start(f32[4,192]{1,0:T(4,128)} %param.31) | copy-start | bytes 9220
  6.2 10.3 %copy-start.8 = (f32[4,12]{1,0:T(4,128)S(1)}, f32[4,12]{1,0:T(4,128)}, u32[]{:S(2)}) copy-start(f32[4,12]{1,0:T(4,128)} %param.29) | copy-start | bytes 580
  6.2 10.3 %copy-start.11 = (f32[4,192]{1,0:T(4,128)S(1)}, f32[4,192]{1,0:T(4,128)}, u32[]{:S(2)}) copy-start(f32[4,192]{1,0:T(4,128)} %param.28) | copy-start | bytes 9220
  13.8 4.5 %copy-start.4 = (f32[768,96]{0,1:T(8,128)S(1)}, f32[768,96]{0,1:T(8,128)}, u32[]{:S(2)}) copy-start(f32[768,96]{0,1:T(8,128)} %param.22) | copy-start | bytes 884740
  14.8 4.2 %copy-start.5 = (f32[96,768]{1,0:T(8,128)S(1)}, f32[96,768]{1,0:T(8,128)}, u32[]{:S(2)}) copy-start(f32[96,768]{1,0:T(8,128)} %param.23) | copy-start | bytes 884740
  116.0 72.5 %copy-start.10 = (f32[4,4,4]{2,1,0:T(4,128)S(1)}, f32[4,4,4]{2,1,0:T(4,128)}, u32[]{:S(2)}) copy-start(f32[4,4,4]{2,1,0:T(4,128)} %param.27) | copy-start | bytes 772
  184.9 4.9 %copy-start.3 = (f32[768,128]{1,0:T(8,128)S(1)}, f32[768,128]{1,0:T(8,128)}, u32[]{:S(2)}) copy-start(f32[768,128]{1,0:T(8,128)} %get-tuple-element.55) | copy-start | bytes 1179652
  320.7 3.3 %copy-start.2 = (bf16[8,128,768]{2,1,0:T(8,128)(2,1)S(1)}, bf16[8,128,768]{2,1,0:T(8,128)(2,1)}, u32[]{:S(2)}) copy-start(bf16[8,128,768]{2,1,0:T(8,128)(2,1)} %get-tuple-element.57) | copy-start | bytes 4718596
  324.1 2.0 copy-start.1
  326.1 1.1 copy-start.7
  326.1 1.9 copy-start.6

commit v3 on v2

--- a/solution.py
+++ b/solution.py
@@ -14,6 +14,7 @@
 NB = 32
 MAXDIST = 128
 ADAPT = 48
+KRON = 4
 LEN_LONG = 512
 LEN_MID = 256
 LEN_SHORT = 128
@@ -45,20 +46,6 @@
     return values * lax.rsqrt(jnp.mean(values * values, axis=-1, keepdims=True) + NORM_EPS) * gain
 
 
-def gelu_exact(values):
-    return jax.nn.gelu(values, approximate=False)
-
-
-def adapter_weights(phm_rules, down_left, down_right, up_left, up_right):
-    w_down = jnp.einsum(
-        "iab,ip,iq->apbq", phm_rules, down_left, down_right, precision=FULL_PRECISION
-    ).reshape(D, ADAPT)
-    w_up = jnp.einsum(
-        "iab,ip,iq->apbq", phm_rules, up_left, up_right, precision=FULL_PRECISION
-    ).reshape(ADAPT, D)
-    return (w_down, w_up)
-
-
 MESH = pl.DeviceIdType.MESH
 
 
@@ -82,6 +69,13 @@
         for core in (0, 1):
             pl.when(self.c == core)(functools.partial(run, core))
 
+    def nearest(self, e):
+        n, z = self.depth, self.z
+        ahead = 1 - 2 * (z // ((n + 1) // 2))
+        short = jnp.minimum(z, n - 1 - z)
+        around = (1 - 2 * (e % 2)) * ((e + 1) // 2)
+        return z + ahead * jnp.where(e <= 2 * short, around, e - short)
+
     def flip(self, bit):
         step = 1 << bit
         return (self.d + step * (1 - 2 * ((self.d // step) % 2)), self.m)
@@ -190,18 +184,15 @@
         if not (isinstance(k, int) and k == 0):
             pl.when(p.z + k < p.depth)(lambda: p.by_core(lambda core: one(p.z + k, core)))
 
+    def finish_at(self, z):
+        def one(core):
+            for b in (0, 1):
+                self._sib(1 - core, b, z).wait_recv()
+
+        self.p.by_core(one)
+
     def finish(self):
-        p, n = self.p, self.p.depth
-
-        def each(z, carry):
-            def one(core):
-                for b in (0, 1):
-                    self._sib(1 - core, b, z).wait_recv()
-
-            p.by_core(one)
-            return carry
-
-        lax.fori_loop(0, n, each, 0)
+        each_of(self.p.depth, self.finish_at)
 
     def drain(self):
         p, n = self.p, self.p.depth
@@ -606,20 +597,15 @@
 TILE = 128
 QKV_PAD = 640
 CTX_PAD = 256
+ADAPT_PAD = 128
 MASK_LOW = -1e9
 NN = (((1,), (0,)), ((), ()))
 NT = (((1,), (1,)), ((), ()))
+TN = (((0,), (0,)), ((), ()))
 
 
 def dot(a, b, dims=NN):
     return lax.dot_general(a, b, dims, preferred_element_type=jnp.float32)
-
-
-def offset_row(pos_table):
-    buckets = rel_buckets(257)
-    offset = np.clip(256 - np.arange(512), -256, 256) + 256
-    onehot = (buckets[offset][:, None] == np.arange(NB)[None, :]).astype(np.float32)
-    return jnp.einsum("rb,bh->hr", jnp.asarray(onehot), pos_table, precision=FULL_PRECISION)
 
 
 def table_onehot():
@@ -741,7 +727,7 @@
                 outs.append(dot(values, probs))
             whole = jnp.concatenate([outs[h][lo:hi] for lo, hi, h in head_runs(group)], axis=0)
             context[here, :] = whole.T.astype(jnp.bfloat16)
-        tick(number)
+            tick((number, q0))
 
 
 def attend_group_back(packed, mask_ref, rows, grad_context, grad_packed, sums, group, tick=no_tick):
@@ -881,22 +867,108 @@
     return jnp.concatenate([qk, v], axis=1)
 
 
-def from_head_columns(g, group):
-    n = g.shape[0]
-    qk = g[:, : 6 * DH].reshape(n, 3, 2 * DH)
-    v = g[:, 6 * DH :].reshape(n, 3 * DH // group, group * 4 // 3)[:, :, :group].reshape(n, 3, DH)
-    return jnp.concatenate([qk, v], axis=2)
-
-
 def key_mask(live):
     lane = jnp.arange(TILE)[None, :]
     return jnp.where((lane == DH) & ~live[:, None], MASK_LOW, 0.0).astype(jnp.bfloat16)
 
 
-TN = (((0,), (0,)), ((), ()))
-FCH = 512
+def precise(a, b, dims=NN):
+    return lax.dot_general(a, b, dims, precision=FULL_PRECISION, preferred_element_type=jnp.float32)
+
+
+def offset_onehot():
+    buckets = rel_buckets(257)
+    offset = np.clip(256 - np.arange(512), -256, 256) + 256
+    return (np.arange(NB)[:, None] == buckets[offset][None, :]).astype(np.float32)
+
+
+def column_choice(group):
+    choice = np.zeros((9 * DH, QKV_PAD), np.float32)
+    for h in range(3):
+        for k in range(2 * DH):
+            choice[3 * DH * h + k, TILE * h + k] = 1
+    heads, column = value_lanes(group)
+    for lane in range(CTX_PAD):
+        if heads[lane] >= 0:
+            choice[3 * DH * heads[lane] + 2 * DH + column[lane] % DH, 3 * TILE + lane] = 1
+    return choice
+
+
+def own_length(lengths, member, number):
+    at = (member, 4 + member // 2 + 2 * (member % 2), 8 + member, 12 + member)[number]
+    return lengths[at]
+
+
+def fill_mask(mask, lengths, member):
+    for number, (offset, length) in enumerate(SPANS):
+        row = lax.broadcasted_iota(jnp.int32, (length, TILE), 0)
+        lane = lax.broadcasted_iota(jnp.int32, (length, TILE), 1)
+        dead = jnp.logical_and(row >= own_length(lengths, member, number), lane == DH)
+        mask[offset : offset + length, :] = jnp.where(dead, MASK_LOW, 0.0).astype(jnp.bfloat16)
+
+
+def fill_rows(rows, pos_table, onehot):
+    table = precise(pos_table[...], onehot[...])
+    for m in range(4):
+        rows[m] = table[3 * m : 3 * m + 3, :]
+
+
+KA = ADAPT // KRON
+
+
+def adapter_constants():
+    i, b = np.arange(16) // 4, np.arange(16) % 4
+    same = (np.arange(4)[:, None] == i[None, :]).astype(np.float32)
+    pick = np.zeros((4, 4, 16), np.float32)
+    pick[i, b, np.arange(16)] = 1
+    fold = np.zeros((ADAPT_PAD, KA), np.float32)
+    fold[np.arange(ADAPT), np.arange(ADAPT) % KA] = 1
+    agree = np.zeros((ADAPT_PAD, 16), np.float32)
+    agree[:ADAPT] = np.arange(ADAPT)[:, None] // KA == b[None, :]
+    return same, pick, fold, agree
+
+
+class Factor:
+    def __init__(self, rules, tall, short, consts):
+        self.same, _, self.fold, self.agree = consts
+        spread = precise(tall, self.same, TN)
+        self.tall = jnp.concatenate([spread] * KRON, axis=0)
+        rows = spread.shape[0]
+        self.rules = jnp.concatenate(
+            [jnp.broadcast_to(rules[a : a + 1, :], (rows, 16)) for a in range(KRON)], axis=0
+        )
+        self.short = precise(self.fold, precise(short, self.same, TN)) * self.agree
+
+    def whole(self):
+        return precise(self.rules * self.tall, self.short, NT)
+
+    def back(self, grad):
+        wide = precise(grad, self.short)
+        rows = wide.shape[0] // KRON
+        tall = wide * self.rules
+        tall = sum(tall[a * rows : (a + 1) * rows] for a in range(KRON))
+        rules = wide * self.tall
+        rules = [jnp.sum(rules[a * rows : (a + 1) * rows], axis=0, keepdims=True) for a in range(KRON)]
+        short = precise(self.rules * self.tall, grad, TN) * self.agree.T
+        short = precise(precise(self.same, short), self.fold)
+        return jnp.concatenate(rules, axis=0), precise(self.same, tall, NT), short
+
+
+def rule_tables(rules, pick):
+    return [sum(precise(rules[i], pick[i], dims) for i in range(KRON)) for dims in (NN, TN)]
+
+
+ROW_GAIN, ROW_TABLE, ROW_OTHER = 0, 8, 24
+ROW_FFN, ROW_DL, ROW_UR, ROW_DR, ROW_UL, ROW_RULES, ROW_END = 0, 8, 16, 24, 28, 32, 48
+
+
+def put_row(ref, at, row):
+    for k in range(row.shape[1] // 128):
+        ref[at + k : at + k + 1, :] = row[:, 128 * k : 128 * (k + 1)]
+
+
+FCH = 768
 RCH = 256
-ADAPT_PAD = 128
 
 
 def gelu_both(v):
@@ -912,14 +984,145 @@
     lax.fori_loop(0, count, lambda i, carry: (body(i), carry)[1], 0)
 
 
+class Layer:
+    def __init__(self, **refs):
+        self.__dict__.update(refs)
+        self.n = self.n2.shape[0]
+
+    def midway(self, i):
+        r = rows_of(i)
+        total = self.x_rows(i)
+        for m in range(4):
+            total = total + dot(self.ctx[m, r, :], self.wo(m))
+        self.mid[r, :] = total
+        scale = lax.rsqrt(jnp.mean(total * total, axis=-1, keepdims=True) + NORM_EPS)
+        self.n2[r, :] = (total * scale * self.gain[...]).astype(jnp.bfloat16)
+
+    def forward(self, j):
+        f = rows_of(j, self.chunk)
+        for half in range(2):
+            r = pl.ds(half * (self.n // 2), self.n // 2)
+            value, slope = gelu_both(dot(self.n2[r, :], self.wi(j), NT))
+            value = value.astype(jnp.bfloat16)
+            self.act[r, f] = value
+            self.dg[r, f] = slope.astype(jnp.bfloat16)
+            self.acc[r, :] += dot(value, self.wu(j))
+
+    def factors(self):
+        consts = [c[...] for c in self.consts]
+        by_a, by_b = rule_tables(self.rules, consts[1])
+        d_left, d_right, u_left, u_right = self.sides
+        return (
+            Factor(by_a, d_left[...], d_right[...], consts),
+            Factor(by_b, u_right[...], u_left[...], consts),
+        )
+
+    def prepare(self, member):
+        down, up = self.factors()
+        self.down[...] = down.whole().astype(jnp.bfloat16)
+        self.up[...] = up.whole().astype(jnp.bfloat16)
+        for number, (offset, length) in enumerate(SPANS):
+            row = lax.broadcasted_iota(jnp.int32, (length, 1), 0)
+            alive = row < own_length(self.lengths, member, number)
+            self.live[offset : offset + length, :] = jnp.where(alive, 1.0, 0.0)
+
+    def adapter(self, i):
+        bf = jnp.bfloat16
+        r = rows_of(i)
+        ffn = self.acc[r, :]
+        low = ffn.astype(bf)
+        value, slope = gelu_both(dot(low, self.down[...]))
+        value = value.astype(bf)
+        self.res[r, :] = (self.mid[r, :] + ffn + dot(value, self.up[...], NT)).astype(bf)
+        g_out = self.cot_rows(i) * self.live[r, :]
+        g_low = g_out.astype(bf)
+        self.gout[r, :] = g_low
+        g_sq = (dot(g_low, self.up[...]) * slope).astype(bf)
+        self.g_up[...] += dot(g_low, value, TN)
+        self.g_down[...] += dot(low, g_sq, TN)
+        self.gffn[r, :] = (g_out + dot(g_sq, self.down[...], NT)).astype(bf)
+
+    def backward(self, j):
+        bf = jnp.bfloat16
+        f = rows_of(j, self.chunk)
+        for half in range(2):
+            r = pl.ds(half * (self.n // 2), self.n // 2)
+            g = (dot(self.gffn[r, :], self.wu(j), NT) * self.dg[r, f].astype(jnp.float32)).astype(bf)
+            self.dg[r, f] = g
+            self.acc[r, :] += dot(g, self.wi(j))
+        self.act[: self.chunk, f] = dot(self.act[:, f], self.gffn[...], TN).astype(bf)
+        self.dg[: self.chunk, f] = dot(self.dg[:, f], self.n2[...], TN).astype(bf)
+        for store in self.stores(j):
+            store.start()
+
+    def stores(self, j):
+        f = rows_of(j, self.chunk)
+        return [
+            pltpu.make_async_copy(src.at[pl.ds(0, self.chunk), f], dst.at[f], self.sem.at[k, j])
+            for k, (src, dst) in enumerate(((self.act, self.gu_hbm), (self.dg, self.gi_hbm)))
+        ]
+
+    def last(self, i):
+        r = rows_of(i)
+        total = self.mid[r, :]
+        g_n2 = self.acc[r, :]
+        scale = lax.rsqrt(jnp.mean(total * total, axis=-1, keepdims=True) + NORM_EPS)
+        self.g_gain[...] += jnp.sum(total * scale * g_n2, axis=0, keepdims=True)
+        scaled = self.gain[...] * g_n2
+        centre = jnp.mean(total * scaled, axis=-1, keepdims=True)
+        g_mid = self.gout[r, :].astype(jnp.float32) + scale * scaled - total * (scale * scale * scale * centre)
+        self.mid[r, :] = g_mid
+        self.glow[r, :] = g_mid.astype(jnp.bfloat16)
+
+    def rest(self, out_sems):
+        n, bf = self.n, jnp.bfloat16
+        self.g_down[...] = jnp.zeros_like(self.g_down)
+        self.g_up[...] = jnp.zeros_like(self.g_up)
+        self.g_gain[...] = jnp.zeros_like(self.g_gain)
+        each_of(n // RCH, self.adapter)
+        copies = [pltpu.make_async_copy(self.res, self.res_hbm, out_sems.at[0])]
+        copies[0].start()
+        self.acc[...] = jnp.zeros_like(self.acc)
+        each_of(self.count, self.backward)
+        each_of(n // RCH, self.last)
+        copies.append(pltpu.make_async_copy(self.mid, self.gmid_hbm, out_sems.at[1]))
+        copies[1].start()
+        for m in range(4):
+            rows = slice(CTX_PAD * m, CTX_PAD * (m + 1))
+            self.gffn[rows, :] = dot(self.ctx[m], self.glow[...], TN).astype(bf)
+            self.ctx[m] = dot(self.glow[...], self.wo(m), NT).astype(bf)
+        copies.append(pltpu.make_async_copy(self.gffn, self.go_hbm, out_sems.at[2]))
+        copies.append(pltpu.make_async_copy(self.ctx, self.gctx_hbm, out_sems.at[3]))
+        for copy in copies[2:]:
+            copy.start()
+        self.small_grads()
+        each_of(self.count, lambda j: [store.wait() for store in self.stores(j)])
+        for copy in copies:
+            copy.wait()
+
+    def small_grads(self):
+        other, pick = self.other, self.consts[1]
+        down, up = self.factors()
+        g_a, g_dl, g_dr = down.back(self.g_down[...])
+        g_b, g_ur, g_ul = up.back(self.g_up[...])
+        other[...] = jnp.zeros_like(other)
+        put_row(other, ROW_FFN, self.g_gain[...])
+        for at, tall in ((ROW_DL, g_dl), (ROW_UR, g_ur)):
+            other[at : at + 4, :] = tall[:, :128]
+            other[at + 4 : at + 8, : tall.shape[1] - 128] = tall[:, 128:]
+        for at, short in ((ROW_DR, g_dr), (ROW_UL, g_ul)):
+            other[at : at + 4, :KA] = short
+        for i in range(KRON):
+            at = ROW_RULES + 4 * i
+            other[at : at + 4, :KRON] = precise(g_a, pick[i], NT) + precise(pick[i], g_b, NT)
+
+
 def middle_kernel(
-    x_hbm, ctx_hbm, wo_hbm, wi_hbm, wu_hbm, cot_hbm, gain, down, up, live,
-    res_hbm, gmid_hbm, gctx_hbm, go_hbm, gi_hbm, gu_hbm, g_gain, g_down, g_up,
-    x, ctx, wo, wi, wu, cot, mid, n2, act, dg, acc, gffn, glow, stage, sems,
+    x_hbm, ctx_hbm, wo_hbm, wi_hbm, wu_hbm, cot_hbm, gain, lengths, rules, d_left, d_right, u_left, u_right,
+    same, pick, fold, agree,
+    res_hbm, gmid_hbm, gctx_hbm, go_hbm, gi_hbm, gu_hbm, other,
+    down, up, g_down, g_up, g_gain, live, x, ctx, wo, wi, wu, cot, mid, n2, act, dg, acc, gffn, glow, sem, sems, out_sems,
 ):
-    n = x.shape[0]
-    ff = wi.shape[0]
-    bf = jnp.bfloat16
     loads = [
         pltpu.make_async_copy(src, dst, sems.at[i])
         for i, (src, dst) in enumerate(
@@ -928,121 +1131,25 @@
     ]
     for load in loads:
         load.start()
-    for load in loads[:3]:
+    layer = Layer(
+        x_rows=lambda i: x[rows_of(i), :].astype(jnp.float32), cot_rows=lambda i: cot[rows_of(i), :].astype(jnp.float32),
+        wo=lambda m: wo[m], wi=lambda j: wi[rows_of(j, FCH), :], wu=lambda j: wu[rows_of(j, FCH), :],
+        chunk=FCH, count=wi.shape[0] // FCH, ctx=ctx, gain=gain, lengths=lengths, rules=rules,
+        sides=(d_left, d_right, u_left, u_right), consts=(same, pick, fold, agree), down=down, up=up, g_down=g_down,
+        g_up=g_up, g_gain=g_gain, live=live, mid=mid, n2=n2, act=act, dg=dg, acc=acc, gffn=gffn, glow=glow, res=x,
+        gout=cot, other=other, sem=sem, res_hbm=res_hbm, gmid_hbm=gmid_hbm, gctx_hbm=gctx_hbm, go_hbm=go_hbm,
+        gi_hbm=gi_hbm, gu_hbm=gu_hbm,
+    )
+    layer.prepare(lax.axis_index("mp"))
+    for load in loads:
         load.wait()
-
-    def first(i):
-        r = rows_of(i)
-        total = x[r, :].astype(jnp.float32)
-        for m in range(4):
-            total = total + dot(ctx[m, r, :], wo[m])
-        mid[r, :] = total
-        scale = lax.rsqrt(jnp.mean(total * total, axis=-1, keepdims=True) + NORM_EPS)
-        n2[r, :] = (total * scale * gain[...]).astype(bf)
-
-    each_of(n // RCH, first)
-    loads[3].wait()
-    loads[4].wait()
+    each_of(layer.n // RCH, layer.midway)
     acc[...] = jnp.zeros_like(acc)
-
-    def forward(j):
-        f = rows_of(j, FCH)
-        for half in range(2):
-            r = pl.ds(half * (n // 2), n // 2)
-            value, slope = gelu_both(dot(n2[r, :], wi[f, :], NT))
-            value = value.astype(bf)
-            act[r, f] = value
-            dg[r, f] = slope.astype(bf)
-            acc[r, :] += dot(value, wu[f, :])
-
-    each_of(ff // FCH, forward)
-    loads[5].wait()
-    g_down[...] = jnp.zeros_like(g_down)
-    g_up[...] = jnp.zeros_like(g_up)
-    g_gain[...] = jnp.zeros_like(g_gain)
-
-    def adapter(i):
-        r = rows_of(i)
-        ffn = acc[r, :]
-        low = ffn.astype(bf)
-        value, slope = gelu_both(dot(low, down[...]))
-        value = value.astype(bf)
-        x[r, :] = (mid[r, :] + ffn + dot(value, up[...], NT)).astype(bf)
-        g_out = cot[r, :].astype(jnp.float32) * live[r, :]
-        g_low = g_out.astype(bf)
-        cot[r, :] = g_low
-        g_sq = (dot(g_low, up[...]) * slope).astype(bf)
-        g_up[...] += dot(g_low, value, TN)
-        g_down[...] += dot(low, g_sq, TN)
-        gffn[r, :] = (g_out + dot(g_sq, down[...], NT)).astype(bf)
-
-    each_of(n // RCH, adapter)
-    out_copy = pltpu.make_async_copy(x, res_hbm, sems.at[0])
-    out_copy.start()
-    acc[...] = jnp.zeros_like(acc)
-
-    def stores(j, slot):
-        f = rows_of(j, FCH)
-        return [
-            pltpu.make_async_copy(stage.at[k, slot], dst.at[f], sems.at[6 + 2 * k + slot])
-            for k, dst in enumerate((gu_hbm, gi_hbm))
-        ]
-
-    def backward(j):
-        f = rows_of(j, FCH)
-        slot = lax.rem(j, 2)
-
-        def settle():
-            for store in stores(j - 2, slot):
-                store.wait()
-
-        pl.when(j >= 2)(settle)
-        for half in range(2):
-            r = pl.ds(half * (n // 2), n // 2)
-            g = (dot(gffn[r, :], wu[f, :], NT) * dg[r, f].astype(jnp.float32)).astype(bf)
-            dg[r, f] = g
-            acc[r, :] += dot(g, wi[f, :])
-        stage[0, slot] = dot(act[:, f], gffn[...], TN).astype(bf)
-        stage[1, slot] = dot(dg[:, f], n2[...], TN).astype(bf)
-        for store in stores(j, slot):
-            store.start()
-
-    count = ff // FCH
-    each_of(count, backward)
-
-    def last(i):
-        r = rows_of(i)
-        total = mid[r, :]
-        g_n2 = acc[r, :]
-        scale = lax.rsqrt(jnp.mean(total * total, axis=-1, keepdims=True) + NORM_EPS)
-        g_gain[...] += jnp.sum(total * scale * g_n2, axis=0, keepdims=True)
-        scaled = gain[...] * g_n2
-        centre = jnp.mean(total * scaled, axis=-1, keepdims=True)
-        g_mid = cot[r, :].astype(jnp.float32) + scale * scaled - total * (scale * scale * scale * centre)
-        mid[r, :] = g_mid
-        low = g_mid.astype(bf)
-        glow[r, :] = low
-
-    each_of(n // RCH, last)
-    mid_copy = pltpu.make_async_copy(mid, gmid_hbm, sems.at[1])
-    mid_copy.start()
-    for j in range(max(count - 2, 0), count):
-        for store in stores(j, j % 2):
-            store.wait()
-    for m in range(4):
-        stage[0, m // 2, (m % 2) * 256 : (m % 2 + 1) * 256] = dot(ctx[m], glow[...], TN).astype(bf)
-    go_copies = [pltpu.make_async_copy(stage.at[0, k], go_hbm.at[pl.ds(512 * k, 512)], sems.at[6 + k]) for k in range(2)]
-    for copy in go_copies:
-        copy.start()
-    for m in range(4):
-        ctx[m] = dot(glow[...], wo[m], NT).astype(bf)
-    ctx_copy = pltpu.make_async_copy(ctx, gctx_hbm, sems.at[2])
-    ctx_copy.start()
-    for copy in (out_copy, mid_copy, *go_copies, ctx_copy):
-        copy.wait()
-
-
-def middle(x, ctx, wo, wi, wu, cot, gain, down, up, live):
+    each_of(layer.count, layer.forward)
+    layer.rest(out_sems)
+
+
+def middle(x, ctx, wo, wi, wu, cot, gain, lengths, factors):
     n, ff = x.shape[0], wi.shape[0]
     bf, f32 = jnp.bfloat16, jnp.float32
     hbm = pl.BlockSpec(memory_space=pl.ANY)
@@ -1057,13 +1164,17 @@
             shape((4 * CTX_PAD, D), bf),
             shape((ff, D), bf),
             shape((ff, D), bf),
-            shape((1, D), f32),
-            shape((D, ADAPT_PAD), f32),
-            shape((D, ADAPT_PAD), f32),
+            shape((ROW_END, 128), f32),
         ],
-        in_specs=[hbm] * 6 + [vmem] * 4,
-        out_specs=[hbm] * 6 + [vmem] * 3,
+        in_specs=[hbm] * 6 + [vmem] + [pl.BlockSpec(memory_space=pltpu.SMEM)] + [vmem] * 9,
+        out_specs=[hbm] * 6 + [vmem],
         scratch_shapes=[
+            pltpu.VMEM((D, ADAPT_PAD), bf),
+            pltpu.VMEM((D, ADAPT_PAD), bf),
+            pltpu.VMEM((D, ADAPT_PAD), f32),
+            pltpu.VMEM((D, ADAPT_PAD), f32),
+            pltpu.VMEM((1, D), f32),
+            pltpu.VMEM((n, 1), f32),
             pltpu.VMEM((n, D), bf),
             pltpu.VMEM((4, n, CTX_PAD), bf),
             pltpu.VMEM((4, CTX_PAD, D), bf),
@@ -1077,12 +1188,13 @@
             pltpu.VMEM((n, D), f32),
             pltpu.VMEM((n, D), bf),
             pltpu.VMEM((n, D), bf),
-            pltpu.VMEM((2, 2, FCH, D), bf),
-            pltpu.SemaphoreType.DMA((10,)),
+            pltpu.SemaphoreType.DMA((2, ff // FCH)),
+            pltpu.SemaphoreType.DMA((6,)),
+            pltpu.SemaphoreType.DMA((4,)),
         ],
         compiler_params=pltpu.CompilerParams(vmem_limit_bytes=63 * 2**20),
         name="middle",
-    )(x, ctx, wo, wi, wu, cot, gain, down, up, live)
+    )(x, ctx, wo, wi, wu, cot, gain, lengths, *factors, *map(jnp.asarray, adapter_constants()))
 
 
 class Slots:
@@ -1102,122 +1214,227 @@
             pl.when(i == place[0])(functools.partial(self.run, place))
 
 
+FRONT = (
+    "s:o s:q s:i a:o0",
+    "ex0 a:q0 a:i0 a:q1",
+    "n c:o0 c:q0 a:o1",
+    "a:q2 s:u c:q1 c:q2",
+    "a:o2 a:q3 c:q3 a:i1",
+    "a:u0 c:o1 f:q c:i0",
+    "c:o2 A A A",
+    "a:o3 ex1 A A",
+    "A a:u1 A A",
+    "c:o3 c:i1 A A",
+    "A a:i2 A A",
+    "A A a:u2 c:u0",
+    "A f:o O a:i3",
+    "c:u1 F0 a:u3 c:i2",
+    "c:u2 F1 c:i3 c:u3",
+    "F2 F3",
+)
+
+
+def front_order():
+    plan, now = {"first": []}, "first"
+    pieces = 0
+    for step in " ".join(FRONT).split():
+        if step == "A":
+            now, pieces = ("A", pieces), pieces + 1
+        elif step[0] in "OF":
+            plan["before", step] = plan.pop("open", [])
+            now = "open"
+        else:
+            plan.setdefault(now, []).append(step)
+    return plan
+
+
 def front_kernel(
-    depth, group, tok, cot, wq, wo, wi, wu, gain, mask, rows,
-    tok_s, cot_s, gq_hbm, go, gi, gu, normed_hbm, packed_hbm, ctx_hbm,
-    x, gq, nrm, packed, ctx, local, *sems,
+    depth, group, tok, cot, w_qkv, w_o, w_in, w_out, choice, gain, gain_ffn, lengths, pos_table, onehot,
+    rules, d_left, d_right, u_left, u_right, same, pick, fold, agree,
+    tok_s, gq_hbm, normed_hbm, packed_hbm, res_hbm, gmid_hbm, gctx_hbm, go_hbm, gi_hbm, gu_hbm, other,
+    wq, wo, wi, wu, mask, rows, x, y, gq, go, gi, gu, nrm, packed, ctx,
+    down, up, g_down, g_up, g_gain, live, mid, n2, act, dg, acc, gffn, res, glow, sem, out_sems, local, *sems,
 ):
     p = Place(depth)
-    n = depth
     bf = jnp.bfloat16
-    arrays = [
-        Gather(p, by_head, shard, buf, *sems[3 * i : 3 * i + 3])
-        for i, (by_head, shard, buf) in enumerate(
-            ((True, wq, gq), (False, wo, go), (False, wi, gi), (False, wu, gu))
-        )
-    ]
-    q, rest = arrays[0], arrays[1:]
-    first, second = Exchange(p, tok, x, *sems[12:15]), Exchange(p, cot, cot_s, *sems[15:18])
+    per_head = [dot(w_qkv[h].astype(bf), choice[3 * DH * h : 3 * DH * (h + 1), :]) for h in range(3)]
+    wq[...] = sum(per_head).astype(bf)
+    wo[...] = jnp.zeros_like(wo)
+    wo[: w_o.shape[0], :] = w_o[...].astype(bf)
+    wi[...] = w_in[...].astype(bf)
+    wu[...] = w_out[...].astype(bf)
+    arrays = {
+        name: Gather(p, name == "q", shard, buf, *sems[3 * i : 3 * i + 3])
+        for i, (name, shard, buf) in enumerate((("q", wq, gq), ("o", wo, go), ("i", wi, gi), ("u", wu, gu)))
+    }
+    first, second = Exchange(p, tok, x, *sems[12:15]), Exchange(p, cot, y, *sems[15:18])
+    keep_x = pltpu.make_async_copy(x, tok_s, local.at[0])
+    keep_n = pltpu.make_async_copy(nrm, normed_hbm, local.at[1])
+    keep_q = pltpu.make_async_copy(gq, gq_hbm, local.at[2])
+    quarter = RCH // SEG
+
+    def float_rows(ref):
+        return lambda i: ref[pl.ds(quarter * i, quarter)].reshape(RCH, D).astype(jnp.float32)
+
+    layer = Layer(
+        x_rows=float_rows(x), cot_rows=float_rows(y),
+        wo=lambda m: go[m].reshape(CTX_PAD, D), wi=lambda j: gi[j].reshape(-1, D), wu=lambda j: gu[j].reshape(-1, D),
+        chunk=8 * wi.shape[0], count=depth, ctx=ctx, gain=gain_ffn, lengths=lengths, rules=rules,
+        sides=(d_left, d_right, u_left, u_right), consts=(same, pick, fold, agree), down=down, up=up, g_down=g_down,
+        g_up=g_up, g_gain=g_gain, live=live, mid=mid, n2=n2, act=act, dg=dg, acc=acc, gffn=gffn, glow=glow, res=res,
+        gout=nrm, other=other, sem=sem, res_hbm=res_hbm, gmid_hbm=gmid_hbm, gctx_hbm=gctx_hbm, go_hbm=go_hbm,
+        gi_hbm=gi_hbm, gu_hbm=gu_hbm,
+    )
+
+    def norm(i):
+        v = x[i].astype(jnp.float32)
+        scale = lax.rsqrt(jnp.mean(v * v, axis=-1, keepdims=True) + NORM_EPS)
+        nrm[rows_of(i, SEG), :] = (v * scale * gain[...]).astype(bf)
+
+    def norms():
+        first.finish()
+        keep_x.start()
+        each_of(x.shape[0], norm)
+        keep_n.start()
+        fill_mask(mask, lengths, p.m)
+        fill_rows(rows, pos_table, onehot)
+        layer.prepare(p.m)
+        acc[...] = jnp.zeros_like(acc)
+
+    def step(name):
+        kind, rest = name[0], name[2:]
+        if name == "n":
+            norms()
+        elif name in ("ex0", "ex1"):
+            (first, second)[int(name[2])].start()
+        elif kind == "s":
+            arrays[rest].start()
+        elif kind == "f":
+            arrays[rest].finish()
+        elif kind == "a":
+            arrays[rest[0]].along(int(rest[1:]))
+        elif kind == "c":
+            arrays[rest[0]].across(int(rest[1:]))
+
+    def steps(names):
+        for name in names:
+            step(name)
+
+    plan = front_order()
     p.barrier(0)
-    for g in arrays:
-        g.start()
-    first.start()
-    for g in arrays:
-        g.along(0)
-    for k in range(1, n):
-        for g in arrays:
-            g.along(k)
-        for g in arrays if k < n - 1 else [q]:
-            g.across(k - 1)
-        if k == 1:
-            first.finish()
-            keep_x = pltpu.make_async_copy(x, tok_s, local.at[0])
-            keep_x.start()
-            second.start()
-
-            def norm(i):
-                v = x[i].astype(jnp.float32)
-                scale = lax.rsqrt(jnp.mean(v * v, axis=-1, keepdims=True) + NORM_EPS)
-                nrm[rows_of(i, SEG), :] = (v * scale * gain[...]).astype(bf)
-
-            each_of(x.shape[0], norm)
-            keep_n = pltpu.make_async_copy(nrm, normed_hbm, local.at[1])
-            keep_n.start()
-    q.across(n - 1)
-    q.finish()
-    keep_q = pltpu.make_async_copy(gq, gq_hbm, local.at[2])
+    steps(plan["first"])
     keep_q.start()
-    places = {(m, j): 5.0 * m + t for m in range(4) for j, t in enumerate((2.5, 4.0, 4.5, 5.0))}
-    timed = []
-    for i, g in enumerate(rest):
-        timed.append((2.0 * i + 1.0, functools.partial(g.across, n - 2)))
-        timed.append((2.0 * i + 7.0, functools.partial(g.across, n - 1)))
-    slots = Slots(places, timed)
-
-    def keeps(m):
-        return [
-            pltpu.make_async_copy(packed.at[m], packed_hbm.at[m], local.at[3 + m]),
-            pltpu.make_async_copy(ctx.at[m], ctx_hbm.at[m], local.at[7 + m]),
-        ]
+
+    def piece(m, place):
+        number, q0 = place
+        at = {(0, 0): 0, (0, 256): 1, (1, 0): 2, (3, 0): 3}.get(place)
+        if at is not None:
+            for loop in range(4):
+                names = plan.get(("A", 4 * loop + at))
+                if names:
+                    pl.when(m == loop)(functools.partial(steps, names))
+
+    def keep(m):
+        return pltpu.make_async_copy(packed.at[m], packed_hbm.at[m], local.at[3 + m])
 
     def heads(m):
         w = gq[m // 2, m % 2].reshape(D, QKV_PAD)
         packed[m] = dot(nrm[...], w).astype(bf)
-        attend_group(packed.at[m], mask, rows[m], ctx.at[m], group, functools.partial(slots.tick, m))
-        for copy in keeps(m):
-            copy.start()
+        keep(m).start()
+        attend_group(packed.at[m], mask, rows[m], ctx.at[m], group, functools.partial(piece, m))
 
     each_of(4, heads)
-    slots.run(None)
-    for g in rest:
-        g.finish()
+    steps(plan[("before", "O")])
+    each_of(layer.n // RCH, layer.midway)
+
+    def chunk(e):
+        for k in range(depth):
+            pl.when(e == k)(functools.partial(steps, plan[("before", f"F{k}")]))
+        z = p.nearest(e)
+        for name in "iu":
+            arrays[name].finish_at(z)
+        layer.forward(z)
+
+    each_of(depth, chunk)
     second.finish()
-    for copy in [keep_x, keep_n, keep_q] + [c for m in range(4) for c in keeps(m)]:
+    for copy in [keep_x, keep_n, keep_q] + [keep(m) for m in range(4)]:
         copy.wait()
-    for g in arrays + [first, second]:
+    layer.rest(out_sems)
+    for g in (*arrays.values(), first, second):
         g.drain()
 
 
-def front(depth, group, tok, cot, shards, gain, mask, rows):
+def front(depth, group, tok, cot, shards, rows_of_shards, gains, lengths, pos_table, factors):
     hbm = pl.BlockSpec(memory_space=pl.ANY)
     vmem = pl.BlockSpec(memory_space=pltpu.VMEM)
-    bf = jnp.bfloat16
+    bf, f32 = jnp.bfloat16, jnp.float32
+    shape = jax.ShapeDtypeStruct
     n = tok.shape[0] * SEG
-    outs = [jax.ShapeDtypeStruct(tok.shape, tok.dtype)] * 2
-    for i, s in enumerate(shards):
-        lead = (2, 2, depth, 2) if i == 0 else (depth, 2, 2, 2)
-        outs.append(jax.ShapeDtypeStruct(lead + s.shape, s.dtype))
-    outs += [jax.ShapeDtypeStruct(shape, bf) for shape in ((n, D), (4, n, QKV_PAD), (4, n, CTX_PAD))]
+    kept = [(rows, QKV_PAD if i == 0 else D) for i, rows in enumerate(rows_of_shards)]
+    whole = [((2, 2, depth, 2) if i == 0 else (depth, 2, 2, 2)) + s for i, s in enumerate(kept)]
+    ff = 8 * depth * kept[2][0]
     return pl.pallas_call(
         functools.partial(front_kernel, depth, group),
-        out_shape=outs,
-        in_specs=[hbm] * 6 + [vmem] * 3,
-        out_specs=[hbm] * 9,
-        scratch_shapes=[
+        out_shape=[
+            shape(tok.shape, bf),
+            shape(whole[0], bf),
+            shape((n, D), bf),
+            shape((4, n, QKV_PAD), bf),
+            shape((n, D), bf),
+            shape((n, D), f32),
+            shape((4, n, CTX_PAD), bf),
+            shape((4 * CTX_PAD, D), bf),
+            shape((ff, D), bf),
+            shape((ff, D), bf),
+            shape((ROW_END, 128), f32),
+        ],
+        in_specs=[hbm] * 2 + [vmem] * 7 + [pl.BlockSpec(memory_space=pltpu.SMEM)] + [vmem] * 11,
+        out_specs=[hbm] * 10 + [vmem],
+        scratch_shapes=[pltpu.VMEM(s, bf) for s in kept]
+        + [
+            pltpu.VMEM((n, TILE), bf),
+            pltpu.VMEM((4, 3, 512), f32),
             pltpu.VMEM(tok.shape, bf),
-            pltpu.VMEM(outs[2].shape, bf),
+            pltpu.VMEM(tok.shape, bf),
+            *[pltpu.VMEM(s, bf) for s in whole],
             pltpu.VMEM((n, D), bf),
             pltpu.VMEM((4, n, QKV_PAD), bf),
             pltpu.VMEM((4, n, CTX_PAD), bf),
-            pltpu.SemaphoreType.DMA((11,)),
+            pltpu.VMEM((D, ADAPT_PAD), bf),
+            pltpu.VMEM((D, ADAPT_PAD), bf),
+            pltpu.VMEM((D, ADAPT_PAD), f32),
+            pltpu.VMEM((D, ADAPT_PAD), f32),
+            pltpu.VMEM((1, D), f32),
+            pltpu.VMEM((n, 1), f32),
+            pltpu.VMEM((n, D), f32),
+            pltpu.VMEM((n, D), bf),
+            pltpu.VMEM((n, ff), bf),
+            pltpu.VMEM((n, ff), bf),
+            pltpu.VMEM((n, D), f32),
+            pltpu.VMEM((n, D), bf),
+            pltpu.VMEM((n, D), bf),
+            pltpu.VMEM((n, D), bf),
+            pltpu.SemaphoreType.DMA((2, depth)),
+            pltpu.SemaphoreType.DMA((4,)),
+            pltpu.SemaphoreType.DMA((7,)),
         ]
         + Gather.sems(depth) * 4
         + Exchange.sems() * 2,
         compiler_params=pltpu.CompilerParams(
-            collective_id=2, has_side_effects=True, vmem_limit_bytes=56 * 2**20
+            collective_id=2, has_side_effects=True, vmem_limit_bytes=63 * 2**20
         ),
         name="front",
-    )(tok, cot, *shards, gain, mask, rows)
-
-
-ROW_GAIN, ROW_TABLE, ROW_OTHER = 0, 8, 24
+    )(
+        tok, cot, *shards, jnp.asarray(column_choice(group), bf), *gains, lengths, pos_table,
+        jnp.asarray(offset_onehot()), *factors, *map(jnp.asarray, adapter_constants()),
+    )
 
 
 def back_kernel(
     depth, bits, group,
-    packed_hbm, gctx_hbm, gq_hbm, nrm_hbm, x_hbm, gmid_hbm, pu, pi, po, out_s, gain, mask, rows, onehot, other,
+    packed_hbm, gctx_hbm, gq_hbm, nrm_hbm, x_hbm, gmid_hbm, pu, pi, po, out_s, gain, lengths, pos_table, spread, onehot, other,
     oq, oo, oi, ou, small, out, gtok,
-    packed, gctx, gq, nrm, x, gmid, acc, sums_s, part_q, gtok_s, local, mine_u, mine_i, mine_o, sem_u, sem_i, sem_o, *scr,
+    mask, rows, packed, gctx, gq, nrm, x, gmid, acc, sums_s, part_q, gtok_s, res, local, mine_u, mine_i, mine_o, sem_u, sem_i, sem_o, *scr,
 ):
     p = Place(depth)
     n = depth
@@ -1227,7 +1444,7 @@
     o = Scatter(p, False, po, oo, *scr[12:18], mine_o, sem_o)
     q = Scatter(p, True, part_q, oq, *scr[18:24])
     arrays = [u, i_, o, q]
-    row_out, row_g = Exchange(p, out_s, out, *scr[24:27]), Exchange(p, gtok_s, gtok, *scr[27:30])
+    row_out, row_g = Exchange(p, res, out, *scr[24:27]), Exchange(p, gtok_s, gtok, *scr[27:30])
     total = Sum(p, bits, small, *scr[30:33])
     heads_in = [
         [
@@ -1238,7 +1455,7 @@
     ]
     others_in = [
         pltpu.make_async_copy(src, dst, local.at[8 + k])
-        for k, (src, dst) in enumerate(((nrm_hbm, nrm), (gq_hbm, gq), (x_hbm, x), (gmid_hbm, gmid)))
+        for k, (src, dst) in enumerate(((nrm_hbm, nrm), (gq_hbm, gq), (x_hbm, x), (gmid_hbm, gmid), (out_s, res)))
     ]
     for copy in heads_in[0]:
         copy.start()
@@ -1251,17 +1468,19 @@
     for copies in heads_in[1:]:
         for copy in copies:
             copy.start()
-    row_out.start()
     for k in range(n):
         o.start(k)
     small[...] = jnp.zeros_like(small)
     small[ROW_OTHER:, :] = other[...]
     acc[...] = jnp.zeros_like(acc)
+    fill_mask(mask, lengths, p.m)
+    fill_rows(rows, pos_table, spread)
     for copies in heads_in:
         for copy in copies:
             copy.wait()
     for copy in others_in:
         copy.wait()
+    row_out.start()
 
     span = 10.0
     places = {(m, j): span * m + 0.63 * (j + 1) for m in range(4) for j in range(12)}
@@ -1309,8 +1528,7 @@
         return g_gain + jnp.sum(v * scale * g_n1, axis=0, keepdims=True)
 
     g_gain = lax.fori_loop(0, x.shape[0], last, jnp.zeros((1, D), jnp.float32))
-    for k in range(D // 128):
-        small[ROW_GAIN + k : ROW_GAIN + k + 1, :] = g_gain[:, 128 * k : 128 * (k + 1)]
+    put_row(small, ROW_GAIN, g_gain)
     for k in range(n):
         q.to_half(k)
     row_g.start()
@@ -1326,7 +1544,7 @@
         g.drain()
 
 
-def back(depth, bits, group, packed, gctx, gq, nrm, x, gmid, parts, out_s, gain, mask, rows, onehot, other):
+def back(depth, bits, group, packed, gctx, gq, nrm, x, gmid, parts, out_s, gain, lengths, pos_table, onehot, other):
     hbm = pl.BlockSpec(memory_space=pl.ANY)
     vmem = pl.BlockSpec(memory_space=pltpu.VMEM)
     bf, f32 = jnp.bfloat16, jnp.float32
@@ -1337,6 +1555,8 @@
     outs += [shape((small_rows, 128), f32), shape(out_s.shape, bf), shape(x.shape, bf)]
     dma = pltpu.SemaphoreType.DMA
     scratch = [
+        pltpu.VMEM((nrm.shape[0], TILE), bf),
+        pltpu.VMEM((4, 3, 512), f32),
         pltpu.VMEM(packed.shape, bf),
         pltpu.VMEM(gctx.shape, bf),
         pltpu.VMEM(gq.shape, bf),
@@ -1347,7 +1567,8 @@
         pltpu.VMEM((4, 3, 768), f32),
         pltpu.VMEM(pq_shape, bf),
         pltpu.VMEM(x.shape, bf),
-        dma((12,)),
+        pltpu.VMEM(x.shape, bf),
+        dma((13,)),
     ]
     scratch += [pltpu.VMEM((depth, 2, 2) + s.shape[4:], bf) for s in parts]
     scratch += [dma((depth,))] * 3
@@ -1357,14 +1578,49 @@
     return pl.pallas_call(
         functools.partial(back_kernel, depth, bits, group),
         out_shape=outs,
-        in_specs=[hbm] * 10 + [vmem] * 5,
+        in_specs=[hbm] * 10 + [vmem] + [pl.BlockSpec(memory_space=pltpu.SMEM)] + [vmem] * 4,
         out_specs=[vmem] * 5 + [hbm] * 2,
         scratch_shapes=scratch,
         compiler_params=pltpu.CompilerParams(
             collective_id=3, has_side_effects=True, vmem_limit_bytes=63 * 2**20
         ),
         name="back",
-    )(packed, gctx, gq, nrm, x, gmid, *parts, out_s, gain, mask, rows, onehot, other)
+    )(packed, gctx, gq, nrm, x, gmid, *parts, out_s, gain, lengths, pos_table, jnp.asarray(offset_onehot()), onehot, other)
+
+
+def finish_kernel(
+    q, o, i, u, small, choice,
+    gq, go, gi, gu, g_attn, g_ffn, g_table, g_rules, g_dl, g_dr, g_ul, g_ur,
+):
+    for h in range(3):
+        gq[h] = precise(q[: gq.shape[1], :], choice[3 * DH * h : 3 * DH * (h + 1), :], NT)
+    go[...] = o[: go.shape[0], :]
+    gi[...] = i[: gi.shape[0], :]
+    gu[...] = u[: gu.shape[0], :]
+    for k in range(D // 128):
+        lanes = slice(128 * k, 128 * (k + 1))
+        g_attn[:, lanes] = small[ROW_GAIN + k : ROW_GAIN + k + 1, :]
+        g_ffn[:, lanes] = small[ROW_OTHER + ROW_FFN + k : ROW_OTHER + ROW_FFN + k + 1, :]
+    g_table[...] = small[ROW_TABLE : ROW_TABLE + g_table.shape[0], :NB]
+    for i in range(KRON):
+        at = ROW_OTHER + ROW_RULES + 4 * i
+        g_rules[i] = small[at : at + 4, :KRON]
+    for ref, at in ((g_dl, ROW_OTHER + ROW_DL), (g_ur, ROW_OTHER + ROW_UR)):
+        ref[:, :128] = small[at : at + 4, :]
+        ref[:, 128:] = small[at + 4 : at + 8, : ref.shape[1] - 128]
+    for ref, at in ((g_dr, ROW_OTHER + ROW_DR), (g_ul, ROW_OTHER + ROW_UL)):
+        ref[...] = small[at : at + 4, :KA]
+
+
+def finish(q, o, i, u, small, group, shapes):
+    vmem = pl.BlockSpec(memory_space=pltpu.VMEM)
+    return pl.pallas_call(
+        finish_kernel,
+        out_shape=[jax.ShapeDtypeStruct(s, jnp.float32) for s in shapes],
+        in_specs=[vmem] * 6,
+        out_specs=[vmem] * 12,
+        name="finish",
+    )(q, o, i, u, small, jnp.asarray(column_choice(group)))
 
 
 def round_up(n, m):
@@ -1405,31 +1661,20 @@
     o_rows, in_rows, q_rows = w_o.shape[0], w_in.shape[1], w_qkv.shape[0]
     bf = jnp.bfloat16
     group = o_rows if o_rows % 24 == 0 and round_up(o_rows, 16) * 3 == o_rows * 4 else 3 * DH
-    wq = pad_rows(head_columns(w_qkv.astype(bf), group), round_up(q_rows, 16))
-    wo = pad_rows(w_o.astype(bf), round_up(o_rows, 16))
-    wi = pad_rows(w_in.astype(bf).T, round_up(in_rows, 16))
-    wu = pad_rows(w_out.astype(bf), round_up(in_rows, 16))
-    own_lengths = jnp.stack([
-        lengths[member], lengths[4 + member // 2 + 2 * (member % 2)], lengths[8 + member], lengths[12 + member]
-    ])
-    shapes = ((LEN_LONG, 1), (LEN_MID, 1), (LEN_SHORT, 2))
-    pieces = []
-    first = 0
-    for length, seqs in shapes:
-        spots = jnp.arange(length, dtype=jnp.int32)
-        pieces.append((spots[None, :] < own_lengths[first : first + seqs, None]).reshape(-1))
-        first += seqs
-    live = jnp.concatenate(pieces)
-    mask = key_mask(live)
-    rows = offset_row(pos_table).reshape(mp_count, 3, 512)
+    rows_of_shards = [round_up(r, 16) for r in (q_rows, o_rows, in_rows, in_rows)]
     tok_in, cot_in = tokens.reshape(seg_count, SEG, D), cotangent.reshape(seg_count, SEG, D)
-    merged = depth <= 8 and wq.shape[0] == q_rows
+    merged = depth == 4 and group == o_rows and rows_of_shards[0] == q_rows and rows_of_shards[2] == in_rows
+    factors = (phm_rules, down_left, down_right, up_left, up_right)
+    gains = (gain_attn.reshape(1, D), gain_ffn.reshape(1, D))
     if merged:
-        tok_s, cot_s, gq, go, gi, gu, normed_attn, packed, context = front(
-            depth, group, tok_in, cot_in, (wq, wo, wi, wu), gain_attn[None], mask, rows
+        shards = (w_qkv.transpose(1, 0, 2), w_o, w_in.T, w_out)
+        tok_s, gq, normed_attn, packed, result, grad_mid, grad_context, grad_w_o, grad_w_in, grad_w_out, other = front(
+            depth, group, tok_in, cot_in, shards, rows_of_shards, gains, lengths, pos_table.T, factors
         )
     else:
-        tok_s, cot_s, gq, go, gi, gu = gather_all(depth, tok_in, cot_in, (wq, wo, wi, wu))
+        shards = (head_columns(w_qkv.astype(bf), group), w_o.astype(bf), w_in.astype(bf).T, w_out.astype(bf))
+        shards = [pad_rows(s, r) for s, r in zip(shards, rows_of_shards)]
+        tok_s, cot_s, gq, go, gi, gu = gather_all(depth, tok_in, cot_in, shards)
     tokens_s = tok_s.reshape(tok_rows, D)
 
     def plain(g, rows):
@@ -1439,46 +1684,42 @@
         padded = jnp.pad(g.reshape(devices, rows, D), ((0, 0), (0, round_up(rows, 16) - rows), (0, 0)))
         return padded.reshape(depth, 2, 2, 2, padded.shape[1], D)
 
-    dense_in, dense_out = plain(gi, in_rows), plain(gu, in_rows)
-    if group == o_rows:
-        dense_o = go.reshape(mp_count, CTX_PAD, D)
-    else:
-        dense_o = plain(go, o_rows).reshape(mp_count, 3 * DH, D)
-        dense_o = jnp.pad(dense_o, ((0, 0), (0, CTX_PAD - 3 * DH), (0, 0)))
-    qkv_full = gq.reshape(mp_count, dp_count, wq.shape[0], QKV_PAD)[:, :, :q_rows].reshape(mp_count, D, QKV_PAD)
     if not merged:
-        normed_attn, packed, context = attention(tokens_s, gain_attn[None], qkv_full, mask, rows, group)
-    w_down, w_up = adapter_weights(phm_rules, down_left, down_right, up_left, up_right)
-    wide = ((0, 0), (0, ADAPT_PAD - ADAPT))
-    result, grad_mid, grad_context, grad_w_o, grad_w_in, grad_w_out, grad_gain_ffn, grad_w_down, grad_w_up = middle(
-        tokens_s,
-        context,
-        dense_o,
-        dense_in,
-        dense_out,
-        cot_s.reshape(tok_rows, D),
-        gain_ffn[None],
-        jnp.pad(w_down.astype(bf), wide),
-        jnp.pad(w_up.T.astype(bf), wide),
-        live[:, None].astype(jnp.float32),
-    )
-    grad_w_down, grad_w_up = grad_w_down[:, :ADAPT], grad_w_up[:, :ADAPT].T
+        if group == o_rows:
+            dense_o = go.reshape(mp_count, CTX_PAD, D)
+        else:
+            dense_o = plain(go, o_rows).reshape(mp_count, 3 * DH, D)
+            dense_o = jnp.pad(dense_o, ((0, 0), (0, CTX_PAD - 3 * DH), (0, 0)))
+        qkv_full = gq.reshape(mp_count, dp_count, rows_of_shards[0], QKV_PAD)[:, :, :q_rows]
+        qkv_full = qkv_full.reshape(mp_count, D, QKV_PAD)
+        live = jnp.concatenate(
+            [jnp.arange(length) < own_length(lengths, member, i) for i, (_, length) in enumerate(SPANS)]
+        )
+        mask = key_mask(live)
+        rows = jnp.einsum("bh,br->hr", pos_table, offset_onehot(), precision=FULL_PRECISION).reshape(mp_count, 3, 512)
+        normed_attn, packed, context = attention(tokens_s, gains[0], qkv_full, mask, rows, group)
+        result, grad_mid, grad_context, grad_w_o, grad_w_in, grad_w_out, other = middle(
+            tokens_s,
+            context,
+            dense_o,
+            plain(gi, in_rows),
+            plain(gu, in_rows),
+            cot_s.reshape(tok_rows, D),
+            gains[1],
+            lengths,
+            factors,
+        )
     if group == o_rows:
         part_o = grad_w_o.reshape(depth, 2, 2, 2, round_up(o_rows, 16), D)
     else:
         part_o = slots(grad_w_o.reshape(mp_count, CTX_PAD, D)[:, : 3 * DH].reshape(D, D), o_rows)
-    _, adapter_back = jax.vjp(adapter_weights, phm_rules, down_left, down_right, up_left, up_right)
-    small_list = (grad_gain_ffn[0],) + adapter_back((grad_w_down, grad_w_up))
-    flat = jnp.concatenate([s.reshape(-1) for s in small_list])
-    other_rows = round_up(-(-flat.size // 128), 8)
-    other = jnp.pad(flat, (0, other_rows * 128 - flat.size)).reshape(other_rows, 128)
     part_in, part_out = slots(grad_w_in, in_rows), slots(grad_w_out, in_rows)
     result = result.reshape(seg_count, SEG, D)
     onehot = jnp.asarray(np.pad(table_onehot(), ((0, 0), (0, 128 - NB))))
     if merged:
         oq, oo, oi, ou, summed, out, gtok = back(
             depth, bits, group, packed, grad_context, gq, normed_attn, tok_s, grad_mid,
-            (part_out, part_in, part_o), result, gain_attn[None], mask, rows, onehot, other,
+            (part_out, part_in, part_o), result, gains[0], lengths, pos_table.T, onehot, other,
         )
     else:
         packed_grads, sums = attention_back(packed, grad_context, mask, rows, group)
@@ -1494,28 +1735,26 @@
             other,
         ])
         part_q = grad_w_qkv.reshape(mp_count, dp_count, q_rows, QKV_PAD)
-        part_q = jnp.pad(part_q, ((0, 0), (0, 0), (0, wq.shape[0] - q_rows), (0, 0)))
-        part_q = part_q.reshape(2, 2, depth, 2, wq.shape[0], QKV_PAD)
+        part_q = jnp.pad(part_q, ((0, 0), (0, 0), (0, rows_of_shards[0] - q_rows), (0, 0)))
+        part_q = part_q.reshape(2, 2, depth, 2, rows_of_shards[0], QKV_PAD)
         oq, oo, oi, ou, summed, out, gtok = scatter_all(
             depth, bits, (part_q, part_o, part_in, part_out), small, result, grad_tokens.reshape(seg_count, SEG, D)
         )
-    smalls = [
-        summed[ROW_GAIN : ROW_GAIN + D // 128].reshape(D),
-        summed[ROW_TABLE : ROW_TABLE + HEADS, :NB].T,
-    ]
-    flat = summed[ROW_OTHER:].reshape(-1)
-    first = 0
-    for s in small_list:
-        smalls.append(flat[first : first + s.size].reshape(s.shape))
-        first += s.size
-    smalls = [smalls[0], smalls[2], smalls[1], *smalls[3:]]
+    shapes = (
+        (3, q_rows, 3 * DH), w_o.shape, w_in.shape[::-1], w_out.shape, (1, D), (1, D), pos_table.shape[::-1],
+        phm_rules.shape, down_left.shape, down_right.shape, up_left.shape, up_right.shape,
+    )
+    g_qkv, g_o, g_in, g_out, g_attn, g_ffn, g_table, *smalls = finish(oq, oo, oi, ou, summed, group, shapes)
     return (
         out.reshape(tok_rows, D),
         gtok.reshape(tok_rows, D),
-        from_head_columns(oq[:q_rows], group),
-        oo[:o_rows],
-        oi[:in_rows].T,
-        ou[:in_rows],
+        g_qkv.transpose(1, 0, 2),
+        g_o,
+        g_in.T,
+        g_out,
+        g_attn.reshape(D),
+        g_ffn.reshape(D),
+        g_table.T,
         *smalls,
     )
 

time: 327 us -> 249 us (0.76); the launches traced: 329 us -> 245 us
  Pallas kernels: 282 us -> 236 us
  local copies, waits for them, and re-layouts: 30.6 us -> 5.66 us
  matrix products: 7.92 us -> 0 us
  other arithmetic: 7.43 us -> 2.58 us
    pallas_call x2, Pallas kernels: 163 us -> 124 us  [the longest x1 120 us: front(): pl.pallas_call(functools.partial(front_kernel, depth, group), out_shape=[...]
    slice x13 -> x0, local copies, waits for them, and re-layouts: 9.06 us -> none  [the longest x5 2.52 us: local(): smalls.append(flat[first:first + s.size].reshape(s.shape))]
    dot_general x11 -> x0, matrix products: 7.92 us -> none  [the longest x5 3.32 us: adapter_weights(): jnp.einsum('iab,ip,iq->apbq', phm_rules, up_left, up_right, precision=FUL...]
    pallas_call x1, Pallas kernels: 118 us -> 112 us  [back(): pl.pallas_call(functools.partial(back_kernel, depth, bits, group), out_sh...]
    unnamed x35 -> x6, local copies, waits for them, and re-layouts: 6.4 us -> 3.12 us
where the time goes in v3:
time: 249 us; the launch traced here: 245 us
  Pallas kernels  236 us (95%)
  local copies, waits for them, and re-layouts  5.66 us (2%)
  other arithmetic  2.58 us (1%)
    pallas_call x1, Pallas kernels, front(): pl.pallas_call(functools.partial(front_kernel, depth, group), out_shape=[...  120 us
    pallas_call x1, Pallas kernels, back(): pl.pallas_call(functools.partial(back_kernel, depth, bits, group), out_sh...  112 us

profile of v3, /device:TPU:0, one launch (start us, length us, event | category | flops | bytes accessed | tf_op | source)
XLA Modules:
  0.0 245.2 jit_solution(9591032632096359304)
XLA Ops:
  0.6 1.3 reshape.70.gain
  1.9 1.3 reshape.71.gain_ffn
  3.2 119.9 %front.1 = (bf16[8,128,768]{2,1,0:T(8,128)(2,1)}, bf16[2,2,4,2,96,640]{5,4,3,2,1,0:T(8,128)(2,1)}, bf16[1024,768]{1,0:T(8,128)(2,1)}, bf16[4,1024,640]{2,1,0:T(8...) custom-call(bf16[8,128,768]{2,1,0:T(8,128)(2,1)} %bitcast.20, ...), custom_call_target="tpu_custom_call" | custom-call | tf_op jit(solution)/shard_map/front/pallas_call | solution.py:1376
  123.1 111.7 %back.1 = (f32[96,640]{1,0:T(8,128)}, f32[32,768]{1,0:T(8,128)}, f32[96,768]{1,0:T(8,128)}, f32[96,768]{1,0:T(8,128)}, f32[72,128]{1,0:T(8,128)}, /*index=5*/bf1...) custom-call(bf16[4,1024,640]{2,1,0:T(8,128)(2,1)} %get-tuple-element.44.packed_hbm, ...), custom_call_target="tpu_custom_call" | custom-call | tf_op jit(solution)/shard_map/back/pallas_call | solution.py:1578
  234.8 0.0 copy-start.1
  234.8 4.5 %finish.1 = (f32[3,96,192]{2,1,0:T(8,128)}, f32[24,768]{1,0:T(8,128)}, f32[96,768]{1,0:T(8,128)}, f32[96,768]{1,0:T(8,128)}, f32[1,768]{1,0:T(1,128)}, /*index=5...) custom-call(f32[96,640]{1,0:T(8,128)} %get-tuple-element.57.q, ...), custom_call_target="tpu_custom_call" | custom-call | tf_op jit(solution)/shard_map/finish/pallas_call | solution.py:1617
  239.3 1.3 reduce
  240.6 1.3 reduce.1
  241.9 0.0 copy-done.1
  241.9 0.0 copy-start
  241.9 1.1 copy.40
  243.0 0.8 copy-done
  243.9 1.1 copy.41
Async XLA Ops:
  234.8 7.1 %copy-start.1 = (bf16[8,128,768]{2,1,0:T(8,128)(2,1)S(1)}, bf16[8,128,768]{2,1,0:T(8,128)(2,1)}, u32[]{:S(2)}) copy-start(bf16[8,128,768]{2,1,0:T(8,128)(2,1)} %get-tuple-element.55) | copy-start | bytes 4718596
  241.9 2.0 copy-start
